TPU v7x, 32 devices: a whole 2x2x4 slice. The times are simulated.
32 devices in a mesh: seq: 16 (over z, y, core), txt: 2 (over x).
Axes of the slice: x: 2, y: 2, z: 4, core: 2. Of those that a mesh axis runs over, the one named last changes fastest.
Arguments:
- video_tokens: bfloat16 [8192, 1536], P('seq'), may hold values from -6 to 6
- cotangent: bfloat16 [8192, 1536], P('seq'), may hold values from -6 to 6
- condition: bfloat16 [49, 1024], replicated, may hold values from -6 to 6
- captions: bfloat16 [48, 64, 4096], P('seq', 'txt'), may hold values from -6 to 6
- long_caption: bfloat16 [64, 4096], P('txt'), may hold values from -6 to 6
- null_embed: bfloat16 [64, 4096], P('txt'), may hold values from -6 to 6
- query_key_value: bfloat16 [1536, 3, 1536], P('seq', None, 'txt'), may hold values from -0.15625 to 0.15625
- out_weight: bfloat16 [1536, 1536], P('seq', 'txt'), may hold values from -0.15625 to 0.15625
- gate_weight: bfloat16 [1536, 4096], P('seq', 'txt'), may hold values from -0.15625 to 0.15625
- up_weight: bfloat16 [1536, 4096], P('seq', 'txt'), may hold values from -0.15625 to 0.15625
- down_weight: bfloat16 [1536, 4096], P('seq', 'txt'), may hold values from -0.09375 to 0.09375
- text_weight: bfloat16 [4096, 2, 1536], P('seq', None, 'txt'), may hold values from -0.09375 to 0.09375
- ada_weight: bfloat16 [1024, 6144], P(None, ('seq', 'txt')), may hold values from -0.1875 to 0.1875
- ada_bias: float32 [6144], P(('seq', 'txt')), may hold values from -1.75 to 1.75
- norm_gains: float32 [7, 1536], replicated, may hold values from 0.25 to 1.75
- head_gates: float32 [24], replicated, may hold values from -1.5 to 1.5
- clip_lengths: int32 [16, 3], P('seq'), may hold values from 1 to 224, 448 in all within a row
- null_mask: int32 [49], replicated, may hold values from 0 to 1, as said below
- text_lengths: int32 [49], replicated, may hold values from 16 to 64, as said below
Outputs:
- block_out: bfloat16 [8192, 1536], P('seq')
- video_grad: float32 [8192, 1536], P('seq')
- condition_grad: float32 [49, 1024], replicated
- query_key_value_grad: float32 [1536, 3, 1536], P('seq', None, 'txt')
- out_weight_grad: float32 [1536, 1536], P('seq', 'txt')
- gate_weight_grad: float32 [1536, 4096], P('seq', 'txt')
- up_weight_grad: float32 [1536, 4096], P('seq', 'txt')
- down_weight_grad: float32 [1536, 4096], P('seq', 'txt')
- text_weight_grad: float32 [4096, 2, 1536], P('seq', None, 'txt')
- ada_weight_grad: float32 [1024, 6144], P(None, ('seq', 'txt'))
- ada_bias_grad: float32 [6144], P(('seq', 'txt'))
- null_grad: float32 [64, 4096], replicated
- norm_gains_grad: float32 [7, 1536], replicated
- head_gates_grad: float32 [24], replicated
Inputs may be any that keep to these rules, and one draw needn't show every extreme that they name: `clip_lengths`: row s lists, in order, the lengths of the 3 short clips that follow the 64 long-clip rows on index s of seq; each row sums to 448. `null_mask`: entry 48, that of the long clip, is 0; among the short clips both values occur. Clip c reads its caption's first text_lengths[c] tokens; entry 48 belongs to the long clip.
All inputs are finite; a program needn't handle non-finite values.
Results may differ from a plain program's by a relative error of at most 0.01615.
Values may be sent and summed in bfloat16 or wider, within the bound.
No kernel may reach another device: no remote copies, remote signals or barrier semaphores. Data moves between devices by JAX's collectives and lax.ppermute only.
A program may use at most 320 MiB of HBM per device.

v0:
```python
import math

import jax
import jax.numpy as jnp
from jax import lax
from jax.sharding import PartitionSpec as P

H = 24
HD = 64
TXT_LEN = 64
LONG_DEV = 64


epsilon = 1e-05
negative = -1e30
highest = lax.Precision.HIGHEST


def layout(lengths_row, seq_index, long_rows, short_rows):
    clip_count = lengths_row.shape[0]
    clip_ends = jnp.cumsum(lengths_row)
    clip_starts = clip_ends - lengths_row
    row_ids = jnp.arange(short_rows, dtype=jnp.int32)
    local_clip = jnp.sum(
        (row_ids[:, None] >= clip_ends[None, : clip_count - 1]).astype(jnp.int32), axis=1
    )
    chosen = local_clip[:, None] == jnp.arange(clip_count, dtype=jnp.int32)[None, :]
    clip_begin = jnp.sum(jnp.where(chosen, clip_starts[None, :], 0), axis=1)
    clip_local = jnp.concatenate([jnp.full((long_rows,), clip_count, jnp.int32), local_clip])
    long_place = seq_index * long_rows + jnp.arange(long_rows, dtype=jnp.int32)
    position = jnp.concatenate([long_place, row_ids - clip_begin])
    return (clip_local, position)


def rotate(values, position):
    half_dim = values.shape[-1] // 2
    frequency = jnp.exp(jnp.arange(half_dim, dtype=jnp.float32) * (-math.log(10000.0) / half_dim))
    angles = position.astype(jnp.float32)[..., None] * frequency
    cosine = jnp.cos(angles)[..., None, :]
    sine_part = jnp.sin(angles)[..., None, :]
    front_part = values[..., :half_dim]
    back_part = values[..., half_dim:]
    return jnp.concatenate(
        [front_part * cosine - back_part * sine_part, front_part * sine_part + back_part * cosine],
        axis=-1,
    )


def rms_parts(values):
    inverse = lax.rsqrt(jnp.mean(values * values, axis=-1, keepdims=True) + epsilon)
    return (values * inverse, inverse)


def rms_back(grad_hat, normed, inverse):
    return inverse * (grad_hat - normed * jnp.mean(grad_hat * normed, axis=-1, keepdims=True))


def masked_softmax(scores, visible):
    masked = jnp.where(visible, scores, negative)
    peak_value = jnp.max(masked, axis=-1, keepdims=True)
    exponent = jnp.exp(masked - peak_value)
    row_total = jnp.sum(exponent, axis=-1, keepdims=True)
    return (exponent / row_total, peak_value[..., 0] + jnp.log(row_total[..., 0]))


def recompute_probs(scores, visible, log_total):
    return jnp.where(visible, jnp.exp(scores - log_total[..., None]), 0.0)


def contract_rows(left_side, right_side):
    return lax.dot_general(
        left_side, right_side, (((0,), (0,)), ((), ())), preferred_element_type=jnp.float32
    )


def contract_cols(left_side, right_side):
    return lax.dot_general(
        left_side, right_side, (((1,), (1,)), ((), ())), preferred_element_type=jnp.float32
    )


def head_sum(values):
    return lax.psum(values.astype(jnp.bfloat16), "txt").astype(jnp.float32)


def local(
    video_tokens,
    cotangent,
    condition,
    captions,
    long_caption,
    null_embed,
    query_key_value,
    out_weight,
    gate_weight,
    up_weight,
    down_weight,
    text_weight,
    ada_weight,
    ada_bias,
    norm_gains,
    head_gates,
    clip_lengths,
    null_mask,
    text_lengths,
):
    seq_index = lax.axis_index("seq")
    txt_index = lax.axis_index("txt")
    txt_count = lax.axis_size("txt")
    hidden = video_tokens.astype(jnp.float32)
    token_count = hidden.shape[0]
    model_width = hidden.shape[1]
    own_heads = query_key_value.shape[2] // HD
    own_width = own_heads * HD
    head_start = txt_index * own_heads
    clip_total = condition.shape[0]
    short_clips = clip_lengths.shape[1]
    score_scale = HD ** (-0.5)
    clip_local, position = layout(clip_lengths[0], seq_index, LONG_DEV, token_count - LONG_DEV)
    shifted = jax.nn.silu(condition.astype(jnp.float32)).astype(jnp.bfloat16)
    mod_part = jnp.dot(shifted, ada_weight, preferred_element_type=jnp.float32) + ada_bias
    modulation = lax.all_gather(mod_part, ("seq", "txt"), axis=1, tiled=True)
    own_mod = jnp.concatenate(
        [
            lax.dynamic_slice_in_dim(modulation, seq_index * short_clips, short_clips, 0),
            modulation[clip_total - 1 :],
        ],
        axis=0,
    )
    selector = (
        clip_local[:, None] == jnp.arange(short_clips + 1, dtype=jnp.int32)[None, :]
    ).astype(jnp.float32)
    token_mod = jnp.dot(selector, own_mod, precision=highest)
    scale_attn, gate_attn, scale_ffn, gate_ffn = jnp.split(token_mod, 4, axis=1)
    query_gain = lax.dynamic_slice_in_dim(norm_gains[4].reshape(H, HD), head_start, own_heads, 0)
    key_gain = lax.dynamic_slice_in_dim(norm_gains[5].reshape(H, HD), head_start, own_heads, 0)
    text_gain = lax.dynamic_slice_in_dim(norm_gains[6].reshape(H, HD), head_start, own_heads, 0)
    hidden_hat, hidden_inv = rms_parts(hidden)
    normed_in = (hidden_hat * norm_gains[0] * (1.0 + scale_attn)).astype(jnp.bfloat16)
    qkv_full, out_full, gate_full, up_full, down_full, text_full = (
        lax.all_gather(query_key_value, "seq", axis=0, tiled=True),
        lax.all_gather(out_weight, "seq", axis=0, tiled=True),
        lax.all_gather(gate_weight, "seq", axis=0, tiled=True),
        lax.all_gather(up_weight, "seq", axis=0, tiled=True),
        lax.all_gather(down_weight, "seq", axis=0, tiled=True),
        lax.all_gather(text_weight, "seq", axis=0, tiled=True),
    )
    qkv_matrix = qkv_full.reshape(model_width, 3 * own_width)
    text_matrix = text_full.reshape(text_full.shape[0], 2 * own_width)
    projected = jnp.dot(normed_in, qkv_matrix, preferred_element_type=jnp.float32).reshape(
        token_count, 3, own_heads, HD
    )
    query_hat, query_inv = rms_parts(projected[:, 0])
    key_hat, key_inv = rms_parts(projected[:, 1])
    query_bf = rotate(query_hat * query_gain, position).astype(jnp.bfloat16)
    key_bf = rotate(key_hat * key_gain, position).astype(jnp.bfloat16)
    value_bf = projected[:, 2].astype(jnp.bfloat16)
    short_query = query_bf[LONG_DEV:]
    short_key = key_bf[LONG_DEV:]
    short_value = value_bf[LONG_DEV:]
    short_ids = clip_local[LONG_DEV:]
    same_clip = (short_ids[:, None] == short_ids[None, :])[None]
    short_scores = (
        jnp.einsum("qhe,khe->hqk", short_query, short_key, preferred_element_type=jnp.float32)
        * score_scale
    )
    short_probs, short_lse = masked_softmax(short_scores, same_clip)
    short_out = jnp.einsum(
        "hqk,khe->qhe",
        short_probs.astype(jnp.bfloat16),
        short_value,
        preferred_element_type=jnp.float32,
    )
    long_query = query_bf[:LONG_DEV]
    long_keys, long_values = (
        lax.all_gather(key_bf[:LONG_DEV], "seq", axis=0, tiled=True),
        lax.all_gather(value_bf[:LONG_DEV], "seq", axis=0, tiled=True),
    )
    full_view = jnp.ones((1, 1, 1), dtype=bool)
    long_scores = (
        jnp.einsum("qhe,khe->hqk", long_query, long_keys, preferred_element_type=jnp.float32)
        * score_scale
    )
    long_probs, long_lse = masked_softmax(long_scores, full_view)
    long_out = jnp.einsum(
        "hqk,khe->qhe",
        long_probs.astype(jnp.bfloat16),
        long_values,
        preferred_element_type=jnp.float32,
    )
    own_null = lax.dynamic_slice_in_dim(null_mask, seq_index * short_clips, short_clips, 0) == 1
    short_feats = jnp.where(own_null[:, None, None], null_embed[None], captions)
    long_feats = jnp.where(null_mask[clip_total - 1] == 1, null_embed, long_caption)
    text_rows = (short_clips + 1) * TXT_LEN
    all_short, all_long = (
        lax.all_gather(short_feats, "txt", axis=1, tiled=True),
        lax.all_gather(long_feats, "txt", axis=0, tiled=True),
    )
    feats = jnp.concatenate(
        [all_short.reshape(short_clips * TXT_LEN, all_short.shape[2]), all_long], axis=0
    )
    text_proj = jnp.dot(feats, text_matrix, preferred_element_type=jnp.float32).reshape(
        text_rows, 2, own_heads, HD
    )
    text_hat, text_inv = rms_parts(text_proj[:, 0])
    text_key_bf = (text_hat * text_gain).astype(jnp.bfloat16)
    text_value_bf = text_proj[:, 1].astype(jnp.bfloat16)
    key_clip = jnp.arange(text_rows, dtype=jnp.int32) // TXT_LEN
    key_place = jnp.arange(text_rows, dtype=jnp.int32) % TXT_LEN
    limits = jnp.concatenate(
        [
            lax.dynamic_slice_in_dim(text_lengths, seq_index * short_clips, short_clips, 0),
            text_lengths[clip_total - 1 :],
        ]
    )
    clip_match = key_clip[:, None] == jnp.arange(short_clips + 1, dtype=jnp.int32)[None, :]
    key_limit = jnp.sum(jnp.where(clip_match, limits[None, :], 0), axis=1)
    cross_view = ((clip_local[:, None] == key_clip[None, :]) & (key_place < key_limit)[None, :])[
        None
    ]
    cross_scores = (
        jnp.einsum("qhe,khe->hqk", query_bf, text_key_bf, preferred_element_type=jnp.float32)
        * score_scale
    )
    cross_probs, cross_lse = masked_softmax(cross_scores, cross_view)
    cross_out = jnp.einsum(
        "hqk,khe->qhe",
        cross_probs.astype(jnp.bfloat16),
        text_value_bf,
        preferred_element_type=jnp.float32,
    )
    attended = jnp.concatenate([long_out, short_out], axis=0)
    own_gates = lax.dynamic_slice_in_dim(head_gates, head_start, own_heads, 0)
    gate_tanh = jnp.tanh(own_gates)[None, :, None]
    combined_bf = (
        (attended + gate_tanh * cross_out).astype(jnp.bfloat16).reshape(token_count, own_width)
    )
    attn_out = head_sum(contract_cols(combined_bf, out_full))
    attn_hat, attn_inv = rms_parts(attn_out)
    tanh_attn = jnp.tanh(gate_attn)
    attn_normed = attn_hat * norm_gains[1]
    residual = hidden + tanh_attn * attn_normed
    res_hat, res_inv = rms_parts(residual)
    ffn_in_bf = (res_hat * norm_gains[2] * (1.0 + scale_ffn)).astype(jnp.bfloat16)
    gate_value = jnp.dot(ffn_in_bf, gate_full, preferred_element_type=jnp.float32)
    up_value = jnp.dot(ffn_in_bf, up_full, preferred_element_type=jnp.float32)
    sigmoid_gate = jax.nn.sigmoid(gate_value)
    silu_gate = gate_value * sigmoid_gate
    inner_bf = (silu_gate * up_value).astype(jnp.bfloat16)
    ffn_out = head_sum(contract_cols(inner_bf, down_full))
    ffn_hat, ffn_inv = rms_parts(ffn_out)
    tanh_ffn = jnp.tanh(gate_ffn)
    ffn_normed = ffn_hat * norm_gains[3]
    block_out = residual + tanh_ffn * ffn_normed
    upstream = cotangent.astype(jnp.float32)
    grad_ffn_normed = upstream * tanh_ffn
    grad_gate_ffn = upstream * ffn_normed * (1.0 - tanh_ffn * tanh_ffn)
    gain_three = grad_ffn_normed * ffn_hat
    grad_ffn_out = rms_back(grad_ffn_normed * norm_gains[3], ffn_hat, ffn_inv).astype(jnp.bfloat16)
    qkv_full, out_full, gate_full, up_full, down_full, text_full = (
        lax.all_gather(query_key_value, "seq", axis=0, tiled=True),
        lax.all_gather(out_weight, "seq", axis=0, tiled=True),
        lax.all_gather(gate_weight, "seq", axis=0, tiled=True),
        lax.all_gather(up_weight, "seq", axis=0, tiled=True),
        lax.all_gather(down_weight, "seq", axis=0, tiled=True),
        lax.all_gather(text_weight, "seq", axis=0, tiled=True),
    )
    qkv_matrix = qkv_full.reshape(model_width, 3 * own_width)
    text_matrix = text_full.reshape(text_full.shape[0], 2 * own_width)
    grad_inner = jnp.dot(grad_ffn_out, down_full, preferred_element_type=jnp.float32)
    down_term = contract_rows(grad_ffn_out, inner_bf)
    silu_slope = sigmoid_gate * (1.0 + gate_value * (1.0 - sigmoid_gate))
    grad_gate_bf = (grad_inner * up_value * silu_slope).astype(jnp.bfloat16)
    grad_up_bf = (grad_inner * silu_gate).astype(jnp.bfloat16)
    gate_term = contract_rows(ffn_in_bf, grad_gate_bf)
    up_term = contract_rows(ffn_in_bf, grad_up_bf)
    grad_ffn_in = head_sum(
        contract_cols(grad_gate_bf, gate_full) + contract_cols(grad_up_bf, up_full)
    )
    gain_two = grad_ffn_in * res_hat * (1.0 + scale_ffn)
    grad_scale_ffn = grad_ffn_in * res_hat * norm_gains[2]
    grad_residual = upstream + rms_back(
        grad_ffn_in * norm_gains[2] * (1.0 + scale_ffn), res_hat, res_inv
    )
    grad_attn_normed = grad_residual * tanh_attn
    grad_gate_attn = grad_residual * attn_normed * (1.0 - tanh_attn * tanh_attn)
    gain_one = grad_attn_normed * attn_hat
    grad_attn_bf = rms_back(grad_attn_normed * norm_gains[1], attn_hat, attn_inv).astype(
        jnp.bfloat16
    )
    grad_combined = jnp.dot(grad_attn_bf, out_full, preferred_element_type=jnp.float32).reshape(
        token_count, own_heads, HD
    )
    out_term = contract_rows(grad_attn_bf, combined_bf)
    grad_attended_bf = grad_combined.astype(jnp.bfloat16)
    grad_cross_bf = (gate_tanh * grad_combined).astype(jnp.bfloat16)
    own_gate_grad = jnp.sum(grad_combined * cross_out, axis=(0, 2)) * (
        1.0 - jnp.tanh(own_gates) ** 2
    )
    cross_again = recompute_probs(cross_scores, cross_view, cross_lse)
    grad_cross_probs = jnp.einsum(
        "qhe,khe->hqk", grad_cross_bf, text_value_bf, preferred_element_type=jnp.float32
    )
    cross_delta = jnp.sum(grad_cross_bf.astype(jnp.float32) * cross_out, axis=-1).T
    grad_cross_scores = (cross_again * (grad_cross_probs - cross_delta[:, :, None])).astype(
        jnp.bfloat16
    )
    grad_query = (
        jnp.einsum(
            "hqk,khe->qhe", grad_cross_scores, text_key_bf, preferred_element_type=jnp.float32
        )
        * score_scale
    )
    grad_text_key = (
        jnp.einsum("hqk,qhe->khe", grad_cross_scores, query_bf, preferred_element_type=jnp.float32)
        * score_scale
    )
    grad_text_value = jnp.einsum(
        "hqk,qhe->khe",
        cross_again.astype(jnp.bfloat16),
        grad_cross_bf,
        preferred_element_type=jnp.float32,
    )
    null_flags = jnp.concatenate([own_null, null_mask[clip_total - 1 :] == 1]).astype(jnp.float32)
    head_zeros = jnp.zeros((H, HD), jnp.float32)
    text_gain_grad = jnp.sum(grad_text_key * text_hat, axis=0)
    text_gain_row = lax.dynamic_update_slice_in_dim(
        head_zeros, text_gain_grad, head_start, 0
    ).reshape(model_width)
    grad_text_raw = rms_back(grad_text_key * text_gain, text_hat, text_inv)
    grad_text_bf = (
        jnp.stack([grad_text_raw, grad_text_value], axis=1)
        .astype(jnp.bfloat16)
        .reshape(text_rows, 2 * own_width)
    )
    text_term = contract_rows(feats, grad_text_bf).reshape(feats.shape[1], 2, own_width)
    grad_feats = contract_cols(grad_text_bf, text_matrix)
    null_term = jnp.einsum(
        "c,cld->ld",
        null_flags,
        grad_feats.reshape(short_clips + 1, TXT_LEN, grad_feats.shape[1]),
        precision=highest,
    )
    grad_short_bf = grad_attended_bf[LONG_DEV:]
    short_again = recompute_probs(short_scores, same_clip, short_lse)
    grad_short_probs = jnp.einsum(
        "qhe,khe->hqk", grad_short_bf, short_value, preferred_element_type=jnp.float32
    )
    short_delta = jnp.sum(grad_short_bf.astype(jnp.float32) * short_out, axis=-1).T
    grad_short_scores = (short_again * (grad_short_probs - short_delta[:, :, None])).astype(
        jnp.bfloat16
    )
    grad_short_q = (
        jnp.einsum("hqk,khe->qhe", grad_short_scores, short_key, preferred_element_type=jnp.float32)
        * score_scale
    )
    grad_short_k = (
        jnp.einsum(
            "hqk,qhe->khe", grad_short_scores, short_query, preferred_element_type=jnp.float32
        )
        * score_scale
    )
    grad_short_v = jnp.einsum(
        "hqk,qhe->khe",
        short_again.astype(jnp.bfloat16),
        grad_short_bf,
        preferred_element_type=jnp.float32,
    )
    grad_long_bf = grad_attended_bf[:LONG_DEV]
    long_again = recompute_probs(long_scores, full_view, long_lse)
    grad_long_probs = jnp.einsum(
        "qhe,khe->hqk", grad_long_bf, long_values, preferred_element_type=jnp.float32
    )
    long_delta = jnp.sum(grad_long_bf.astype(jnp.float32) * long_out, axis=-1).T
    grad_long_scores = (long_again * (grad_long_probs - long_delta[:, :, None])).astype(
        jnp.bfloat16
    )
    grad_long_q = (
        jnp.einsum("hqk,khe->qhe", grad_long_scores, long_keys, preferred_element_type=jnp.float32)
        * score_scale
    )
    long_prob_bf = long_again.astype(jnp.bfloat16)
    key_part = (
        jnp.einsum("hqk,qhe->khe", grad_long_scores, long_query, preferred_element_type=jnp.float32)
        * score_scale
    )
    value_part = jnp.einsum(
        "hqk,qhe->khe", long_prob_bf, grad_long_bf, preferred_element_type=jnp.float32
    )
    own_terms = lax.psum_scatter(
        jnp.stack([key_part, value_part], axis=1), "seq", scatter_dimension=0, tiled=True
    )
    grad_long_k = own_terms[:, 0]
    grad_long_v = own_terms[:, 1]
    grad_query = grad_query + jnp.concatenate([grad_long_q, grad_short_q], axis=0)
    grad_key = jnp.concatenate([grad_long_k, grad_short_k], axis=0)
    grad_value = jnp.concatenate([grad_long_v, grad_short_v], axis=0)
    grad_query_normed = rotate(grad_query, -position)
    grad_key_normed = rotate(grad_key, -position)
    query_gain_grad = jnp.sum(grad_query_normed * query_hat, axis=0)
    key_gain_grad = jnp.sum(grad_key_normed * key_hat, axis=0)
    grad_query_raw = rms_back(grad_query_normed * query_gain, query_hat, query_inv)
    grad_key_raw = rms_back(grad_key_normed * key_gain, key_hat, key_inv)
    grad_proj_bf = (
        jnp.stack([grad_query_raw, grad_key_raw, grad_value], axis=1)
        .astype(jnp.bfloat16)
        .reshape(token_count, 3 * own_width)
    )
    qkv_term = contract_rows(normed_in, grad_proj_bf).reshape(model_width, 3, own_width)
    grad_normed = head_sum(contract_cols(grad_proj_bf, qkv_matrix))
    gain_zero = grad_normed * hidden_hat * (1.0 + scale_attn)
    grad_scale_attn = grad_normed * hidden_hat * norm_gains[0]
    video_grad = grad_residual + rms_back(
        grad_normed * norm_gains[0] * (1.0 + scale_attn), hidden_hat, hidden_inv
    )
    qkv_grad, out_grad, gate_grad, up_grad, down_grad, text_grad = (
        lax.psum_scatter(qkv_term, "seq", scatter_dimension=0, tiled=True),
        lax.psum_scatter(out_term, "seq", scatter_dimension=0, tiled=True),
        lax.psum_scatter(gate_term, "seq", scatter_dimension=0, tiled=True),
        lax.psum_scatter(up_term, "seq", scatter_dimension=0, tiled=True),
        lax.psum_scatter(down_term, "seq", scatter_dimension=0, tiled=True),
        lax.psum_scatter(text_term, "seq", scatter_dimension=0, tiled=True),
    )
    half_rows = (jnp.arange(token_count, dtype=jnp.int32) % txt_count == txt_index).astype(
        jnp.float32
    )[:, None]
    grad_mod_tok = (
        jnp.concatenate([grad_scale_attn, grad_gate_attn, grad_scale_ffn, grad_gate_ffn], axis=1)
        * half_rows
    )
    own_grad_mod = lax.dot_general(
        selector, grad_mod_tok, (((0,), (0,)), ((), ())), precision=highest
    )
    full_grad_mod = jnp.zeros((clip_total, 4 * model_width), jnp.float32)
    full_grad_mod = lax.dynamic_update_slice_in_dim(
        full_grad_mod, own_grad_mod[:short_clips], seq_index * short_clips, 0
    )
    full_grad_mod = lax.dynamic_update_slice_in_dim(
        full_grad_mod, own_grad_mod[short_clips:], clip_total - 1, 0
    )
    slice_grad_mod = lax.psum_scatter(
        full_grad_mod, ("seq", "txt"), scatter_dimension=1, tiled=True
    )
    ada_weight_grad = lax.dot_general(
        shifted.astype(jnp.float32), slice_grad_mod, (((0,), (0,)), ((), ())), precision=highest
    )
    ada_bias_grad = jnp.sum(slice_grad_mod, axis=0)
    grad_shifted = lax.dot_general(
        slice_grad_mod, ada_weight.astype(jnp.float32), (((1,), (1,)), ((), ())), precision=highest
    )
    cond_value = condition.astype(jnp.float32)
    cond_sigmoid = jax.nn.sigmoid(cond_value)
    cond_part = grad_shifted * cond_sigmoid * (1.0 + cond_value * (1.0 - cond_sigmoid))
    gains_term = jnp.stack(
        [
            jnp.sum(gain_zero * half_rows, axis=0),
            jnp.sum(gain_one * half_rows, axis=0),
            jnp.sum(gain_two * half_rows, axis=0),
            jnp.sum(gain_three * half_rows, axis=0),
            lax.dynamic_update_slice_in_dim(head_zeros, query_gain_grad, head_start, 0).reshape(
                model_width
            ),
            lax.dynamic_update_slice_in_dim(head_zeros, key_gain_grad, head_start, 0).reshape(
                model_width
            ),
            text_gain_row,
        ],
        axis=0,
    )
    gates_term = lax.dynamic_update_slice_in_dim(
        jnp.zeros((H,), jnp.float32), own_gate_grad, head_start, 0
    )
    condition_grad, null_grad, norm_gains_grad, head_gates_grad = lax.psum(
        (cond_part, null_term, gains_term, gates_term), ("seq", "txt")
    )
    return (
        block_out.astype(jnp.bfloat16),
        video_grad,
        condition_grad,
        qkv_grad,
        out_grad,
        gate_grad,
        up_grad,
        down_grad,
        text_grad,
        ada_weight_grad,
        ada_bias_grad,
        null_grad,
        norm_gains_grad,
        head_gates_grad,
    )


def solution(mesh):
    placed = (
        P("seq", None),
        P("seq", None),
        P(),
        P("seq", "txt", None),
        P("txt", None),
        P("txt", None),
        P("seq", None, "txt"),
        P("seq", "txt"),
        P("seq", "txt"),
        P("seq", "txt"),
        P("seq", "txt"),
        P("seq", None, "txt"),
        P(None, ("seq", "txt")),
        P(("seq", "txt")),
        P(),
        P(),
        P("seq", None),
        P(),
        P(),
    )
    return jax.shard_map(
        local,
        mesh=mesh,
        in_specs=placed,
        out_specs=(
            P("seq", None),
            P("seq", None),
            P(),
            P("seq", None, "txt"),
            P("seq", "txt"),
            P("seq", "txt"),
            P("seq", "txt"),
            P("seq", "txt"),
            P("seq", None, "txt"),
            P(None, ("seq", "txt")),
            P(("seq", "txt")),
            P(),
            P(),
            P(),
        ),
        check_vma=False,
    )
```

profile of v0, /device:TPU:0, one launch (start us, length us, event | category | flops | bytes accessed | tf_op | source)
XLA Modules:
  0.0 2166.8 jit_solution(3268246575567116273)
XLA Ops:
  17.5 52.6 %all-gather.31.cloned.1.call-done = f32[32,192,49]{1,2,0:T(8,128)} async-done(((f32[1,192,49]{1,2,0:T(8,128)}), f32[32,192,49]{1,2,0:T(8,128)}) %all-gather.31.cloned.1.call-update) | async-done | bytes 1204240 | tf_op jit(solution)/shard_map/all_gather | solution.py:122
  85.7 52.3 %all-gather.13.cloned.1.call-done = bf16[1536,3,768]{2,0,1:T(8,128)(2,1)} async-done(((bf16[96,3,768]{2,0,1:T(8,128)(2,1)}), bf16[1536,3,768]{2,0,1:T(8,128)(2,1)}) %all-gather.13.cloned.1.call-update) | async-done | bytes 7077904 | tf_op jit(solution)/shard_map/all_gather | solution.py:141
  193.1 16.8 all-gather.15.cloned.1.call-done
  215.3 46.3 %all-gather.29.cloned.1.call-done = bf16[1024,1,12,64]{3,2,1,0:T(8,128)(2,1)} async-done(((bf16[64,1,12,64]{3,2,1,0:T(8,128)(2,1)}), bf16[1024,1,12,64]{3,2,1,0:T(8,128)(2,1)}) %all-gather.29.cloned.1.call-update) | async-done | bytes 1572880 | tf_op jit(solution)/shard_map/all_gather | solution.py:177
  272.2 90.8 %all-gather.19.cloned.1.call-done = bf16[4096,2,768]{2,1,0:T(2,128)(2,1)} async-done(((bf16[256,2,768]{2,1,0:T(2,128)(2,1)}), bf16[4096,2,768]{2,1,0:T(2,128)(2,1)}) %all-gather.19.cloned.1.call-update) | async-done | bytes 12582928 | tf_op jit(solution)/shard_map/all_gather | solution.py:146
  409.0 25.9 %all-gather.21.cloned.1.call-done = bf16[1536,768]{1,0:T(8,128)(2,1)} async-done(((bf16[96,768]{1,0:T(8,128)(2,1)}), bf16[1536,768]{1,0:T(8,128)(2,1)}) %all-gather.21.cloned.1.call-update) | async-done | bytes 2359312 | tf_op jit(solution)/shard_map/all_gather | solution.py:142
  441.6 48.3 %all-reduce.9.cloned.1.call-done = bf16[512,1536]{1,0:T(8,128)(2,1)} async-done(((bf16[512,1536]{1,0:T(8,128)(2,1)}), bf16[512,1536]{1,0:T(8,128)(2,1)}) %all-reduce.9.cloned.1.call-update) | async-done | bytes 1572880 | tf_op jit(solution)/shard_map/psum | solution.py:83
  500.9 53.4 %all-gather.23.cloned.1.call-done = bf16[1536,2048]{1,0:T(8,128)(2,1)} async-done(((bf16[96,2048]{1,0:T(8,128)(2,1)}), bf16[1536,2048]{1,0:T(8,128)(2,1)}) %all-gather.23.cloned.1.call-update) | async-done | bytes 6291472 | tf_op jit(solution)/shard_map/all_gather | solution.py:143
  563.0 54.1 %all-gather.25.cloned.1.call-done = bf16[1536,2048]{1,0:T(8,128)(2,1)} async-done(((bf16[96,2048]{1,0:T(8,128)(2,1)}), bf16[1536,2048]{1,0:T(8,128)(2,1)}) %all-gather.25.cloned.1.call-update) | async-done | bytes 6291472 | tf_op jit(solution)/shard_map/all_gather | solution.py:144
  627.8 52.4 %all-gather.27.cloned.1.call-done = bf16[1536,2048]{1,0:T(8,128)(2,1)} async-done(((bf16[96,2048]{1,0:T(8,128)(2,1)}), bf16[1536,2048]{1,0:T(8,128)(2,1)}) %all-gather.27.cloned.1.call-update) | async-done | bytes 6291472 | tf_op jit(solution)/shard_map/all_gather | solution.py:145
  689.1 49.4 %all-reduce.11.cloned.1.call-done = bf16[512,1536]{1,0:T(8,128)(2,1)} async-done(((bf16[512,1536]{1,0:T(8,128)(2,1)}), bf16[512,1536]{1,0:T(8,128)(2,1)}) %all-reduce.11.cloned.1.call-update) | async-done | bytes 1572880 | tf_op jit(solution)/shard_map/psum | solution.py:83
  767.5 49.9 %all-reduce.13.cloned.1.call-done = bf16[512,1536]{1,0:T(8,128)(2,1)} async-done(((bf16[512,1536]{1,0:T(8,128)(2,1)}), bf16[512,1536]{1,0:T(8,128)(2,1)}) %all-reduce.13.cloned.1.call-update) | async-done | bytes 1572880 | tf_op jit(solution)/shard_map/psum | solution.py:83
  886.0 54.6 %reduce-scatter.25.cloned.1.call-done = f32[64,1536]{1,0:T(8,128)} async-done(((f32[1024,1536]{1,0:T(8,128)}), f32[64,1536]{1,0:T(8,128)}) %reduce-scatter.25.cloned.1.call-update) | async-done | bytes 393232
  969.1 41.4 %all-reduce.15.cloned.1.call-done = bf16[512,1536]{1,0:T(8,128)(2,1)} async-done(((bf16[512,1536]{1,0:T(8,128)(2,1)}), bf16[512,1536]{1,0:T(8,128)(2,1)}) %all-reduce.15.cloned.1.call-update) | async-done | bytes 1572880 | tf_op jit(solution)/shard_map/psum | solution.py:83
  1043.4 27.4 %reshape.524 = bf16[4096,1536,1]{1,0,2:T(8,128)(2,1)} reshape(bf16[4096,2,768]{2,1,0:T(2,128)(2,1)} %all-gather.19.cloned.1.call-done) | data formatting | bytes 25165824 | tf_op jit(solution)/shard_map/reshape | solution.py:149
  1089.5 36.8 %reduce-scatter.27.cloned.1.call-done = f32[192,49]{1,0:T(8,128)} async-done(((f32[6144,49]{1,0:T(8,128)}), f32[192,49]{1,0:T(8,128)}) %reduce-scatter.27.cloned.1.call-update) | async-done | bytes 37648
  1190.6 45.2 %all-reduce.1 = (f32[7,1536]{1,0:T(8,128)}, f32[24]{0:T(128)}) all-reduce(f32[7,1536]{1,0:T(8,128)} %stack.53, f32[24]{0:T(128)} %multiply_dynamic-update-slice_fusion), channel_id=1, replica_groups=mesh['seq'=16,'txt'=2] {'seq','txt'}, use_global_device_ids=true, to_apply=%region_49.50 | all-reduce | flops 10776 | bytes 86208 | tf_op jit(solution)/shard_map/psum | solution.py:473
  1243.5 130.9 %reduce-scatter.23.cloned.1.call-done = f32[256,2,768]{2,0,1:T(8,128)} async-done(((f32[4096,2,768]{2,0,1:T(8,128)}), f32[256,2,768]{2,0,1:T(8,128)}) %reduce-scatter.23.cloned.1.call-update) | async-done | bytes 1572880 | tf_op jit(solution)/shard_map/reduce_scatter | solution.py:422
  1378.2 75.7 %reduce-scatter.15.cloned.1.call-done = f32[96,768]{1,0:T(8,128)} async-done(((f32[1536,768]{1,0:T(8,128)}), f32[96,768]{1,0:T(8,128)}) %reduce-scatter.15.cloned.1.call-update) | async-done | bytes 294928 | tf_op jit(solution)/shard_map/reduce_scatter | solution.py:418
  1453.9 137.2 %all-reduce.17.cloned.1.call-done = (f32[49,1024]{1,0:T(8,128)}, f32[64,4096]{1,0:T(8,128)}) async-done(((f32[49,1024]{1,0:T(8,128)}, f32[64,4096]{1,0:T(8,128)}), (f32[49,1024]{1,0:T(8,128)}, f32[64,4096]{1,0:T(8,128)})) %all-reduce.17.cloned.1.call-update) | async-done | bytes 1249296 | tf_op jit(solution)/shard_map/psum | solution.py:473
  1591.1 138.5 %reduce-scatter.21.cloned.1.call-done = f32[96,2048]{1,0:T(8,128)} async-done(((f32[1536,2048]{1,0:T(8,128)}), f32[96,2048]{1,0:T(8,128)}) %reduce-scatter.21.cloned.1.call-update) | async-done | bytes 786448 | tf_op jit(solution)/shard_map/reduce_scatter | solution.py:421
  1729.5 138.6 %reduce-scatter.17.cloned.1.call-done = f32[96,2048]{1,0:T(8,128)} async-done(((f32[1536,2048]{1,0:T(8,128)}), f32[96,2048]{1,0:T(8,128)}) %reduce-scatter.17.cloned.1.call-update) | async-done | bytes 786448 | tf_op jit(solution)/shard_map/reduce_scatter | solution.py:419
  1868.1 138.6 %reduce-scatter.19.cloned.1.call-done = f32[96,2048]{1,0:T(8,128)} async-done(((f32[1536,2048]{1,0:T(8,128)}), f32[96,2048]{1,0:T(8,128)}) %reduce-scatter.19.cloned.1.call-update) | async-done | bytes 786448 | tf_op jit(solution)/shard_map/reduce_scatter | solution.py:420
  2006.7 149.5 %reduce-scatter.13.cloned.1.call-done = f32[96,3,768]{2,0,1:T(8,128)} async-done(((f32[1536,3,768]{2,0,1:T(8,128)}), f32[96,3,768]{2,0,1:T(8,128)}) %reduce-scatter.13.cloned.1.call-update) | async-done | bytes 884752 | tf_op jit(solution)/shard_map/reduce_scatter | solution.py:417
  (519 shorter events, 443.4 us)
Async XLA Ops:
  7.2 62.8 %all-gather.31.cloned.1.call-start = ((), (), s32[]{:S(2)}) async-start(), calls=%async_computation.27 | async-start | bytes 1892352 | tf_op jit(solution)/shard_map/all_gather | solution.py:122
  10.0 128.0 %all-gather.13.cloned.1.call-start = ((), (), s32[]{:S(2)}) async-start(), calls=%async_computation.8 | async-start | bytes 7520256 | tf_op jit(solution)/shard_map/all_gather | solution.py:141
  10.7 199.2 %all-gather.15.cloned.1.call-start = ((), (), s32[]{:S(2)}) async-start(), calls=%async_computation.9 | async-start | bytes 4456448 | tf_op jit(solution)/shard_map/all_gather | solution.py:176
  15.3 142.2 %copy-start.88 = (f32[12,64]{1,0:T(8,128)}, f32[12,64]{1,0:T(8,128)S(1)}, u32[]{:S(2)}) copy-start(f32[12,64]{1,0:T(8,128)S(1)} %get-tuple-element.152) | copy-start | bytes 9220
  160.7 100.8 %all-gather.29.cloned.1.call-start = ((), (), s32[]{:S(2)}) async-start(), calls=%async_computation.26 | async-start | bytes 4456448 | tf_op jit(solution)/shard_map/all_gather | solution.py:177
  163.1 199.9 %all-gather.19.cloned.1.call-start = ((), (), s32[]{:S(2)}) async-start(), calls=%async_computation.11 | async-start | bytes 13369344 | tf_op jit(solution)/shard_map/all_gather | solution.py:146
  163.7 229.2 %all-gather.17.cloned.1.call-start = ((), (), s32[]{:S(2)}) async-start(), calls=%async_computation.10 | async-start | bytes 2359296 | tf_op jit(solution)/shard_map/all_gather | solution.py:196
  164.9 270.1 %all-gather.21.cloned.1.call-start = ((), (), s32[]{:S(2)}) async-start(), calls=%async_computation.12 | async-start | bytes 2506752 | tf_op jit(solution)/shard_map/all_gather | solution.py:142
  165.6 324.2 %all-reduce.9.cloned.1.call-start = ((), (), s32[]{:S(2)}) async-start(), calls=%async_computation.13 | async-start | bytes 3145728 | tf_op jit(solution)/shard_map/psum | solution.py:83
  439.4 114.8 %all-gather.23.cloned.1.call-start = ((), (), s32[]{:S(2)}) async-start(), calls=%async_computation.14 | async-start | bytes 6684672 | tf_op jit(solution)/shard_map/all_gather | solution.py:143
  440.2 177.0 %all-gather.25.cloned.1.call-start = ((), (), s32[]{:S(2)}) async-start(), calls=%async_computation.15 | async-start | bytes 6684672 | tf_op jit(solution)/shard_map/all_gather | solution.py:144
  440.8 239.4 %all-gather.27.cloned.1.call-start = ((), (), s32[]{:S(2)}) async-start(), calls=%async_computation.16 | async-start | bytes 6684672 | tf_op jit(solution)/shard_map/all_gather | solution.py:145
  441.5 297.0 %all-reduce.11.cloned.1.call-start = ((), (), s32[]{:S(2)}) async-start(), calls=%async_computation.17 | async-start | bytes 3145728 | tf_op jit(solution)/shard_map/psum | solution.py:83
  688.2 129.1 %all-reduce.13.cloned.1.call-start = ((), (), s32[]{:S(2)}) async-start(), calls=%async_computation.18 | async-start | bytes 3145728 | tf_op jit(solution)/shard_map/psum | solution.py:83
  765.7 174.9 %reduce-scatter.25.cloned.1.call-start = ((), (), s32[]{:S(2)}) async-start(), calls=%async_computation.28 | async-start | bytes 6684672
  855.2 155.3 %all-reduce.15.cloned.1.call-start = ((), (), s32[]{:S(2)}) async-start(), calls=%async_computation.19 | async-start | bytes 3145728 | tf_op jit(solution)/shard_map/psum | solution.py:83
  959.8 166.5 %reduce-scatter.27.cloned.1.call-start = ((), (), s32[]{:S(2)}) async-start(), calls=%async_computation.29 | async-start | bytes 3244032
  1024.7 349.7 %reduce-scatter.23.cloned.1.call-start = ((), (), s32[]{:S(2)}) async-start(), calls=%async_computation.25 | async-start | bytes 26738688 | tf_op jit(solution)/shard_map/reduce_scatter | solution.py:422
  1038.1 415.8 %reduce-scatter.15.cloned.1.call-start = ((), (), s32[]{:S(2)}) async-start(), calls=%async_computation.21 | async-start | bytes 5013504 | tf_op jit(solution)/shard_map/reduce_scatter | solution.py:418
  1043.3 547.8 %all-reduce.17.cloned.1.call-start = ((), (), s32[]{:S(2)}) async-start(), calls=%async_computation.30 | async-start | bytes 2555904 | tf_op jit(solution)/shard_map/psum | solution.py:473
  1128.3 601.2 %reduce-scatter.21.cloned.1.call-start = ((), (), s32[]{:S(2)}) async-start(), calls=%async_computation.24 | async-start | bytes 13369344 | tf_op jit(solution)/shard_map/reduce_scatter | solution.py:421
  1137.1 731.1 %reduce-scatter.17.cloned.1.call-start = ((), (), s32[]{:S(2)}) async-start(), calls=%async_computation.22 | async-start | bytes 13369344 | tf_op jit(solution)/shard_map/reduce_scatter | solution.py:419
  1150.0 856.7 %reduce-scatter.19.cloned.1.call-start = ((), (), s32[]{:S(2)}) async-start(), calls=%async_computation.23 | async-start | bytes 13369344 | tf_op jit(solution)/shard_map/reduce_scatter | solution.py:420
  1161.3 994.9 %reduce-scatter.13.cloned.1.call-start = ((), (), s32[]{:S(2)}) async-start(), calls=%async_computation.20 | async-start | bytes 15040512 | tf_op jit(solution)/shard_map/reduce_scatter | solution.py:417
  (148 other events, 1583.6 us)
Sparse Core Ops, SparseCore 0:
  11.5 58.4 all-gather.30
  72.3 65.6 all-gather.12
  160.9 48.9 all-gather.14
  212.5 49.0 all-gather.28
  263.7 99.2 all-gather.18
  365.0 25.3 all-gather.16
  392.7 42.2 all-gather.20
  439.6 50.2 all-reduce.8
  492.4 61.8 all-gather.22
  556.7 60.4 all-gather.24
  619.7 60.4 all-gather.26
  688.3 50.0 all-reduce.10
  765.8 51.4 all-reduce.12
  855.3 85.2 reduce-scatter.24
  959.9 50.6 all-reduce.14
  1024.8 101.4 reduce-scatter.26
  1130.8 243.5 reduce-scatter.22
  1379.2 74.6 reduce-scatter.14
  1460.5 130.5 all-reduce.16
  1595.5 133.9 reduce-scatter.20
  1734.2 133.8 reduce-scatter.16
  1872.7 133.8 reduce-scatter.18
  2011.4 144.7 reduce-scatter.12
where the time goes:
time: 2180 us; the launch traced here: 2170 us
  waiting for transfers between devices  1640 us (75%)
  matrix products  209 us (10%)
  local copies, waits for them, and re-layouts  162 us (7%)
  other arithmetic  84.5 us (4%)
  blocking collectives  54.5 us (2%)
    psum x4, waiting for transfers between devices, head_sum(): return lax.psum(values.astype(jnp.bfloat16), 'txt').astype(jnp.float32)  189 us
    reduce_scatter x1, waiting for transfers between devices, local(): lax.psum_scatter(qkv_term, 'seq', scatter_dimension=0, tiled=True)  149 us
    reduce_scatter x1, waiting for transfers between devices, local(): lax.psum_scatter(gate_term, 'seq', scatter_dimension=0, tiled=True)  139 us
    reduce_scatter x1, waiting for transfers between devices, local(): lax.psum_scatter(up_term, 'seq', scatter_dimension=0, tiled=True)  139 us
    reduce_scatter x1, waiting for transfers between devices, local(): lax.psum_scatter(down_term, 'seq', scatter_dimension=0, tiled=True)  138 us
    psum x1, waiting for transfers between devices, local(): lax.psum((cond_part, null_term, gains_term, gates_term), ('seq', 'txt'))  137 us
    reduce_scatter x1, waiting for transfers between devices, local(): lax.psum_scatter(text_term, 'seq', scatter_dimension=0, tiled=True)  131 us
    unnamed x25, waiting for transfers between devices  95.6 us
  transfers between devices with their start and end apart: 23, of which 22 were waited for; matrix products, arithmetic and copies ran while one was open for 14% of the time, Pallas kernels for 0%

commit v1 on v0

v1 whole, which is shorter than its diff:
```python
import functools
import math

import jax
import jax.numpy as jnp
from jax import lax
from jax.experimental import pallas as pl
from jax.experimental.pallas import tpu as pltpu
from jax.sharding import PartitionSpec as P

H = 24
HD = 64
TXT_LEN = 64
LONG_DEV = 64

epsilon = 1e-05
negative = -1e30
highest = lax.Precision.HIGHEST
bf16 = jnp.bfloat16
f32 = jnp.float32


def layout(lengths_row, seq_index, long_rows, short_rows):
    clip_count = lengths_row.shape[0]
    clip_ends = jnp.cumsum(lengths_row)
    clip_starts = clip_ends - lengths_row
    row_ids = jnp.arange(short_rows, dtype=jnp.int32)
    local_clip = jnp.sum(
        (row_ids[:, None] >= clip_ends[None, : clip_count - 1]).astype(jnp.int32), axis=1
    )
    chosen = local_clip[:, None] == jnp.arange(clip_count, dtype=jnp.int32)[None, :]
    clip_begin = jnp.sum(jnp.where(chosen, clip_starts[None, :], 0), axis=1)
    clip_local = jnp.concatenate([jnp.full((long_rows,), clip_count, jnp.int32), local_clip])
    long_place = seq_index * long_rows + jnp.arange(long_rows, dtype=jnp.int32)
    position = jnp.concatenate([long_place, row_ids - clip_begin])
    return (clip_local, position)


def rms_parts(values):
    inverse = lax.rsqrt(jnp.mean(values * values, axis=-1, keepdims=True) + epsilon)
    return (values * inverse, inverse)


def rms_back(grad_hat, normed, inverse):
    return inverse * (grad_hat - normed * jnp.mean(grad_hat * normed, axis=-1, keepdims=True))


def dot(left_side, right_side):
    return jnp.dot(left_side, right_side, preferred_element_type=f32)


def dot_pieces(left_side, pieces):
    depth = pieces[0].shape[0]
    total = 0.0
    for place, piece in enumerate(pieces):
        total = total + dot(left_side[:, place * depth : (place + 1) * depth], piece)
    return total


def contract_rows(left_side, right_side):
    return lax.dot_general(
        left_side, right_side, (((0,), (0,)), ((), ())), preferred_element_type=f32
    )


def contract_cols(left_side, right_side):
    return lax.dot_general(
        left_side, right_side, (((1,), (1,)), ((), ())), preferred_element_type=f32
    )


def swap_txt(values):
    return lax.ppermute(values, "txt", [(0, 1), (1, 0)])


def rounded(values):
    return lax.reduce_precision(values, exponent_bits=8, mantissa_bits=7)


def fence(*values):
    return lax.optimization_barrier(values)


class Grid:
    def __init__(self):
        self.count = lax.axis_size("seq")
        self.outer_count = 4
        self.inner_count = self.count // 8
        self.index = lax.axis_index("seq")
        self.core = self.index % 2
        self.inner = (self.index // 2) % self.inner_count
        self.outer = self.index // (2 * self.inner_count)

    def send(self, values, outer=0, inner=0, core=0):
        pairs = []
        for index in range(self.count):
            to_core = (index + core) % 2
            to_inner = (index // 2 + inner) % self.inner_count
            to_outer = (index // (2 * self.inner_count) + outer) % self.outer_count
            pairs.append((index, (to_outer * self.inner_count + to_inner) * 2 + to_core))
        return lax.ppermute(values, "seq", pairs)

    def lines(self):
        step = 2 * self.inner_count
        return [[first + step * k for k in range(self.outer_count)] for first in range(step)]

    def owners(self):
        place = jnp.arange(self.count, dtype=jnp.int32)
        outer = place % self.outer_count
        inner = (self.inner - (place // self.outer_count) % self.inner_count) % self.inner_count
        core = (self.core + place // (self.outer_count * self.inner_count)) % 2
        return (outer * self.inner_count + inner) * 2 + core


def gather_outer(grid, block):
    return lax.all_gather(block, "seq", axis=0, tiled=True, axis_index_groups=grid.lines())


def send_inner(grid, near):
    return [grid.send(near, inner=step) for step in range(1, grid.inner_count)]


def send_core(grid, pieces):
    return [grid.send(piece, core=1) for piece in pieces]


def stack(pieces):
    return jnp.concatenate(pieces, axis=0) if len(pieces) > 1 else pieces[0]


def add_blocks(*refs):
    *sources, target = refs
    total = sources[0][...].astype(f32)
    for source in sources[1:]:
        total = total + source[...].astype(f32)
    target[...] = total.astype(target.dtype)


def add_rows(arrays, starts, rows):
    cols = arrays[0].shape[1]
    block = 256 if rows % 256 == 0 else 128 if rows % 128 == 0 else rows

    def from_row(start):
        return pl.BlockSpec((block, cols), lambda i: (start // block + i, 0))

    return pl.pallas_call(
        add_blocks,
        grid=(rows // block,),
        in_specs=[from_row(start) for start in starts],
        out_specs=from_row(0),
        out_shape=jax.ShapeDtypeStruct((rows, cols), bf16),
        cost_estimate=pl.CostEstimate(flops=1, bytes_accessed=1, transcendentals=0),
        compiler_params=pltpu.CompilerParams(vmem_limit_bytes=48 * 1024 * 1024),
        name="add_rows",
    )(*arrays)


def core_away(grid, kept, moved):
    rows = kept.shape[0] // grid.inner_count
    return [
        add_rows([kept, moved], [step * rows] * 2, rows) for step in range(1, grid.inner_count)
    ]


def inner_total(grid, kept, moved, arrived):
    rows = kept.shape[0] // grid.inner_count
    return add_rows([kept, moved] + arrived, [0] * (2 + len(arrived)), rows)


def swap_inner(grid, away):
    return [grid.send(part, inner=-step) for step, part in enumerate(away, 1)]


def sum_outer(grid, total):
    return lax.psum_scatter(
        total, "seq", scatter_dimension=0, tiled=True, axis_index_groups=grid.lines()
    )


def pair_sum(grid, values, bit):
    pairs = [(index, index ^ bit) for index in range(grid.count)]
    return lax.ppermute(values, "seq", pairs)


def turn_stage(values, axis, size, own, send):
    moved = [lax.dynamic_index_in_dim(values, own, axis, keepdims=False)]
    for step in range(1, size):
        piece = lax.dynamic_index_in_dim(values, (own + step) % size, axis, keepdims=False)
        moved.append(send(piece, step))
    stacked = jnp.stack(moved, axis=axis)
    order = (own - jnp.arange(size, dtype=jnp.int32)) % size
    return jnp.take(stacked, order, axis=axis)


def turn_seq(grid, values):
    rest = values.shape[1:]
    values = values.reshape((grid.outer_count, grid.inner_count, 2) + rest)
    values = turn_stage(
        values, 0, grid.outer_count, grid.outer, lambda v, k: grid.send(v, outer=k)
    )
    values = turn_stage(
        values, 1, grid.inner_count, grid.inner, lambda v, k: grid.send(v, inner=k)
    )
    values = turn_stage(values, 2, 2, grid.core, lambda v, k: grid.send(v, core=k))
    return values.reshape((grid.count,) + rest)


def sum_seq(grid, values, bit):
    while bit < grid.count:
        values = values + pair_sum(grid, values, bit)
        bit *= 2
    return values


def copy_blocks(to_order, count, order_ref, source_ref, target_ref):
    width = source_ref.shape[1] // count
    for block in range(count):
        moved = pl.ds(pl.multiple_of(order_ref[block] * width, width), width)
        plain = pl.ds(block * width, width)
        if to_order:
            target_ref[:, plain] = source_ref[:, moved]
        else:
            target_ref[:, moved] = source_ref[:, plain]


def reorder_columns(values, order, to_order):
    rows, cols = values.shape
    count = order.shape[0]
    width = cols // count
    if width % 128:
        taken = order if to_order else jnp.argsort(order)
        return jnp.take(values.reshape(rows, count, width), taken, axis=1).reshape(rows, cols)
    return pl.pallas_call(
        functools.partial(copy_blocks, to_order, count),
        out_shape=jax.ShapeDtypeStruct(values.shape, values.dtype),
        in_specs=[
            pl.BlockSpec(memory_space=pltpu.SMEM),
            pl.BlockSpec(memory_space=pltpu.VMEM),
        ],
        out_specs=pl.BlockSpec(memory_space=pltpu.VMEM),
        name="reorder_columns",
    )(order, values)


def split_three(values):
    high = rounded(values)
    rest = values - high
    middle = rounded(rest)
    return high.astype(bf16), middle.astype(bf16), (rest - middle).astype(bf16)


def exact_dot(values, one_hot):
    rows = values.shape[0]
    parts = dot(jnp.concatenate(split_three(values), axis=0), one_hot)
    return parts[:rows] + parts[rows : 2 * rows] + parts[2 * rows :]


def choose(clip, rows):
    chosen = rows[-1:]
    for index in range(rows.shape[0] - 1):
        chosen = jnp.where(clip == index, rows[index : index + 1], chosen)
    return chosen


def add_clip_sums(clip, values, sums_ref):
    @pl.when(pl.program_id(0) == 0)
    def _():
        sums_ref[...] = jnp.zeros_like(sums_ref)

    for index in range(sums_ref.shape[0]):
        part = jnp.sum(jnp.where(clip == index, values, 0.0), axis=0, keepdims=True)
        sums_ref[index : index + 1, :] += part


def add_pair(own_ref, moved_ref):
    return own_ref[...].astype(f32) + moved_ref[...].astype(f32)


def enter_rows(clip_ref, hidden_ref, part_ref, moved_ref, tanh_ref, scale_ref, gains_ref, res_ref, in_ref):
    clip = clip_ref[...]
    attn_hat, _ = rms_parts(add_pair(part_ref, moved_ref))
    tanh_tok = choose(clip, tanh_ref[...])
    residual = hidden_ref[...].astype(f32) + tanh_tok * attn_hat * gains_ref[1:2]
    res_hat, _ = rms_parts(residual)
    res_ref[...] = residual
    in_ref[...] = (res_hat * gains_ref[2:3] * choose(clip, scale_ref[...])).astype(bf16)


def leave_rows(clip_ref, res_ref, part_ref, moved_ref, up_ref, tanh_ref, gains_ref, out_ref, grad_ref, sums_ref):
    clip = clip_ref[...]
    hat, inverse = rms_parts(add_pair(part_ref, moved_ref))
    upstream = up_ref[...].astype(f32)
    tanh_tok = choose(clip, tanh_ref[...])
    out_ref[...] = (res_ref[...] + tanh_tok * hat * gains_ref[3:4]).astype(bf16)
    grad_ref[...] = rms_back(upstream * tanh_tok * gains_ref[3:4], hat, inverse).astype(bf16)
    add_clip_sums(clip, upstream * hat, sums_ref)


def middle_rows(
    clip_ref, res_ref, grad_part_ref, grad_moved_ref, up_ref, part_ref, moved_ref, tanh_ref,
    scale_ref, gains_ref, grad_res_ref, grad_attn_ref, res_sums_ref, attn_sums_ref,
):
    clip = clip_ref[...]
    grad = add_pair(grad_part_ref, grad_moved_ref)
    hat, inverse = rms_parts(res_ref[...])
    add_clip_sums(clip, grad * hat, res_sums_ref)
    grad_hat = grad * gains_ref[2:3] * choose(clip, scale_ref[...])
    grad_res = up_ref[...].astype(f32) + rms_back(grad_hat, hat, inverse)
    grad_res_ref[...] = grad_res
    hat, inverse = rms_parts(add_pair(part_ref, moved_ref))
    add_clip_sums(clip, grad_res * hat, attn_sums_ref)
    grad_hat = grad_res * gains_ref[1:2] * choose(clip, tanh_ref[...])
    grad_attn_ref[...] = rms_back(grad_hat, hat, inverse).astype(bf16)


def last_rows(
    clip_ref, hidden_ref, part_ref, moved_ref, grad_res_ref, scale_ref, gains_ref, high_ref, low_ref,
    sums_ref,
):
    clip = clip_ref[...]
    grad = add_pair(part_ref, moved_ref)
    hat, inverse = rms_parts(hidden_ref[...].astype(f32))
    add_clip_sums(clip, grad * hat, sums_ref)
    grad_hat = grad * gains_ref[0:1] * choose(clip, scale_ref[...])
    total = grad_res_ref[...] + rms_back(grad_hat, hat, inverse)
    high = total.astype(bf16)
    high_ref[...] = high
    low_ref[...] = (total - high.astype(f32)).astype(bf16)


def row_call(body, name, arrays, tables, outs, sums):
    count, width = arrays[1].shape
    rows = count // 4

    def by_rows(array):
        return pl.BlockSpec((rows, array.shape[1]), lambda i: (i, 0))

    def whole(array):
        return pl.BlockSpec(array.shape, lambda i: (0, 0))

    out_shapes = [jax.ShapeDtypeStruct((count, width), kind) for kind in outs]
    sum_shapes = [jax.ShapeDtypeStruct((tables[0].shape[0], width), f32)] * sums
    return pl.pallas_call(
        body,
        grid=(4,),
        in_specs=[by_rows(array) for array in arrays] + [whole(table) for table in tables],
        out_specs=[by_rows(shape) for shape in out_shapes] + [whole(shape) for shape in sum_shapes],
        out_shape=out_shapes + sum_shapes,
        cost_estimate=pl.CostEstimate(flops=1, bytes_accessed=1, transcendentals=0),
        compiler_params=pltpu.CompilerParams(vmem_limit_bytes=48 * 1024 * 1024),
        name=name,
    )(*arrays, *tables)


def head_means(values):
    first = lax.broadcasted_iota(jnp.int32, values.shape, 1) < HD
    front = jnp.sum(jnp.where(first, values, 0.0), axis=1, keepdims=True)
    back = jnp.sum(jnp.where(first, 0.0, values), axis=1, keepdims=True)
    return jnp.where(first, front, back) * (1.0 / HD)


def turn_lanes(values, cosine, sine):
    lane = lax.broadcasted_iota(jnp.int32, values.shape, 1) % HD
    ahead = pltpu.roll(values, 2 * HD - HD // 2, 1)
    behind = pltpu.roll(values, HD // 2, 1)
    return values * cosine + jnp.where(lane < HD // 2, -ahead, behind) * sine


def norm_heads(values_ref, gain_ref, cos_ref, sin_ref, out_ref):
    cosine, sine = cos_ref[...], sin_ref[...]
    for start in range(0, out_ref.shape[1], 2 * HD):
        part = slice(start, start + 2 * HD)
        values = values_ref[:, part]
        hat = values * lax.rsqrt(head_means(values * values) + epsilon)
        out_ref[:, part] = turn_lanes(hat * gain_ref[:, part], cosine, sine).astype(bf16)


def norm_heads_back(*refs):
    values_ref, gain_ref, cos_ref, sin_ref, *grad_refs, out_ref, sums_ref = refs
    cosine, sine = cos_ref[...], sin_ref[...]

    @pl.when(pl.program_id(0) == 0)
    def _():
        sums_ref[...] = jnp.zeros_like(sums_ref)

    for start in range(0, out_ref.shape[1], 2 * HD):
        part = slice(start, start + 2 * HD)
        values = values_ref[:, part]
        inverse = lax.rsqrt(head_means(values * values) + epsilon)
        hat = values * inverse
        grad = grad_refs[0][:, part]
        for grad_ref in grad_refs[1:]:
            grad = grad + grad_ref[:, part]
        grad = turn_lanes(grad, cosine, -sine)
        sums_ref[:, part] += jnp.sum(grad * hat, axis=0, keepdims=True)
        grad = grad * gain_ref[:, part]
        out_ref[:, part] = (inverse * (grad - hat * head_means(grad * hat))).astype(bf16)


def head_call(body, name, values, column, gain, turns, grads=()):
    count, width = turns[0].shape[0], gain.shape[1]
    rows = count // 4
    by_rows = pl.BlockSpec((rows, width), lambda i: (i, 0))
    whole = pl.BlockSpec((1, width), lambda i: (0, 0))
    turn = pl.BlockSpec((rows, 2 * HD), lambda i: (i, 0))
    out_shape = [jax.ShapeDtypeStruct((count, width), bf16)]
    out_specs = [by_rows]
    if grads:
        out_shape.append(jax.ShapeDtypeStruct((1, width), f32))
        out_specs.append(whole)
    results = pl.pallas_call(
        body,
        grid=(4,),
        in_specs=[pl.BlockSpec((rows, width), lambda i: (i, column)), whole, turn, turn]
        + [by_rows] * len(grads),
        out_specs=out_specs,
        out_shape=out_shape,
        cost_estimate=pl.CostEstimate(flops=1, bytes_accessed=1, transcendentals=0),
        compiler_params=pltpu.CompilerParams(vmem_limit_bytes=48 * 1024 * 1024),
        name=name,
    )(values, gain, *turns, *grads)
    return results if grads else results[0]


def attend_heads(clip_ref, key_clip_ref, query_ref, key_ref, value_ref, out_ref, total_ref):
    visible = clip_ref[...] == key_clip_ref[...]
    for start in range(0, 2 * HD, HD):
        head = slice(start, start + HD)
        scores = contract_cols(query_ref[:, head], key_ref[:, head]) * HD ** (-0.5)
        scores = jnp.where(visible, scores, negative)
        peak = jnp.max(scores, axis=1, keepdims=True)
        exponent = jnp.exp(scores - peak)
        total = jnp.sum(exponent, axis=1, keepdims=True)
        out_ref[:, head] = dot((exponent / total).astype(bf16), value_ref[:, head])
        total_ref[:, head] = jnp.broadcast_to(peak + jnp.log(total), (total_ref.shape[0], HD))


def attend_heads_back(
    clip_ref, key_clip_ref, query_ref, key_ref, value_ref, grad_ref, out_ref, total_ref,
    grad_query_ref, grad_key_ref, grad_value_ref,
):
    visible = clip_ref[...] == key_clip_ref[...]
    for start in range(0, 2 * HD, HD):
        head = slice(start, start + HD)
        query, key = query_ref[:, head], key_ref[:, head]
        grad = grad_ref[:, head]
        scores = contract_cols(query, key) * HD ** (-0.5)
        weights = jnp.where(visible, jnp.exp(scores - total_ref[:, start : start + 1]), 0.0)
        delta = jnp.sum(grad.astype(f32) * out_ref[:, head], axis=1, keepdims=True)
        grad_scores = weights * (contract_cols(grad, value_ref[:, head]) - delta)
        grad_scores = grad_scores.astype(bf16)
        grad_query_ref[:, head] = dot(grad_scores, key) * HD ** (-0.5)
        grad_key = contract_rows(grad_scores, query) * HD ** (-0.5)
        grad_key_ref[:, head] = grad_key.astype(grad_key_ref.dtype)
        grad_value = contract_rows(weights.astype(bf16), grad)
        grad_value_ref[:, head] = grad_value.astype(grad_value_ref.dtype)


def attend_call(name, clips, key_clips, query, key, value, value_column=0, back=(), kind=f32):
    count, keys, width = query.shape[0], key.shape[0], query.shape[1]
    first = value_column // (2 * HD)
    queries = pl.BlockSpec((count, 2 * HD), lambda i: (0, i))
    seen = pl.BlockSpec((keys, 2 * HD), lambda i: (0, i))
    whole = [pl.BlockSpec(array.shape, lambda i: (0, 0)) for array in (clips, key_clips)]
    out_shape = [jax.ShapeDtypeStruct((count, width), f32)]
    if back:
        out_shape += [jax.ShapeDtypeStruct((keys, width), kind)] * 2
        out_specs = [queries, seen, seen]
    else:
        out_shape += out_shape
        out_specs = [queries, queries]
    return pl.pallas_call(
        attend_heads_back if back else attend_heads,
        grid=(width // (2 * HD),),
        in_specs=whole
        + [queries, seen, pl.BlockSpec((keys, 2 * HD), lambda i: (0, first + i))]
        + [queries] * len(back),
        out_specs=out_specs,
        out_shape=out_shape,
        cost_estimate=pl.CostEstimate(flops=1, bytes_accessed=1, transcendentals=0),
        compiler_params=pltpu.CompilerParams(vmem_limit_bytes=48 * 1024 * 1024),
        name=name,
    )(clips, key_clips, query, key, value, *back)


def local(
    video_tokens,
    cotangent,
    condition,
    captions,
    long_caption,
    null_embed,
    query_key_value,
    out_weight,
    gate_weight,
    up_weight,
    down_weight,
    text_weight,
    ada_weight,
    ada_bias,
    norm_gains,
    head_gates,
    clip_lengths,
    null_mask,
    text_lengths,
):
    grid = Grid()
    seq_index = grid.index
    seq_count = grid.count
    txt_index = lax.axis_index("txt")
    first_half = txt_index == 0
    token_count, model_width = video_tokens.shape
    depth = query_key_value.shape[0]
    text_depth, text_width = text_weight.shape[0], captions.shape[2]
    half_width = model_width // 2
    own_heads = query_key_value.shape[2] // HD
    own_width = own_heads * HD
    head_start = txt_index * own_heads
    clip_total = condition.shape[0]
    short_clips = clip_lengths.shape[1]
    clip_local, position = layout(clip_lengths[0], seq_index, LONG_DEV, token_count - LONG_DEV)
    owners = grid.owners()
    text_rows = (short_clips + 1) * TXT_LEN

    half_text = text_width // 2
    text_block = text_weight.reshape(text_depth, 2 * own_width)

    qkv_block, condition = fence(query_key_value.reshape(depth, 3 * own_width), condition)
    qkv_near = gather_outer(grid, qkv_block)
    shifted = jax.nn.silu(condition.astype(f32)).astype(bf16)
    mod_part = dot(shifted, ada_weight) + ada_bias
    short_part = mod_part[: clip_total - 1].reshape(seq_count, short_clips, mod_part.shape[1])
    long_part = jnp.broadcast_to(
        mod_part[clip_total - 1 :][None], (seq_count, 1, mod_part.shape[1])
    )
    own_part = turn_seq(grid, jnp.concatenate([short_part, long_part], axis=1))
    other_part = swap_txt(own_part)
    own_null = lax.dynamic_slice_in_dim(null_mask, seq_index * short_clips, short_clips, 0) == 1
    short_feats = jnp.where(own_null[:, None, None], null_embed[None], captions)
    long_feats = jnp.where(null_mask[clip_total - 1] == 1, null_embed, long_caption)
    own_feats = jnp.concatenate([short_feats, long_feats[None]], axis=0).reshape(-1, text_width)
    own_feats = reorder_columns(own_feats, owners, True)

    columns = jnp.arange(model_width, dtype=jnp.int32)
    column_order = jnp.repeat(owners, depth) * depth + columns % depth
    one_hot = (columns[:, None] == column_order[None, :]).astype(bf16)
    hidden = dot(video_tokens, one_hot).astype(bf16)
    hidden_hat, _ = rms_parts(hidden.astype(f32))
    clip_column = clip_local[:, None]
    tkey_block, tval_block = text_block[:, :own_width], text_block[:, own_width:]
    qkv_near, own_part, other_part, own_feats, tkey_block, tval_block, out_weight = fence(
        qkv_near, own_part, other_part, own_feats, tkey_block, tval_block, out_weight
    )

    qkv_y = send_inner(grid, qkv_near)
    qkv_near_core = send_core(grid, [qkv_near])
    tkey_near = gather_outer(grid, tkey_block)
    out_near = gather_outer(grid, out_weight)
    other_feats = swap_txt(own_feats)
    own_mod = jnp.stack(
        [jnp.where(first_half, own_part, other_part), jnp.where(first_half, other_part, own_part)],
        axis=1,
    )
    own_mod = jnp.transpose(own_mod, (2, 0, 1, 3)).reshape((short_clips + 1) * 4, model_width)
    rows = exact_dot(jnp.concatenate([own_mod, norm_gains[:4]], axis=0), one_hot)
    gains = rows[-4:]
    own_mod = rows[:-4].reshape(short_clips + 1, 4, model_width)
    own_scales = 1.0 + own_mod[:, 0], 1.0 + own_mod[:, 2]
    own_tanhs = jnp.tanh(own_mod[:, 1]), jnp.tanh(own_mod[:, 3])
    selector = clip_local[:, None] == jnp.arange(short_clips + 1, dtype=jnp.int32)[None, :]

    def per_token(rows):
        chosen = rows[short_clips:]
        for clip in range(short_clips):
            chosen = jnp.where(selector[:, clip : clip + 1], rows[clip : clip + 1], chosen)
        return chosen

    normed_in = (hidden_hat * gains[0] * per_token(own_scales[0])).astype(bf16)
    query_gain, key_gain, text_gain = [
        lax.dynamic_slice(norm_gains, (row, head_start * HD), (1, own_width)) for row in (4, 5, 6)
    ]
    frequency = jnp.exp(
        jnp.arange(HD // 2, dtype=f32) * (-math.log(10000.0) / (HD // 2))
    )
    angles = jnp.tile(position.astype(f32)[:, None] * frequency, (1, 4))
    turns = jnp.cos(angles), jnp.sin(angles)
    text_turns = jnp.ones((text_rows, 2 * HD), f32), jnp.zeros((text_rows, 2 * HD), f32)
    normed_in, other_feats, tkey_near, out_near, tval_block, qkv_near_core, qkv_y = fence(
        normed_in, other_feats, tkey_near, out_near, tval_block, qkv_near_core, qkv_y
    )

    tkey_y = send_inner(grid, tkey_near)
    tkey_near_core = send_core(grid, [tkey_near])
    out_near_core = send_core(grid, [out_near])
    tval_near = gather_outer(grid, tval_block)
    qkv_core, normed_in = fence(send_core(grid, qkv_y), normed_in)
    qkv_own, qkv_other = stack([qkv_near] + qkv_y), stack(qkv_near_core + qkv_core)
    projected = dot(normed_in[:, :half_width], qkv_own) + dot(normed_in[:, half_width:], qkv_other)
    query_bf = head_call(norm_heads, "norm_queries", projected, 0, query_gain, turns)
    key_bf = head_call(norm_heads, "norm_keys", projected, 1, key_gain, turns)
    value_bf = projected[:, 2 * own_width :].astype(bf16)
    long_block = jnp.concatenate([key_bf[:LONG_DEV], value_bf[:LONG_DEV]], axis=1)
    (
        query_bf, key_bf, value_bf, long_block, tkey_y, tkey_near_core, out_near, out_near_core,
        tval_near, gate_weight,
    ) = fence(
        query_bf, key_bf, value_bf, long_block, tkey_y, tkey_near_core, out_near, out_near_core,
        tval_near, gate_weight,
    )

    tail = long_block.size // gate_weight.shape[1]
    gate_near = gather_outer(
        grid, jnp.concatenate([gate_weight, long_block.reshape(tail, -1)], axis=0)
    )
    tval_y = send_inner(grid, tval_near)
    tval_near_core = send_core(grid, [tval_near])
    short_query = query_bf[LONG_DEV:]
    short_key = key_bf[LONG_DEV:]
    short_value = value_bf[LONG_DEV:]
    short_clip = clip_column[LONG_DEV:]
    short_seen = clip_local[LONG_DEV:][None, :]
    short_out, short_lse = attend_call(
        "attend_short", short_clip, short_seen, short_query, short_key, short_value
    )
    out_y = send_inner(grid, out_near)
    tkey_core = send_core(grid, tkey_y)
    feats = jnp.concatenate(
        [
            jnp.where(first_half, own_feats, other_feats).reshape(-1, TXT_LEN // 2, text_width),
            jnp.where(first_half, other_feats, own_feats).reshape(-1, TXT_LEN // 2, text_width),
        ],
        axis=1,
    ).reshape(text_rows, text_width)
    tval_y, tval_near_core, gate_near, tkey_core, out_y, up_weight, feats, short_out = fence(
        tval_y, tval_near_core, gate_near, tkey_core, out_y, up_weight, feats, short_out
    )

    gate_near = gate_near.reshape(grid.outer_count, depth + tail, -1)
    long_near = gate_near[:, depth:].reshape(-1, 2 * own_width)
    gate_near = gate_near[:, :depth].reshape(grid.outer_count * depth, -1)
    long_y = send_inner(grid, long_near)
    long_near_core = send_core(grid, [long_near])
    gate_y = send_inner(grid, gate_near)
    gate_near_core = send_core(grid, [gate_near])
    up_near = gather_outer(grid, up_weight)
    tval_core = send_core(grid, tval_y)
    long_core = send_core(grid, long_y)
    out_core = send_core(grid, out_y)
    tkey_pieces = [tkey_near] + tkey_y + tkey_near_core + tkey_core
    text_raw = dot_pieces(feats, tkey_pieces)
    text_key_bf = head_call(norm_heads, "norm_text", text_raw, 0, text_gain, text_turns)
    tval_core, out_core, long_core, long_near_core, long_y, text_key_bf, query_bf = fence(
        tval_core, out_core, long_core, long_near_core, long_y, text_key_bf, query_bf
    )

    out_own, out_other = stack([out_near] + out_y), stack(out_near_core + out_core)
    long_pairs = stack([long_near] + long_y + long_near_core + long_core)
    long_count = long_pairs.shape[0]
    long_query = query_bf[:LONG_DEV]
    long_clip = clip_column[:LONG_DEV]
    long_seen = jnp.full((1, long_count), short_clips, jnp.int32)
    long_out, long_lse = attend_call(
        "attend_long", long_clip, long_seen, long_query, long_pairs, long_pairs, own_width
    )
    tval_pieces = [tval_near] + tval_y + tval_near_core + tval_core
    text_value_bf = dot_pieces(feats, tval_pieces).astype(bf16)
    key_clip = jnp.arange(text_rows, dtype=jnp.int32) // TXT_LEN
    key_place = jnp.arange(text_rows, dtype=jnp.int32) % TXT_LEN
    limits = jnp.concatenate(
        [
            lax.dynamic_slice_in_dim(text_lengths, seq_index * short_clips, short_clips, 0),
            text_lengths[clip_total - 1 :],
        ]
    )
    clip_match = key_clip[:, None] == jnp.arange(short_clips + 1, dtype=jnp.int32)[None, :]
    key_limit = jnp.sum(jnp.where(clip_match, limits[None, :], 0), axis=1)
    cross_seen = jnp.where(key_place < key_limit, key_clip, -1)[None, :]
    cross_out, cross_lse = attend_call(
        "attend_cross", clip_column, cross_seen, query_bf, text_key_bf, text_value_bf
    )
    attended = jnp.concatenate([long_out, short_out], axis=0)
    own_gates = lax.dynamic_slice_in_dim(head_gates, head_start, own_heads, 0)
    gate_tanh = jnp.repeat(jnp.tanh(own_gates), HD)[None, :]
    combined_bf = (attended + gate_tanh * cross_out).astype(bf16)
    attn_part = rounded(
        jnp.concatenate(
            [contract_cols(combined_bf, out_own), contract_cols(combined_bf, out_other)], axis=1
        )
    ).astype(bf16)
    attn_part, gate_y, gate_near_core, up_near, down_weight = fence(
        attn_part, gate_y, gate_near_core, up_near, down_weight
    )

    attn_moved = swap_txt(attn_part)
    up_y = send_inner(grid, up_near)
    up_near_core = send_core(grid, [up_near])
    down_near = gather_outer(grid, down_weight)
    gate_core = send_core(grid, gate_y)
    attn_moved, up_y, up_near_core, down_near, gate_core = fence(
        attn_moved, up_y, up_near_core, down_near, gate_core
    )

    down_y = send_inner(grid, down_near)
    down_near_core = send_core(grid, [down_near])
    up_core = send_core(grid, up_y)
    gate_own, gate_other = stack([gate_near] + gate_y), stack(gate_near_core + gate_core)
    residual, ffn_in_bf = row_call(
        enter_rows,
        "enter_rows",
        [clip_column, hidden, attn_part, attn_moved],
        [own_tanhs[0], own_scales[1], gains],
        [f32, bf16],
        0,
    )
    gate_value = dot(ffn_in_bf[:, :half_width], gate_own) + dot(
        ffn_in_bf[:, half_width:], gate_other
    )
    up_core, gate_value = fence(up_core, gate_value)
    up_own, up_other = stack([up_near] + up_y), stack(up_near_core + up_core)
    up_value = dot(ffn_in_bf[:, :half_width], up_own) + dot(ffn_in_bf[:, half_width:], up_other)
    sigmoid_gate = jax.nn.sigmoid(gate_value)
    silu_gate = gate_value * sigmoid_gate
    inner_bf = (silu_gate * up_value).astype(bf16)
    inner_bf, down_y, down_near_core = fence(inner_bf, down_y, down_near_core)

    down_core = send_core(grid, down_y)
    upstream = dot(cotangent, one_hot).astype(bf16)
    down_core, inner_bf, upstream = fence(down_core, inner_bf, upstream)
    down_own, down_other = stack([down_near] + down_y), stack(down_near_core + down_core)
    ffn_part = rounded(
        jnp.concatenate(
            [contract_cols(inner_bf, down_own), contract_cols(inner_bf, down_other)], axis=1
        )
    ).astype(bf16)
    (ffn_part,) = fence(ffn_part)

    ffn_moved = swap_txt(ffn_part)
    ffn_moved, ffn_part = fence(ffn_moved, ffn_part)

    block_out, grad_ffn_out, ffn_sums = row_call(
        leave_rows,
        "leave_rows",
        [clip_column, residual, ffn_part, ffn_moved, upstream],
        [own_tanhs[1], gains],
        [bf16, bf16],
        1,
    )
    down_kept = contract_rows(grad_ffn_out[:, :half_width], inner_bf).astype(bf16)
    down_away = contract_rows(grad_ffn_out[:, half_width:], inner_bf).astype(bf16)
    grad_ffn_out, down_away, down_kept = fence(grad_ffn_out, down_away, down_kept)

    down_core = grid.send(down_away, core=1)
    grad_inner = dot(grad_ffn_out[:, :half_width], down_own) + dot(
        grad_ffn_out[:, half_width:], down_other
    )
    silu_slope = sigmoid_gate * (1.0 + gate_value * (1.0 - sigmoid_gate))
    grad_gate_bf = (grad_inner * up_value * silu_slope).astype(bf16)
    grad_up_bf = (grad_inner * silu_gate).astype(bf16)
    ffn_in_part = rounded(
        jnp.concatenate(
            [
                contract_cols(grad_gate_bf, gate_own) + contract_cols(grad_up_bf, up_own),
                contract_cols(grad_gate_bf, gate_other) + contract_cols(grad_up_bf, up_other),
            ],
            axis=1,
        )
    ).astype(bf16)
    gate_kept = contract_rows(ffn_in_bf[:, :half_width], grad_gate_bf).astype(bf16)
    gate_away = contract_rows(ffn_in_bf[:, half_width:], grad_gate_bf).astype(bf16)
    down_away = core_away(grid, down_kept, down_core)
    down_core, down_away, ffn_in_part, gate_kept, gate_away, grad_up_bf = fence(
        down_core, down_away, ffn_in_part, gate_kept, gate_away, grad_up_bf
    )

    ffn_in_moved = swap_txt(ffn_in_part)
    down_moved = swap_inner(grid, down_away)
    gate_core = grid.send(gate_away, core=1)
    up_kept = contract_rows(ffn_in_bf[:, :half_width], grad_up_bf).astype(bf16)
    up_away = contract_rows(ffn_in_bf[:, half_width:], grad_up_bf).astype(bf16)
    block_out = contract_cols(block_out, one_hot).astype(bf16)
    gate_away = core_away(grid, gate_kept, gate_core)
    block_out, ffn_in_moved, down_moved, up_kept = fence(
        block_out, ffn_in_moved, down_moved, up_kept
    )

    down_total = inner_total(grid, down_kept, down_core, down_moved)
    gate_moved = swap_inner(grid, gate_away)
    up_core = grid.send(up_away, core=1)
    ffn_in_moved, down_total = fence(ffn_in_moved, down_total)
    down_sum = sum_outer(grid, down_total)
    grad_residual, grad_attn_bf, res_sums, attn_sums = row_call(
        middle_rows,
        "middle_rows",
        [clip_column, residual, ffn_in_part, ffn_in_moved, upstream, attn_part, attn_moved],
        [own_tanhs[0], own_scales[1], gains],
        [f32, bf16],
        2,
    )
    grad_combined = dot(grad_attn_bf[:, :half_width], out_own) + dot(
        grad_attn_bf[:, half_width:], out_other
    )
    grad_attended_bf = grad_combined.astype(bf16)
    grad_long_bf = grad_attended_bf[:LONG_DEV]
    grad_long_q, *long_parts = attend_call(
        "attend_long_back", long_clip, long_seen, long_query, long_pairs, long_pairs, own_width,
        (grad_long_bf, long_out, long_lse), bf16,
    )
    long_terms = jnp.concatenate(long_parts, axis=1)
    long_kept, long_away = long_terms[: long_count // 2], long_terms[long_count // 2 :]
    out_kept = contract_rows(grad_attn_bf[:, :half_width], combined_bf).astype(bf16)
    out_away = contract_rows(grad_attn_bf[:, half_width:], combined_bf).astype(bf16)
    up_away = core_away(grid, up_kept, up_core)
    (
        grad_combined, grad_attended_bf, gate_moved, up_core, up_away, long_kept, long_away, out_kept,
        out_away, grad_long_q,
    ) = fence(
        grad_combined, grad_attended_bf, gate_moved, up_core, up_away, long_kept, long_away, out_kept,
        out_away, grad_long_q,
    )

    up_moved = swap_inner(grid, up_away)
    long_core = grid.send(long_away, core=1)
    out_core = grid.send(out_away, core=1)
    gate_total = inner_total(grid, gate_kept, gate_core, gate_moved)
    grad_combined, gate_total = fence(grad_combined, gate_total)
    gate_sum = sum_outer(grid, gate_total)
    grad_cross_bf = (gate_tanh * grad_combined).astype(bf16)
    own_gate_grad = jnp.sum(
        jnp.sum(grad_combined * cross_out, axis=0).reshape(own_heads, HD), axis=1
    ) * (1.0 - jnp.tanh(own_gates) ** 2)
    grad_query, grad_text_key, grad_text_value = attend_call(
        "attend_cross_back", clip_column, cross_seen, query_bf, text_key_bf, text_value_bf, 0,
        (grad_cross_bf, cross_out, cross_lse),
    )
    grad_tkey, text_gain_grad = head_call(
        norm_heads_back, "norm_text_back", text_raw, 0, text_gain, text_turns, (grad_text_key,)
    )
    grad_tval = grad_text_value.astype(bf16)
    tkey_kept = contract_rows(feats[:, :half_text], grad_tkey).astype(bf16)
    tkey_away = contract_rows(feats[:, half_text:], grad_tkey).astype(bf16)
    long_away = core_away(grid, long_kept, long_core)
    out_away = core_away(grid, out_kept, out_core)
    (
        gate_sum, down_sum, up_moved, long_core, long_away, out_core, out_away, grad_query, grad_tkey,
        grad_tval, tkey_kept, tkey_away, grad_attended_bf,
    ) = fence(
        gate_sum, down_sum, up_moved, long_core, long_away, out_core, out_away, grad_query, grad_tkey,
        grad_tval, tkey_kept, tkey_away, grad_attended_bf,
    )

    long_moved = swap_inner(grid, long_away)
    out_moved = swap_inner(grid, out_away)
    tkey_core = grid.send(tkey_away, core=1)
    down_grad = down_sum.astype(f32)
    gate_grad = gate_sum.astype(f32)
    up_total = inner_total(grid, up_kept, up_core, up_moved)
    grad_attended_bf, up_total = fence(grad_attended_bf, up_total)
    up_sum = sum_outer(grid, up_total)
    grad_short_bf = grad_attended_bf[LONG_DEV:]
    grad_short_q, grad_short_k, grad_short_v = attend_call(
        "attend_short_back", short_clip, short_seen, short_query, short_key, short_value, 0,
        (grad_short_bf, short_out, short_lse),
    )
    tval_kept = contract_rows(feats[:, :half_text], grad_tval).astype(bf16)
    tval_away = contract_rows(feats[:, half_text:], grad_tval).astype(bf16)
    null_flags = jnp.concatenate([own_null, null_mask[clip_total - 1 :] == 1]).astype(f32)
    row_ids = jnp.arange(text_rows, dtype=jnp.int32)
    null_chosen = jnp.where(
        row_ids[None, :] % TXT_LEN == jnp.arange(TXT_LEN, dtype=jnp.int32)[:, None],
        jnp.repeat(null_flags, TXT_LEN)[None, :],
        0.0,
    ).astype(bf16)
    null_rows = jnp.concatenate(
        [dot(null_chosen, grad_tkey), dot(null_chosen, grad_tval)], axis=1
    ).astype(bf16)
    tkey_away = core_away(grid, tkey_kept, tkey_core)
    (
        up_sum, long_moved, out_moved, tkey_core, tkey_away, tval_kept, tval_away, grad_short_q,
        grad_short_k, grad_short_v, null_rows,
    ) = fence(
        up_sum, long_moved, out_moved, tkey_core, tkey_away, tval_kept, tval_away, grad_short_q,
        grad_short_k, grad_short_v, null_rows,
    )

    tkey_moved = swap_inner(grid, tkey_away)
    tval_core = grid.send(tval_away, core=1)
    null_moved = pair_sum(grid, null_rows, 1)
    up_grad = up_sum.astype(f32)
    long_total = inner_total(grid, long_kept, long_core, long_moved)
    out_total = inner_total(grid, out_kept, out_core, out_moved)
    long_rows = LONG_DEV * 2
    both_total = jnp.concatenate(
        [
            long_total.reshape(grid.outer_count, long_rows, own_width),
            out_total.reshape(grid.outer_count, depth, own_width),
        ],
        axis=1,
    ).reshape(-1, own_width)
    both_sum = sum_outer(grid, both_total)
    grad_query_raw, query_gain_grad = head_call(
        norm_heads_back, "norm_queries_back", projected, 0, query_gain, turns,
        (grad_query, jnp.concatenate([grad_long_q, grad_short_q], axis=0)),
    )
    tval_away = core_away(grid, tval_kept, tval_core)
    (
        both_sum, tkey_moved, tval_core, tval_away, null_moved, grad_query_raw, grad_short_k,
        grad_short_v, query_gain_grad,
    ) = fence(
        both_sum, tkey_moved, tval_core, tval_away, null_moved, grad_query_raw, grad_short_k,
        grad_short_v, query_gain_grad,
    )

    tval_moved = swap_inner(grid, tval_away)
    null_rows = null_rows + null_moved
    null_moved = pair_sum(grid, null_rows, 2)
    out_grad = both_sum[long_rows:].astype(f32)
    tkey_total = inner_total(grid, tkey_kept, tkey_core, tkey_moved)
    both_sum, tkey_total = fence(both_sum, tkey_total)
    tkey_sum = sum_outer(grid, tkey_total)
    own_terms = both_sum[:long_rows].reshape(LONG_DEV, 2 * own_width).astype(f32)
    grad_key = jnp.concatenate([own_terms[:, :own_width], grad_short_k], axis=0)
    grad_value = jnp.concatenate([own_terms[:, own_width:], grad_short_v], axis=0)
    grad_key_raw, key_gain_grad = head_call(
        norm_heads_back, "norm_keys_back", projected, 1, key_gain, turns, (grad_key,)
    )
    grad_proj_bf = jnp.concatenate(
        [grad_query_raw, grad_key_raw, grad_value.astype(bf16)], axis=1
    )
    normed_part = rounded(
        jnp.concatenate(
            [contract_cols(grad_proj_bf, qkv_own), contract_cols(grad_proj_bf, qkv_other)], axis=1
        )
    ).astype(bf16)
    qkv_kept = contract_rows(normed_in[:, :half_width], grad_proj_bf).astype(bf16)
    qkv_away = contract_rows(normed_in[:, half_width:], grad_proj_bf).astype(bf16)
    first_rows = token_count // 2
    moved_first = swap_txt(normed_part[:first_rows])
    moved_last = swap_txt(normed_part[first_rows:])
    qkv_core = grid.send(qkv_away, core=1)
    qkv_away = core_away(grid, qkv_kept, qkv_core)
    (
        tkey_sum, tval_moved, null_moved, moved_first, qkv_kept, qkv_core, qkv_away, grad_residual,
    ) = fence(
        tkey_sum, tval_moved, null_moved, moved_first, qkv_kept, qkv_core, qkv_away, grad_residual,
    )

    qkv_moved = swap_inner(grid, qkv_away)
    null_rows = null_rows + null_moved
    tval_total = inner_total(grid, tval_kept, tval_core, tval_moved)
    tval_total, null_rows, moved_first, grad_residual = fence(
        tval_total, null_rows, moved_first, grad_residual
    )
    tval_sum = sum_outer(grid, tval_total)
    null_rows = null_rows + pair_sum(grid, null_rows, 4)
    null_moved = pair_sum(grid, null_rows, 8)
    normed_moved = jnp.concatenate([moved_first, moved_last], axis=0)
    video_high, video_low, hidden_sums = row_call(
        last_rows,
        "last_rows",
        [clip_column, hidden, normed_part, normed_moved, grad_residual],
        [own_scales[0], gains],
        [bf16, bf16],
        1,
    )
    hidden_sums, tval_sum, qkv_moved, null_rows, null_moved = fence(
        hidden_sums, tval_sum, qkv_moved, null_rows, null_moved
    )

    text_grad = jnp.stack([tkey_sum.astype(f32), tval_sum.astype(f32)], axis=1)
    qkv_total = inner_total(grid, qkv_kept, qkv_core, qkv_moved)
    hidden_sums, qkv_total = fence(hidden_sums, qkv_total)
    qkv_sum = sum_outer(grid, qkv_total)

    grad_mod = jnp.stack(
        [
            hidden_sums * gains[0],
            attn_sums * gains[1] * (1.0 - own_tanhs[0] * own_tanhs[0]),
            res_sums * gains[2],
            ffn_sums * gains[3] * (1.0 - own_tanhs[1] * own_tanhs[1]),
        ],
        axis=1,
    ).reshape(-1, model_width)
    gain_rows = jnp.stack(
        [
            jnp.sum(hidden_sums * own_scales[0], axis=0),
            jnp.sum(attn_sums * own_tanhs[0], axis=0),
            jnp.sum(res_sums * own_scales[1], axis=0),
            jnp.sum(ffn_sums * own_tanhs[1], axis=0),
        ],
        axis=0,
    )
    rows = contract_cols(
        jnp.concatenate(split_three(jnp.concatenate([grad_mod, gain_rows], axis=0)), axis=0),
        one_hot,
    )
    row_count = rows.shape[0] // 3
    rows = rows[:row_count] + rows[row_count : 2 * row_count] + rows[2 * row_count :]
    gain_rows = rows[-4:]
    own_grad_mod = rows[:-4].reshape(short_clips + 1, 4 * model_width)
    column_count = mod_part.shape[1]
    mod_blocks = lax.dynamic_index_in_dim(
        own_grad_mod.reshape(short_clips + 1, seq_count, 2, column_count),
        txt_index,
        2,
        keepdims=False,
    )
    mod_blocks = turn_seq(grid, jnp.transpose(mod_blocks, (1, 0, 2)))
    null_rows = sum_seq(grid, null_rows + null_moved, 16)
    null_part = jnp.concatenate(
        [
            contract_cols(null_rows[:, :own_width], key_piece)
            + contract_cols(null_rows[:, own_width:], value_piece)
            for key_piece, value_piece in zip(tkey_pieces, tval_pieces)
        ],
        axis=1,
    )
    null_part = rounded(null_part).astype(bf16)
    null_moved = swap_txt(null_part)
    video_grad = contract_cols(video_high, one_hot) + contract_cols(video_low, one_hot)
    slice_grad_mod = jnp.concatenate(
        [
            mod_blocks[:, :short_clips].reshape(clip_total - 1, column_count),
            jnp.sum(mod_blocks[:, short_clips], axis=0, keepdims=True),
        ],
        axis=0,
    )
    ada_weight_grad = lax.dot_general(
        shifted.astype(f32), slice_grad_mod, (((0,), (0,)), ((), ())), precision=highest
    )
    ada_bias_grad = jnp.sum(slice_grad_mod, axis=0)
    grad_shifted = lax.dot_general(
        slice_grad_mod, ada_weight.astype(f32), (((1,), (1,)), ((), ())), precision=highest
    )
    cond_value = condition.astype(f32)
    cond_sigmoid = jax.nn.sigmoid(cond_value)
    cond_part = grad_shifted * cond_sigmoid * (1.0 + cond_value * (1.0 - cond_sigmoid))

    head_rows = [
        lax.dynamic_update_slice(jnp.zeros((1, model_width), f32), rows, (0, head_start * HD))
        for rows in (query_gain_grad, key_gain_grad, text_gain_grad)
    ]
    gains_term = jnp.concatenate([jnp.where(first_half, gain_rows, 0.0)] + head_rows, axis=0)
    gates_term = lax.dynamic_update_slice_in_dim(jnp.zeros((H,), f32), own_gate_grad, head_start, 0)
    cond_count, gains_count = cond_part.size, gains_term.size
    packed = jnp.concatenate([cond_part.reshape(-1), gains_term.reshape(-1), gates_term])
    packed = jnp.pad(packed, (0, -packed.shape[0] % 1024)).reshape(-1, 1024)
    packed = packed + pair_sum(grid, packed, 1)
    packed = packed + pair_sum(grid, packed, 2)
    packed, qkv_sum = fence(packed, qkv_sum)
    packed = packed + pair_sum(grid, packed, 4)
    packed, null_moved = fence(packed, null_moved)
    null_grad = reorder_columns(
        null_part.astype(f32) + null_moved.astype(f32), owners, False
    )
    qkv_grad = qkv_sum.astype(f32).reshape(depth, 3, own_width)
    packed = sum_seq(grid, packed, 8)
    packed = (packed + swap_txt(packed)).reshape(-1)
    condition_grad = packed[:cond_count].reshape(cond_part.shape)
    norm_gains_grad = packed[cond_count : cond_count + gains_count].reshape(gains_term.shape)
    head_gates_grad = packed[cond_count + gains_count : cond_count + gains_count + H]
    return (
        block_out,
        video_grad,
        condition_grad,
        qkv_grad,
        out_grad,
        gate_grad,
        up_grad,
        down_grad,
        text_grad,
        ada_weight_grad,
        ada_bias_grad,
        null_grad,
        norm_gains_grad,
        head_gates_grad,
    )


def solution(mesh):
    placed = (
        P("seq", None),
        P("seq", None),
        P(),
        P("seq", "txt", None),
        P("txt", None),
        P("txt", None),
        P("seq", None, "txt"),
        P("seq", "txt"),
        P("seq", "txt"),
        P("seq", "txt"),
        P("seq", "txt"),
        P("seq", None, "txt"),
        P(None, ("seq", "txt")),
        P(("seq", "txt")),
        P(),
        P(),
        P("seq", None),
        P(),
        P(),
    )
    return jax.shard_map(
        local,
        mesh=mesh,
        in_specs=placed,
        out_specs=(
            P("seq", None),
            P("seq", None),
            P(),
            P("seq", None, "txt"),
            P("seq", "txt"),
            P("seq", "txt"),
            P("seq", "txt"),
            P("seq", "txt"),
            P("seq", None, "txt"),
            P(None, ("seq", "txt")),
            P(("seq", "txt")),
            P(),
            P(),
            P(),
        ),
        check_vma=False,
    )
```

time: 2180 us -> 876 us (0.40)
  waiting for transfers between devices: 1640 us -> 286 us
  Pallas kernels: 0 us -> 171 us
  matrix products: 209 us -> 144 us
  starting transfers between devices: 1.9 us -> 51.2 us
  other arithmetic: 84.5 us -> 44.3 us
  local copies, waits for them, and re-layouts: 162 us -> 126 us
  blocking collectives: 54.5 us -> 23.9 us
    reduce_scatter x6 -> x7, waiting for transfers between devices: 772 us -> 8.51 us  [sum_outer(): lax.psum_scatter(total, 'seq', scatter_dimension=0, tiled=True, axis_inde...]
    all_gather x10 -> x6, waiting for transfers between devices: 445 us -> 20.2 us  [gather_outer(): lax.all_gather(block, 'seq', axis=0, tiled=True, axis_index_groups=grid.l...]
    psum x5 -> x0, waiting for transfers between devices: 326 us -> none  [the longest x4 189 us: head_sum(): return lax.psum(values.astype(jnp.bfloat16), 'txt').astype(jnp.float32)]
    ppermute x0 -> x67, waiting for transfers between devices: none -> 257 us  [the longest x50 139 us: send(): return lax.ppermute(values, 'seq', pairs)]
    pallas_call x0 -> x34, Pallas kernels: none -> 171 us  [the longest x6 67.9 us: attend_call(): pl.pallas_call(attend_heads_back if back else attend_heads, grid=(width /...]
    unnamed x25 -> x13, waiting for transfers between devices: 95.6 us -> 0.23 us
    dot_general x30 -> x26, matrix products: 119 us -> 59.4 us  [the longest x24 56.7 us: dot(): return jnp.dot(left_side, right_side, preferred_element_type=f32)]
    ppermute x0 -> x67, starting transfers between devices: none -> 49.9 us  [the longest x50 32.2 us: send(): return lax.ppermute(values, 'seq', pairs)]
  transfers between devices with their start and end apart: 23 -> 80, of which waited for: 22 -> 29; matrix products, arithmetic and copies ran while one was open for 14% -> 26% of each run, Pallas kernels for 0% -> 17%
where the time goes in v1:
time: 876 us; the launch traced here: 865 us
  waiting for transfers between devices  286 us (33%)
  Pallas kernels  171 us (20%)
  matrix products  144 us (16%)
  local copies, waits for them, and re-layouts  126 us (14%)
  starting transfers between devices  51.2 us (6%)
  other arithmetic  44.3 us (5%)
  blocking collectives  23.9 us (3%)
  between operations  18.7 us (2%)
    ppermute x50, waiting for transfers between devices, send(): return lax.ppermute(values, 'seq', pairs)  139 us
    unnamed x500, local copies, waits for them, and re-layouts  80.5 us
    ppermute x9, waiting for transfers between devices, swap_txt(): return lax.ppermute(values, 'txt', [(0, 1), (1, 0)])  74 us
    pallas_call x6, Pallas kernels, attend_call(): pl.pallas_call(attend_heads_back if back else attend_heads, grid=(width /...  67.9 us
    dot_general x24, matrix products, dot(): return jnp.dot(left_side, right_side, preferred_element_type=f32)  56.7 us
    dot_general x22, matrix products, contract_cols(): lax.dot_general(left_side, right_side, (((1,), (1,)), ((), ())), preferre...  48.4 us
    ppermute x8, waiting for transfers between devices, pair_sum(): return lax.ppermute(values, 'seq', pairs)  44 us
    pallas_call x16, Pallas kernels, add_rows(): pl.pallas_call(add_blocks, grid=(rows // block,), in_specs=[from_row(star...  43 us
  transfers between devices with their start and end apart: 80, of which 29 were waited for; matrix products, arithmetic and copies ran while one was open for 26% of the time, Pallas kernels for 17%

profile of v1, /device:TPU:0, one launch (start us, length us, event | category | flops | bytes accessed | tf_op | source)
XLA Modules:
  0.0 864.7 jit_solution(1882715388456511853)
XLA Ops:
  40.1 13.2 %all-gather.7.cloned.1.call-done = bf16[384,2304]{1,0:T(8,128)(2,1)} async-done(((bf16[96,2304]{1,0:T(8,128)(2,1)}), bf16[384,2304]{1,0:T(8,128)(2,1)}) %all-gather.7.cloned.1.call-update) | async-done | bytes 1769488 | tf_op jit(solution)/shard_map/all_gather | solution.py:116
  60.8 23.9 %all_gather.23 = bf16[384,768]{1,0:T(8,128)(2,1)} all-gather(bf16[96,768]{1,0:T(8,128)(2,1)} %param.32), channel_id=1, replica_groups={{0,8,16,24},{2,10,18,26},{4,12,20,28},{6,14,22,30},{1,9,17,25},{3,11,19..., dimensions={0}, use_global_device_ids=true | all-gather | bytes 737280 | tf_op jit(solution)/shard_map/all_gather | solution.py:116
  93.9 7.0 all-gather.9.cloned.1.call-done
  128.1 13.7 %collective-permute-done.10 = bf16[1024,768]{1,0:T(8,128)(2,1)} collective-permute-done((bf16[1024,768]{1,0:T(8,128)(2,1)}, bf16[1024,768]{1,0:T(8,128)(2,1)}, u32[]{:S(2)}, u32[]{:S(2)}) %collective-permute-start.10) | collective-permute-done | bytes 1572896 | tf_op jit(solution)/shard_map/ppermute | solution.py:101
  152.1 11.6 %attend_short.1 = (f32[448,768]{1,0:T(8,128)S(1)}, f32[448,768]{1,0:T(8,128)S(1)}) custom-call(s32[448,1]{1,0:T(8,128)S(1)} %copy.183.clip_ref, s32[1,448]{1,0:T(1,128)S(1)} %bitcast.186, bf16[448,768]{1,0:T(8,128)(2,1)S(1)} %slice.300.query_ref, bf16[448,768]{1,0:T(8,128)(2,1)S(1)} %slice.301.key_ref, bf16[448,768]{1,0:T(8,128)(2,1)S(1)} %slice.302.value_ref), custom_call_target="tpu_custom_call" | custom-call | flops 1 | bytes 1 | tf_op jit(solution)/shard_map/attend_short/pallas_call | solution.py:472
  168.0 28.3 %collective-permute-done.16 = bf16[384,768]{1,0:T(8,128)(2,1)S(1)} collective-permute-done((bf16[384,768]{1,0:T(8,128)(2,1)}, bf16[384,768]{1,0:T(8,128)(2,1)S(1)}, u32[]{:S(2)}, u32[]{:S(2)}) %collective-permute-start.16) | collective-permute-done | bytes 589856 | tf_op jit(solution)/shard_map/ppermute | solution.py:101
  231.5 7.2 attend_long.1
  241.6 12.0 %attend_cross.1 = (f32[512,768]{1,0:T(8,128)S(1)}, f32[512,768]{1,0:T(8,128)S(1)}) custom-call(s32[512,1]{1,0:T(8,128)S(1)} %copy.190.clip_ref, s32[1,256]{1,0:T(1,128)S(1)} %compare_select_fusion.key_clip_ref, bf16[512,768]{1,0:T(8,128)(2,1)S(1)} %copy-done.18, bf16[256,768]{1,0:T(8,128)(2,1)S(1)} %norm_text.1.key_ref, bf16[256,768]{1,0:T(8,128)(2,1)S(1)} %fusion.37.value_ref), custom_call_target="tpu_custom_call" | custom-call | flops 1 | bytes 1 | tf_op jit(solution)/shard_map/attend_cross/pallas_call | solution.py:472
  276.6 24.0 %collective-permute-done.24.moved_ref = bf16[512,1536]{1,0:T(8,128)(2,1)S(1)} collective-permute-done((bf16[512,1536]{1,0:T(8,128)(2,1)S(1)}, bf16[512,1536]{1,0:T(8,128)(2,1)S(1)}, u32[]{:S(2)}, u32[]{:S(2)}) %collective-permute-start.24) | collective-permute-done | bytes 1572896 | tf_op jit(solution)/shard_map/ppermute | solution.py:73
  353.4 35.9 %collective-permute-done.32.moved_ref = bf16[512,1536]{1,0:T(8,128)(2,1)S(1)} collective-permute-done((bf16[512,1536]{1,0:T(8,128)(2,1)S(1)}, bf16[512,1536]{1,0:T(8,128)(2,1)S(1)}, u32[]{:S(2)}, u32[]{:S(2)}) %collective-permute-start.32) | collective-permute-done | bytes 1572896 | tf_op jit(solution)/shard_map/ppermute | solution.py:73
  406.9 7.0 multiply_convert_fusion.1
  447.3 23.1 %collective-permute-done.35.refs_2_ = bf16[384,2048]{1,0:T(8,128)(2,1)S(1)} collective-permute-done((bf16[384,2048]{1,0:T(8,128)(2,1)S(1)}, bf16[384,2048]{1,0:T(8,128)(2,1)S(1)}, u32[]{:S(2)}, u32[]{:S(2)}) %collective-permute-start.35) | collective-permute-done | bytes 1572896 | tf_op jit(solution)/shard_map/ppermute | solution.py:101
  481.3 11.6 %middle_rows.1 = (f32[512,1536]{1,0:T(8,128)}, bf16[512,1536]{1,0:T(8,128)(2,1)S(1)}, f32[4,1536]{1,0:T(4,128)S(1)}, f32[4,1536]{1,0:T(4,128)S(1)}) custom-call(s32[512,1]{1,0:T(8,128)S(1)} %copy.190.clip_ref, f32[512,1536]{1,0:T(8,128)} %get-tuple-element.251.res_ref, bf16[512,1536]{1,0:T(8,128)(2,1)S(1)} %copy-done.33, bf16[512,1536]{1,0:T(8,128)(2,1)S(1)} %copy-done.63, ...), custom_call_target="tpu_custom_call" | custom-call | flops 1 | bytes 1 | tf_op jit(solution)/shard_map/middle_rows/pallas_call | solution.py:343
  500.3 9.7 %attend_long_back.1 = (f32[64,768]{1,0:T(8,128)S(1)}, bf16[1024,768]{1,0:T(8,128)(2,1)S(1)}, bf16[1024,768]{1,0:T(8,128)(2,1)S(1)}) custom-call(s32[64,1]{1,0:T(8,128)S(1)} %copy-done.87, s32[1,1024]{1,0:T(1,128)S(1)} %broadcast_in_dim.215.key_clip_ref, bf16[64,768]{1,0:T(8,128)(2,1)S(1)} %copy-done.76, bf16[1024,1536]{1,0:T(8,128)(2,1)} %copy-done.3, ...), custom_call_target="tpu_custom_call" | custom-call | flops 1 | bytes 1 | tf_op jit(solution)/shard_map/attend_long_back/pallas_call | solution.py:472
  521.2 10.6 %collective-permute-done.37.refs_2_ = bf16[384,2048]{1,0:T(8,128)(2,1)S(1)} collective-permute-done((bf16[384,2048]{1,0:T(8,128)(2,1)S(1)}, bf16[384,2048]{1,0:T(8,128)(2,1)S(1)}, u32[]{:S(2)}, u32[]{:S(2)}) %collective-permute-start.37) | collective-permute-done | bytes 1572896 | tf_op jit(solution)/shard_map/ppermute | solution.py:101
  539.6 10.8 %attend_cross_back.1 = (f32[512,768]{1,0:T(8,128)S(1)}, f32[256,768]{1,0:T(8,128)S(1)}, f32[256,768]{1,0:T(8,128)S(1)}) custom-call(s32[512,1]{1,0:T(8,128)S(1)} %copy.190.clip_ref, s32[1,256]{1,0:T(1,128)S(1)} %compare_select_fusion.key_clip_ref, bf16[512,768]{1,0:T(8,128)(2,1)S(1)} %copy-done.19, bf16[256,768]{1,0:T(8,128)(2,1)S(1)} %copy-done.51, ...), custom_call_target="tpu_custom_call" | custom-call | flops 1 | bytes 1 | tf_op jit(solution)/shard_map/attend_cross_back/pallas_call | solution.py:472
  562.9 10.2 %collective-permute-done.39.refs_2_ = bf16[384,2048]{1,0:T(8,128)(2,1)} collective-permute-done((bf16[384,2048]{1,0:T(8,128)(2,1)}, bf16[384,2048]{1,0:T(8,128)(2,1)}, u32[]{:S(2)}, u32[]{:S(2)}) %collective-permute-start.39) | collective-permute-done | bytes 1572896 | tf_op jit(solution)/shard_map/ppermute | solution.py:101
  584.2 16.7 %attend_short_back.1 = (f32[448,768]{1,0:T(8,128)S(1)}, f32[448,768]{1,0:T(8,128)S(1)}, f32[448,768]{1,0:T(8,128)}) custom-call(s32[448,1]{1,0:T(8,128)S(1)} %copy-done.55, s32[1,448]{1,0:T(1,128)S(1)} %bitcast.187, bf16[448,768]{1,0:T(8,128)(2,1)S(1)} %copy-done.41, bf16[448,768]{1,0:T(8,128)(2,1)S(1)} %copy-done.37, bf16[448,768]{1,0:T(8,128)(2,1)S(1)} %copy-done.39, ...), custom_call_target="tpu_custom_call" | custom-call | flops 1 | bytes 1 | tf_op jit(solution)/shard_map/attend_short_back/pallas_call | solution.py:472
  636.7 23.7 %collective-permute-done.45.refs_2_ = bf16[1024,768]{1,0:T(8,128)(2,1)S(1)} collective-permute-done((bf16[1024,768]{1,0:T(8,128)(2,1)}, bf16[1024,768]{1,0:T(8,128)(2,1)S(1)}, u32[]{:S(2)}, u32[]{:S(2)}) %collective-permute-start.45) | collective-permute-done | bytes 1572896 | tf_op jit(solution)/shard_map/ppermute | solution.py:101
  696.1 23.2 %collective-permute-done.49 = bf16[64,1536]{1,0:T(8,128)(2,1)S(1)} collective-permute-done((bf16[64,1536]{1,0:T(8,128)(2,1)S(1)}, bf16[64,1536]{1,0:T(8,128)(2,1)S(1)}, u32[]{:S(2)}, u32[]{:S(2)}) %collective-permute-start.49) | collective-permute-done | bytes 196640 | tf_op jit(solution)/shard_map/ppermute | solution.py:182
  744.4 11.2 %collective-permute-done.52 = bf16[256,1536]{1,0:T(8,128)(2,1)S(1)} collective-permute-done((bf16[256,1536]{1,0:T(8,128)(2,1)}, bf16[256,1536]{1,0:T(8,128)(2,1)S(1)}, u32[]{:S(2)}, u32[]{:S(2)}) %collective-permute-start.52) | collective-permute-done | bytes 786464 | tf_op jit(solution)/shard_map/ppermute | solution.py:73
  758.1 6.8 last_rows.1
  815.7 8.5 reduce-scatter.20.cloned.1.call-done
  837.7 10.5 %collective-permute-done.65 = f32[60,1024]{1,0:T(8,128)S(1)} collective-permute-done((f32[60,1024]{1,0:T(8,128)S(1)}, f32[60,1024]{1,0:T(8,128)S(1)}, u32[]{:S(2)}, u32[]{:S(2)}) %collective-permute-start.65) | collective-permute-done | bytes 245792 | tf_op jit(solution)/shard_map/ppermute | solution.py:182
  (961 shorter events, 485.8 us)
Async XLA Ops:
  7.2 46.0 %all-gather.7.cloned.1.call-start = ((), (), s32[]{:S(2)}) async-start(), calls=%async_computation.7 | async-start | bytes 2211840 | tf_op jit(solution)/shard_map/all_gather | solution.py:116
  9.3 91.7 %all-gather.9.cloned.1.call-start = ((), (), s32[]{:S(2)}) async-start(), calls=%async_computation.8 | async-start | bytes 1966080 | tf_op jit(solution)/shard_map/all_gather | solution.py:116
  53.3 40.7 %collective-permute-start.8 = (bf16[384,2304]{1,0:T(8,128)(2,1)}, bf16[384,2304]{1,0:T(8,128)(2,1)}, u32[]{:S(2)}, u32[]{:S(2)}) collective-permute-start(bf16[384,2304]{1,0:T(8,128)(2,1)} %all-gather.7.cloned.1.call-done), channel_id=1, source_target_pairs={{0,4},{2,6},{4,0},{6,2},{8,12},{10,14},{12,8},{14,10},{16,20},{18,... | collective-permute-start | bytes 5308424 | tf_op jit(solution)/shard_map/ppermute | solution.py:101
  54.7 39.2 %collective-permute-start.7 = (bf16[384,2304]{1,0:T(8,128)(2,1)}, bf16[384,2304]{1,0:T(8,128)(2,1)}, u32[]{:S(2)}, u32[]{:S(2)}) collective-permute-start(bf16[384,2304]{1,0:T(8,128)(2,1)} %all-gather.7.cloned.1.call-done), channel_id=1, source_target_pairs={{0,2},{2,0},{4,6},{6,4},{8,10},{10,8},{12,14},{14,12},{16,18},{18,... | collective-permute-start | bytes 5308424 | tf_op jit(solution)/shard_map/ppermute | solution.py:101
  55.1 86.7 %all-gather.11.cloned.1.call-start = ((), (), s32[]{:S(2)}) async-start(), calls=%async_computation.9 | async-start | bytes 1966080 | tf_op jit(solution)/shard_map/all_gather | solution.py:116
  105.8 91.9 %all-gather.13.cloned.1.call-start = ((), (), s32[]{:S(2)}) async-start(), calls=%async_computation.10 | async-start | bytes 2949120 | tf_op jit(solution)/shard_map/all_gather | solution.py:116
  143.9 120.1 %all-gather.15.cloned.1.call-start = ((), (), s32[]{:S(2)}) async-start(), calls=%async_computation.11 | async-start | bytes 1966080 | tf_op jit(solution)/shard_map/all_gather | solution.py:116
  146.6 51.1 %collective-permute-start.14 = (bf16[1024,768]{1,0:T(8,128)(2,1)}, bf16[1024,768]{1,0:T(8,128)(2,1)}, u32[]{:S(2)}, u32[]{:S(2)}) collective-permute-start(bf16[1024,768]{1,0:T(8,128)(2,1)} %all-gather.11.cloned.1.call-done), channel_id=1, source_target_pairs={{0,2},{2,0},{4,6},{6,4},{8,10},{10,8},{12,14},{14,12},{16,18},{18,... | collective-permute-start | bytes 4718600 | tf_op jit(solution)/shard_map/ppermute | solution.py:101
  146.7 51.0 %collective-permute-start.13 = (bf16[1024,768]{1,0:T(8,128)(2,1)}, bf16[1024,768]{1,0:T(8,128)(2,1)}, u32[]{:S(2)}, u32[]{:S(2)}) collective-permute-start(bf16[1024,768]{1,0:T(8,128)(2,1)} %all-gather.11.cloned.1.call-done), channel_id=1, source_target_pairs={{0,4},{2,6},{4,0},{6,2},{8,12},{10,14},{12,8},{14,10},{16,20},{18,... | collective-permute-start | bytes 4718600 | tf_op jit(solution)/shard_map/ppermute | solution.py:101
  147.4 48.9 %collective-permute-start.15 = (bf16[1024,768]{1,0:T(8,128)(2,1)}, bf16[1024,768]{1,0:T(8,128)(2,1)S(1)}, u32[]{:S(2)}, u32[]{:S(2)}) collective-permute-start(bf16[1024,768]{1,0:T(8,128)(2,1)} %collective-permute-done.10), channel_id=1, source_target_pairs={{0,2},{2,0},{4,6},{6,4},{8,10},{10,8},{12,14},{14,12},{16,18},{18,... | collective-permute-start | bytes 4718600 | tf_op jit(solution)/shard_map/ppermute | solution.py:101
  149.0 47.3 %collective-permute-start.16 = (bf16[384,768]{1,0:T(8,128)(2,1)}, bf16[384,768]{1,0:T(8,128)(2,1)S(1)}, u32[]{:S(2)}, u32[]{:S(2)}) collective-permute-start(bf16[384,768]{1,0:T(8,128)(2,1)} %all_gather.23), channel_id=1, source_target_pairs={{0,4},{2,6},{4,0},{6,2},{8,12},{10,14},{12,8},{14,10},{16,20},{18,... | collective-permute-start | bytes 1769480 | tf_op jit(solution)/shard_map/ppermute | solution.py:101
  206.7 96.2 %all-gather.17.cloned.1.call-start = ((), (), s32[]{:S(2)}) async-start(), calls=%async_computation.12 | async-start | bytes 1966080 | tf_op jit(solution)/shard_map/all_gather | solution.py:116
  211.6 46.2 %collective-permute-start.23 = (bf16[384,2048]{1,0:T(8,128)(2,1)S(1)}, bf16[384,2048]{1,0:T(8,128)(2,1)}, u32[]{:S(2)}, u32[]{:S(2)}) collective-permute-start(bf16[384,2048]{1,0:T(8,128)(2,1)S(1)} %bitcast.200), channel_id=1, source_target_pairs={{0,2},{2,0},{4,6},{6,4},{8,10},{10,8},{12,14},{14,12},{16,18},{18,... | collective-permute-start | bytes 4718600 | tf_op jit(solution)/shard_map/ppermute | solution.py:101
  264.1 298.8 %reduce-scatter.10.cloned.1.call-start = ((), (), s32[]{:S(2)}) async-start(), calls=%async_computation.14 | async-start | bytes 1966080 | tf_op jit(solution)/shard_map/reduce_scatter | solution.py:175
  433.5 60.3 %collective-permute-start.36 = (bf16[768,2048]{1,0:T(8,128)(2,1)}, bf16[768,2048]{1,0:T(8,128)(2,1)}, u32[]{:S(2)}, u32[]{:S(2)}) collective-permute-start(bf16[768,2048]{1,0:T(8,128)(2,1)} %convolution_convert_fusion.4), channel_id=1, source_target_pairs={{0,2},{2,0},{4,6},{6,4},{8,10},{10,8},{12,14},{14,12},{16,18},{18,... | collective-permute-start | bytes 9437192 | tf_op jit(solution)/shard_map/ppermute | solution.py:101
  443.8 72.5 %collective-permute-start.38 = (bf16[768,2048]{1,0:T(8,128)(2,1)}, bf16[768,2048]{1,0:T(8,128)(2,1)}, u32[]{:S(2)}, u32[]{:S(2)}) collective-permute-start(bf16[768,2048]{1,0:T(8,128)(2,1)} %convolution_convert_fusion.2), channel_id=1, source_target_pairs={{0,2},{2,0},{4,6},{6,4},{8,10},{10,8},{12,14},{14,12},{16,18},{18,... | collective-permute-start | bytes 9437192 | tf_op jit(solution)/shard_map/ppermute | solution.py:101
  476.2 96.8 %reduce-scatter.8.cloned.1.call-start = ((), (), s32[]{:S(2)}) async-start(), calls=%async_computation.13 | async-start | bytes 1966080 | tf_op jit(solution)/shard_map/reduce_scatter | solution.py:175
  535.8 75.8 %reduce-scatter.12.cloned.1.call-start = ((), (), s32[]{:S(2)}) async-start(), calls=%async_computation.15 | async-start | bytes 1966080 | tf_op jit(solution)/shard_map/reduce_scatter | solution.py:175
  577.6 84.0 %reduce-scatter.14.cloned.1.call-start = ((), (), s32[]{:S(2)}) async-start(), calls=%async_computation.16 | async-start | bytes 1720320 | tf_op jit(solution)/shard_map/reduce_scatter | solution.py:175
  623.4 97.7 %reduce-scatter.16.cloned.1.call-start = ((), (), s32[]{:S(2)}) async-start(), calls=%async_computation.17 | async-start | bytes 1966080 | tf_op jit(solution)/shard_map/reduce_scatter | solution.py:175
  677.9 98.0 %reduce-scatter.18.cloned.1.call-start = ((), (), s32[]{:S(2)}) async-start(), calls=%async_computation.18 | async-start | bytes 1966080 | tf_op jit(solution)/shard_map/reduce_scatter | solution.py:175
  677.9 42.0 %collective-permute-start.48 = (bf16[1024,768]{1,0:T(8,128)(2,1)}, bf16[1024,768]{1,0:T(8,128)(2,1)S(1)}, u32[]{:S(2)}, u32[]{:S(2)}) collective-permute-start(bf16[1024,768]{1,0:T(8,128)(2,1)} %add_rows.27), channel_id=1, source_target_pairs={{0,4},{2,6},{4,0},{6,2},{8,12},{10,14},{12,8},{14,10},{16,20},{18,... | collective-permute-start | bytes 4718600 | tf_op jit(solution)/shard_map/ppermute | solution.py:101
  728.5 95.7 %reduce-scatter.20.cloned.1.call-start = ((), (), s32[]{:S(2)}) async-start(), calls=%async_computation.19 | async-start | bytes 2211840 | tf_op jit(solution)/shard_map/reduce_scatter | solution.py:175
  729.8 46.1 %collective-permute-start.53 = (bf16[384,2304]{1,0:T(8,128)(2,1)S(1)}, bf16[384,2304]{1,0:T(8,128)(2,1)S(1)}, u32[]{:S(2)}, u32[]{:S(2)}) collective-permute-start(bf16[384,2304]{1,0:T(8,128)(2,1)S(1)} %copy-done.57), channel_id=1, source_target_pairs={{0,4},{2,6},{4,0},{6,2},{8,12},{10,14},{12,8},{14,10},{16,20},{18,... | collective-permute-start | bytes 5308424 | tf_op jit(solution)/shard_map/ppermute | solution.py:101
  (300 other events, 3603.6 us)
Sparse Core Ops, SparseCore 0:
  10.2 43.0 all-gather.6
  55.4 45.4 all-gather.8
  105.9 35.1 all-gather.10
  144.0 48.5 all-gather.12
  206.8 35.0 all-gather.14
  264.2 35.1 all-gather.16
  476.3 33.1 reduce-scatter.9
  535.9 33.0 reduce-scatter.7
  577.7 33.1 reduce-scatter.11
  623.5 30.9 reduce-scatter.13
  678.0 33.9 reduce-scatter.15
  728.6 38.0 reduce-scatter.17
  787.5 36.6 reduce-scatter.19

commit v2 on v1

--- a/solution.py
+++ b/solution.py
@@ -153,6 +153,38 @@
         compiler_params=pltpu.CompilerParams(vmem_limit_bytes=48 * 1024 * 1024),
         name="add_rows",
     )(*arrays)
+
+
+def join_blocks(*refs):
+    *sources, target = refs
+    half = len(sources) // 2
+    totals = []
+    for part in (sources[:half], sources[half:]):
+        total = part[0][...].astype(f32)
+        for source in part[1:]:
+            total = total + source[...].astype(f32)
+        totals.append(total.astype(bf16))
+    rows, width = totals[0].shape[0], totals[1].shape[1]
+    target[0, :rows, :] = totals[0][:, :width]
+    target[0, rows : 2 * rows, :] = totals[0][:, width:]
+    target[0, 2 * rows :, :] = totals[1]
+
+
+def join_sums(grid, long_parts, out_parts, long_rows, out_rows):
+    width = out_parts[0].shape[1]
+    rows = 2 * long_rows + out_rows
+    long_spec = pl.BlockSpec((long_rows, 2 * width), lambda i: (i, 0))
+    out_spec = pl.BlockSpec((out_rows, width), lambda i: (i, 0))
+    joined = pl.pallas_call(
+        join_blocks,
+        grid=(grid.outer_count,),
+        in_specs=[long_spec] * len(long_parts) + [out_spec] * len(out_parts),
+        out_specs=pl.BlockSpec((1, rows, width), lambda i: (i, 0, 0)),
+        out_shape=jax.ShapeDtypeStruct((grid.outer_count, rows, width), bf16),
+        cost_estimate=pl.CostEstimate(flops=1, bytes_accessed=1, transcendentals=0),
+        name="join_sums",
+    )(*long_parts, *out_parts)
+    return joined.reshape(grid.outer_count * rows, width)
 
 
 def core_away(grid, kept, moved):
@@ -649,9 +681,6 @@
     tkey_pieces = [tkey_near] + tkey_y + tkey_near_core + tkey_core
     text_raw = dot_pieces(feats, tkey_pieces)
     text_key_bf = head_call(norm_heads, "norm_text", text_raw, 0, text_gain, text_turns)
-    tval_core, out_core, long_core, long_near_core, long_y, text_key_bf, query_bf = fence(
-        tval_core, out_core, long_core, long_near_core, long_y, text_key_bf, query_bf
-    )
 
     out_own, out_other = stack([out_near] + out_y), stack(out_near_core + out_core)
     long_pairs = stack([long_near] + long_y + long_near_core + long_core)
@@ -765,16 +794,16 @@
             axis=1,
         )
     ).astype(bf16)
-    gate_kept = contract_rows(ffn_in_bf[:, :half_width], grad_gate_bf).astype(bf16)
     gate_away = contract_rows(ffn_in_bf[:, half_width:], grad_gate_bf).astype(bf16)
     down_away = core_away(grid, down_kept, down_core)
-    down_core, down_away, ffn_in_part, gate_kept, gate_away, grad_up_bf = fence(
-        down_core, down_away, ffn_in_part, gate_kept, gate_away, grad_up_bf
+    down_core, down_away, ffn_in_part, gate_away, grad_gate_bf, grad_up_bf = fence(
+        down_core, down_away, ffn_in_part, gate_away, grad_gate_bf, grad_up_bf
     )
 
     ffn_in_moved = swap_txt(ffn_in_part)
     down_moved = swap_inner(grid, down_away)
     gate_core = grid.send(gate_away, core=1)
+    gate_kept = contract_rows(ffn_in_bf[:, :half_width], grad_gate_bf).astype(bf16)
     up_kept = contract_rows(ffn_in_bf[:, :half_width], grad_up_bf).astype(bf16)
     up_away = contract_rows(ffn_in_bf[:, half_width:], grad_up_bf).astype(bf16)
     block_out = contract_cols(block_out, one_hot).astype(bf16)
@@ -886,16 +915,13 @@
     tval_core = grid.send(tval_away, core=1)
     null_moved = pair_sum(grid, null_rows, 1)
     up_grad = up_sum.astype(f32)
-    long_total = inner_total(grid, long_kept, long_core, long_moved)
-    out_total = inner_total(grid, out_kept, out_core, out_moved)
-    long_rows = LONG_DEV * 2
-    both_total = jnp.concatenate(
-        [
-            long_total.reshape(grid.outer_count, long_rows, own_width),
-            out_total.reshape(grid.outer_count, depth, own_width),
-        ],
-        axis=1,
-    ).reshape(-1, own_width)
+    both_total = join_sums(
+        grid,
+        [long_kept, long_core] + long_moved,
+        [out_kept, out_core] + out_moved,
+        LONG_DEV,
+        depth,
+    )
     both_sum = sum_outer(grid, both_total)
     grad_query_raw, query_gain_grad = head_call(
         norm_heads_back, "norm_queries_back", projected, 0, query_gain, turns,
@@ -913,13 +939,13 @@
     tval_moved = swap_inner(grid, tval_away)
     null_rows = null_rows + null_moved
     null_moved = pair_sum(grid, null_rows, 2)
-    out_grad = both_sum[long_rows:].astype(f32)
+    out_grad = both_sum[2 * LONG_DEV :].astype(f32)
     tkey_total = inner_total(grid, tkey_kept, tkey_core, tkey_moved)
     both_sum, tkey_total = fence(both_sum, tkey_total)
     tkey_sum = sum_outer(grid, tkey_total)
-    own_terms = both_sum[:long_rows].reshape(LONG_DEV, 2 * own_width).astype(f32)
-    grad_key = jnp.concatenate([own_terms[:, :own_width], grad_short_k], axis=0)
-    grad_value = jnp.concatenate([own_terms[:, own_width:], grad_short_v], axis=0)
+    own_terms = both_sum[: 2 * LONG_DEV].astype(f32)
+    grad_key = jnp.concatenate([own_terms[:LONG_DEV], grad_short_k], axis=0)
+    grad_value = jnp.concatenate([own_terms[LONG_DEV:], grad_short_v], axis=0)
     grad_key_raw, key_gain_grad = head_call(
         norm_heads_back, "norm_keys_back", projected, 1, key_gain, turns, (grad_key,)
     )

time: 876 us -> 855 us (0.976)
  local copies, waits for them, and re-layouts: 126 us -> 104 us
    unnamed x500 -> x486, local copies, waits for them, and re-layouts: 80.5 us -> 62.8 us
    pallas_call x16 -> x14, Pallas kernels: 43 us -> 43.2 us  [add_rows(): pl.pallas_call(add_blocks, grid=(rows // block,), in_specs=[from_row(star...]
  transfers between devices with their start and end apart: 80 -> 80, of which waited for: 29 -> 30; matrix products, arithmetic and copies ran while one was open for 26% -> 25% of each run, Pallas kernels for 17% -> 18%
where the time goes in v2:
time: 855 us; the launch traced here: 845 us
  waiting for transfers between devices  287 us (34%)
  Pallas kernels  177 us (21%)
  matrix products  138 us (16%)
  local copies, waits for them, and re-layouts  104 us (12%)
  starting transfers between devices  52.9 us (6%)
  other arithmetic  42.8 us (5%)
  blocking collectives  23.9 us (3%)
  between operations  19.1 us (2%)
    ppermute x50, waiting for transfers between devices, send(): return lax.ppermute(values, 'seq', pairs)  141 us
    ppermute x9, waiting for transfers between devices, swap_txt(): return lax.ppermute(values, 'txt', [(0, 1), (1, 0)])  72.6 us
    pallas_call x6, Pallas kernels, attend_call(): pl.pallas_call(attend_heads_back if back else attend_heads, grid=(width /...  68.1 us
    unnamed x486, local copies, waits for them, and re-layouts  62.8 us
    dot_general x24, matrix products, dot(): return jnp.dot(left_side, right_side, preferred_element_type=f32)  50.7 us
    dot_general x22, matrix products, contract_cols(): lax.dot_general(left_side, right_side, (((1,), (1,)), ((), ())), preferre...  48.1 us
    ppermute x8, waiting for transfers between devices, pair_sum(): return lax.ppermute(values, 'seq', pairs)  43.9 us
    pallas_call x14, Pallas kernels, add_rows(): pl.pallas_call(add_blocks, grid=(rows // block,), in_specs=[from_row(star...  43.2 us
  transfers between devices with their start and end apart: 80, of which 30 were waited for; matrix products, arithmetic and copies ran while one was open for 25% of the time, Pallas kernels for 18%

profile of v2, /device:TPU:0, one launch (start us, length us, event | category | flops | bytes accessed | tf_op | source)
XLA Modules:
  0.0 844.7 jit_solution(2782968192420355578)
XLA Ops:
  40.1 13.2 %all-gather.7.cloned.1.call-done = bf16[384,2304]{1,0:T(8,128)(2,1)} async-done(((bf16[96,2304]{1,0:T(8,128)(2,1)}), bf16[384,2304]{1,0:T(8,128)(2,1)}) %all-gather.7.cloned.1.call-update) | async-done | bytes 1769488 | tf_op jit(solution)/shard_map/all_gather | solution.py:116
  60.9 23.9 %all_gather.23 = bf16[384,768]{1,0:T(8,128)(2,1)} all-gather(bf16[96,768]{1,0:T(8,128)(2,1)} %param.32), channel_id=1, replica_groups={{0,8,16,24},{2,10,18,26},{4,12,20,28},{6,14,22,30},{1,9,17,25},{3,11,19..., dimensions={0}, use_global_device_ids=true | all-gather | bytes 737280 | tf_op jit(solution)/shard_map/all_gather | solution.py:116
  93.9 7.0 all-gather.9.cloned.1.call-done
  128.1 13.7 %collective-permute-done.10 = bf16[1024,768]{1,0:T(8,128)(2,1)} collective-permute-done((bf16[1024,768]{1,0:T(8,128)(2,1)}, bf16[1024,768]{1,0:T(8,128)(2,1)}, u32[]{:S(2)}, u32[]{:S(2)}) %collective-permute-start.10) | collective-permute-done | bytes 1572896 | tf_op jit(solution)/shard_map/ppermute | solution.py:101
  152.1 11.6 %attend_short.1 = (f32[448,768]{1,0:T(8,128)S(1)}, f32[448,768]{1,0:T(8,128)S(1)}) custom-call(s32[448,1]{1,0:T(8,128)S(1)} %copy.183.clip_ref, s32[1,448]{1,0:T(1,128)S(1)} %bitcast.184, bf16[448,768]{1,0:T(8,128)(2,1)S(1)} %slice.301.query_ref, bf16[448,768]{1,0:T(8,128)(2,1)S(1)} %slice.302.key_ref, bf16[448,768]{1,0:T(8,128)(2,1)S(1)} %slice.303.value_ref), custom_call_target="tpu_custom_call" | custom-call | flops 1 | bytes 1 | tf_op jit(solution)/shard_map/attend_short/pallas_call | solution.py:504
  168.5 27.9 %collective-permute-done.16 = bf16[384,768]{1,0:T(8,128)(2,1)} collective-permute-done((bf16[384,768]{1,0:T(8,128)(2,1)}, bf16[384,768]{1,0:T(8,128)(2,1)}, u32[]{:S(2)}, u32[]{:S(2)}) %collective-permute-start.16) | collective-permute-done | bytes 589856 | tf_op jit(solution)/shard_map/ppermute | solution.py:101
  228.7 12.0 %attend_cross.1 = (f32[512,768]{1,0:T(8,128)S(1)}, f32[512,768]{1,0:T(8,128)S(1)}) custom-call(s32[512,1]{1,0:T(8,128)S(1)} %copy.190.clip_ref, s32[1,256]{1,0:T(1,128)S(1)} %compare_select_fusion.key_clip_ref, bf16[512,768]{1,0:T(8,128)(2,1)S(1)} %copy-done.17, bf16[256,768]{1,0:T(8,128)(2,1)S(1)} %norm_text.1.key_ref, bf16[256,768]{1,0:T(8,128)(2,1)S(1)} %fusion.38.value_ref), custom_call_target="tpu_custom_call" | custom-call | flops 1 | bytes 1 | tf_op jit(solution)/shard_map/attend_cross/pallas_call | solution.py:504
  242.0 7.2 attend_long.1
  270.8 24.0 %collective-permute-done.24.moved_ref = bf16[512,1536]{1,0:T(8,128)(2,1)S(1)} collective-permute-done((bf16[512,1536]{1,0:T(8,128)(2,1)S(1)}, bf16[512,1536]{1,0:T(8,128)(2,1)S(1)}, u32[]{:S(2)}, u32[]{:S(2)}) %collective-permute-start.24) | collective-permute-done | bytes 1572896 | tf_op jit(solution)/shard_map/ppermute | solution.py:73
  327.1 7.2 collective-permute-done.29
  343.9 36.0 %collective-permute-done.32.moved_ref = bf16[512,1536]{1,0:T(8,128)(2,1)S(1)} collective-permute-done((bf16[512,1536]{1,0:T(8,128)(2,1)S(1)}, bf16[512,1536]{1,0:T(8,128)(2,1)S(1)}, u32[]{:S(2)}, u32[]{:S(2)}) %collective-permute-start.32) | collective-permute-done | bytes 1572896 | tf_op jit(solution)/shard_map/ppermute | solution.py:73
  397.1 7.0 multiply_convert_fusion.1
  437.6 23.1 %collective-permute-done.35.refs_2_ = bf16[384,2048]{1,0:T(8,128)(2,1)S(1)} collective-permute-done((bf16[384,2048]{1,0:T(8,128)(2,1)S(1)}, bf16[384,2048]{1,0:T(8,128)(2,1)S(1)}, u32[]{:S(2)}, u32[]{:S(2)}) %collective-permute-start.35) | collective-permute-done | bytes 1572896 | tf_op jit(solution)/shard_map/ppermute | solution.py:101
  469.2 12.7 %middle_rows.1 = (f32[512,1536]{1,0:T(8,128)}, bf16[512,1536]{1,0:T(8,128)(2,1)S(1)}, f32[4,1536]{1,0:T(4,128)S(1)}, f32[4,1536]{1,0:T(4,128)S(1)}) custom-call(s32[512,1]{1,0:T(8,128)S(1)} %copy.190.clip_ref, f32[512,1536]{1,0:T(8,128)} %get-tuple-element.237.res_ref, bf16[512,1536]{1,0:T(8,128)(2,1)S(1)} %fusion.22.grad_part_ref, ...), custom_call_target="tpu_custom_call" | custom-call | flops 1 | bytes 1 | tf_op jit(solution)/shard_map/middle_rows/pallas_call | solution.py:375
  488.4 9.9 %attend_long_back.1 = (f32[64,768]{1,0:T(8,128)S(1)}, bf16[1024,768]{1,0:T(8,128)(2,1)S(1)}, bf16[1024,768]{1,0:T(8,128)(2,1)S(1)}) custom-call(s32[64,1]{1,0:T(8,128)S(1)} %copy-done.73, s32[1,1024]{1,0:T(1,128)S(1)} %broadcast_in_dim.215.key_clip_ref, bf16[64,768]{1,0:T(8,128)(2,1)S(1)} %copy-done.65, bf16[1024,1536]{1,0:T(8,128)(2,1)} %copy-done.3, ...), custom_call_target="tpu_custom_call" | custom-call | flops 1 | bytes 1 | tf_op jit(solution)/shard_map/attend_long_back/pallas_call | solution.py:504
  508.4 12.3 %collective-permute-done.37.refs_2_ = bf16[384,2048]{1,0:T(8,128)(2,1)S(1)} collective-permute-done((bf16[384,2048]{1,0:T(8,128)(2,1)S(1)}, bf16[384,2048]{1,0:T(8,128)(2,1)S(1)}, u32[]{:S(2)}, u32[]{:S(2)}) %collective-permute-start.37) | collective-permute-done | bytes 1572896 | tf_op jit(solution)/shard_map/ppermute | solution.py:101
  528.6 10.8 %attend_cross_back.1 = (f32[512,768]{1,0:T(8,128)S(1)}, f32[256,768]{1,0:T(8,128)S(1)}, f32[256,768]{1,0:T(8,128)S(1)}) custom-call(s32[512,1]{1,0:T(8,128)S(1)} %copy.190.clip_ref, s32[1,256]{1,0:T(1,128)S(1)} %compare_select_fusion.key_clip_ref, bf16[512,768]{1,0:T(8,128)(2,1)S(1)} %copy-done.18, bf16[256,768]{1,0:T(8,128)(2,1)S(1)} %copy-done.44, ...), custom_call_target="tpu_custom_call" | custom-call | flops 1 | bytes 1 | tf_op jit(solution)/shard_map/attend_cross_back/pallas_call | solution.py:504
  551.9 10.2 %collective-permute-done.39.refs_2_ = bf16[384,2048]{1,0:T(8,128)(2,1)} collective-permute-done((bf16[384,2048]{1,0:T(8,128)(2,1)}, bf16[384,2048]{1,0:T(8,128)(2,1)}, u32[]{:S(2)}, u32[]{:S(2)}) %collective-permute-start.39) | collective-permute-done | bytes 1572896 | tf_op jit(solution)/shard_map/ppermute | solution.py:101
  573.2 16.7 %attend_short_back.1 = (f32[448,768]{1,0:T(8,128)S(1)}, f32[448,768]{1,0:T(8,128)S(1)}, f32[448,768]{1,0:T(8,128)}) custom-call(s32[448,1]{1,0:T(8,128)S(1)} %copy-done.46, s32[1,448]{1,0:T(1,128)S(1)} %bitcast.185, bf16[448,768]{1,0:T(8,128)(2,1)S(1)} %copy-done.36, bf16[448,768]{1,0:T(8,128)(2,1)S(1)} %copy-done.32, bf16[448,768]{1,0:T(8,128)(2,1)S(1)} %copy-done.34, ...), custom_call_target="tpu_custom_call" | custom-call | flops 1 | bytes 1 | tf_op jit(solution)/shard_map/attend_short_back/pallas_call | solution.py:504
  618.0 23.5 %collective-permute-done.45.refs_2_ = bf16[1024,768]{1,0:T(8,128)(2,1)S(1)} collective-permute-done((bf16[1024,768]{1,0:T(8,128)(2,1)}, bf16[1024,768]{1,0:T(8,128)(2,1)S(1)}, u32[]{:S(2)}, u32[]{:S(2)}) %collective-permute-start.45) | collective-permute-done | bytes 1572896 | tf_op jit(solution)/shard_map/ppermute | solution.py:101
  677.6 22.7 %collective-permute-done.49 = bf16[64,1536]{1,0:T(8,128)(2,1)S(1)} collective-permute-done((bf16[64,1536]{1,0:T(8,128)(2,1)S(1)}, bf16[64,1536]{1,0:T(8,128)(2,1)S(1)}, u32[]{:S(2)}, u32[]{:S(2)}) %collective-permute-start.49) | collective-permute-done | bytes 196640 | tf_op jit(solution)/shard_map/ppermute | solution.py:214
  727.3 9.7 %collective-permute-done.52 = bf16[256,1536]{1,0:T(8,128)(2,1)S(1)} collective-permute-done((bf16[256,1536]{1,0:T(8,128)(2,1)}, bf16[256,1536]{1,0:T(8,128)(2,1)S(1)}, u32[]{:S(2)}, u32[]{:S(2)}) %collective-permute-start.52) | collective-permute-done | bytes 786464 | tf_op jit(solution)/shard_map/ppermute | solution.py:73
  794.4 9.2 %reduce-scatter.20.cloned.1.call-done = bf16[96,2304]{1,0:T(8,128)(2,1)} async-done(((bf16[384,2304]{1,0:T(8,128)(2,1)}), bf16[96,2304]{1,0:T(8,128)(2,1)}) %reduce-scatter.20.cloned.1.call-update) | async-done | bytes 442384 | tf_op jit(solution)/shard_map/reduce_scatter | solution.py:207
  817.2 10.6 %collective-permute-done.65 = f32[60,1024]{1,0:T(8,128)S(1)} collective-permute-done((f32[60,1024]{1,0:T(8,128)S(1)}, f32[60,1024]{1,0:T(8,128)S(1)}, u32[]{:S(2)}, u32[]{:S(2)}) %collective-permute-start.65) | collective-permute-done | bytes 245792 | tf_op jit(solution)/shard_map/ppermute | solution.py:214
  (941 shorter events, 463.6 us)
Async XLA Ops:
  7.2 46.0 %all-gather.7.cloned.1.call-start = ((), (), s32[]{:S(2)}) async-start(), calls=%async_computation.7 | async-start | bytes 2211840 | tf_op jit(solution)/shard_map/all_gather | solution.py:116
  9.3 91.7 %all-gather.9.cloned.1.call-start = ((), (), s32[]{:S(2)}) async-start(), calls=%async_computation.8 | async-start | bytes 1966080 | tf_op jit(solution)/shard_map/all_gather | solution.py:116
  53.3 40.7 %collective-permute-start.8 = (bf16[384,2304]{1,0:T(8,128)(2,1)}, bf16[384,2304]{1,0:T(8,128)(2,1)}, u32[]{:S(2)}, u32[]{:S(2)}) collective-permute-start(bf16[384,2304]{1,0:T(8,128)(2,1)} %all-gather.7.cloned.1.call-done), channel_id=1, source_target_pairs={{0,4},{2,6},{4,0},{6,2},{8,12},{10,14},{12,8},{14,10},{16,20},{18,... | collective-permute-start | bytes 5308424 | tf_op jit(solution)/shard_map/ppermute | solution.py:101
  54.7 39.2 %collective-permute-start.7 = (bf16[384,2304]{1,0:T(8,128)(2,1)}, bf16[384,2304]{1,0:T(8,128)(2,1)}, u32[]{:S(2)}, u32[]{:S(2)}) collective-permute-start(bf16[384,2304]{1,0:T(8,128)(2,1)} %all-gather.7.cloned.1.call-done), channel_id=1, source_target_pairs={{0,2},{2,0},{4,6},{6,4},{8,10},{10,8},{12,14},{14,12},{16,18},{18,... | collective-permute-start | bytes 5308424 | tf_op jit(solution)/shard_map/ppermute | solution.py:101
  55.1 86.7 %all-gather.11.cloned.1.call-start = ((), (), s32[]{:S(2)}) async-start(), calls=%async_computation.9 | async-start | bytes 1966080 | tf_op jit(solution)/shard_map/all_gather | solution.py:116
  105.8 93.1 %all-gather.13.cloned.1.call-start = ((), (), s32[]{:S(2)}) async-start(), calls=%async_computation.10 | async-start | bytes 2949120 | tf_op jit(solution)/shard_map/all_gather | solution.py:116
  143.9 114.3 %all-gather.15.cloned.1.call-start = ((), (), s32[]{:S(2)}) async-start(), calls=%async_computation.11 | async-start | bytes 1966080 | tf_op jit(solution)/shard_map/all_gather | solution.py:116
  146.6 51.0 %collective-permute-start.14 = (bf16[1024,768]{1,0:T(8,128)(2,1)}, bf16[1024,768]{1,0:T(8,128)(2,1)S(1)}, u32[]{:S(2)}, u32[]{:S(2)}) collective-permute-start(bf16[1024,768]{1,0:T(8,128)(2,1)} %all-gather.11.cloned.1.call-done), channel_id=1, source_target_pairs={{0,2},{2,0},{4,6},{6,4},{8,10},{10,8},{12,14},{14,12},{16,18},{18,... | collective-permute-start | bytes 4718600 | tf_op jit(solution)/shard_map/ppermute | solution.py:101
  146.6 52.2 %collective-permute-start.13 = (bf16[1024,768]{1,0:T(8,128)(2,1)}, bf16[1024,768]{1,0:T(8,128)(2,1)}, u32[]{:S(2)}, u32[]{:S(2)}) collective-permute-start(bf16[1024,768]{1,0:T(8,128)(2,1)} %all-gather.11.cloned.1.call-done), channel_id=1, source_target_pairs={{0,4},{2,6},{4,0},{6,2},{8,12},{10,14},{12,8},{14,10},{16,20},{18,... | collective-permute-start | bytes 4718600 | tf_op jit(solution)/shard_map/ppermute | solution.py:101
  147.4 49.0 %collective-permute-start.15 = (bf16[1024,768]{1,0:T(8,128)(2,1)}, bf16[1024,768]{1,0:T(8,128)(2,1)S(1)}, u32[]{:S(2)}, u32[]{:S(2)}) collective-permute-start(bf16[1024,768]{1,0:T(8,128)(2,1)} %collective-permute-done.10), channel_id=1, source_target_pairs={{0,2},{2,0},{4,6},{6,4},{8,10},{10,8},{12,14},{14,12},{16,18},{18,... | collective-permute-start | bytes 4718600 | tf_op jit(solution)/shard_map/ppermute | solution.py:101
  149.0 47.4 %collective-permute-start.16 = (bf16[384,768]{1,0:T(8,128)(2,1)}, bf16[384,768]{1,0:T(8,128)(2,1)}, u32[]{:S(2)}, u32[]{:S(2)}) collective-permute-start(bf16[384,768]{1,0:T(8,128)(2,1)} %all_gather.23), channel_id=1, source_target_pairs={{0,4},{2,6},{4,0},{6,2},{8,12},{10,14},{12,8},{14,10},{16,20},{18,... | collective-permute-start | bytes 1769480 | tf_op jit(solution)/shard_map/ppermute | solution.py:101
  205.0 92.2 %all-gather.17.cloned.1.call-start = ((), (), s32[]{:S(2)}) async-start(), calls=%async_computation.12 | async-start | bytes 1966080 | tf_op jit(solution)/shard_map/all_gather | solution.py:116
  212.0 41.2 %collective-permute-start.23 = (bf16[384,2048]{1,0:T(8,128)(2,1)S(1)}, bf16[384,2048]{1,0:T(8,128)(2,1)}, u32[]{:S(2)}, u32[]{:S(2)}) collective-permute-start(bf16[384,2048]{1,0:T(8,128)(2,1)S(1)} %bitcast.198), channel_id=1, source_target_pairs={{0,2},{2,0},{4,6},{6,4},{8,10},{10,8},{12,14},{14,12},{16,18},{18,... | collective-permute-start | bytes 4718600 | tf_op jit(solution)/shard_map/ppermute | solution.py:101
  258.3 293.6 %reduce-scatter.10.cloned.1.call-start = ((), (), s32[]{:S(2)}) async-start(), calls=%async_computation.14 | async-start | bytes 1966080 | tf_op jit(solution)/shard_map/reduce_scatter | solution.py:207
  423.8 58.9 %collective-permute-start.36 = (bf16[768,2048]{1,0:T(8,128)(2,1)}, bf16[768,2048]{1,0:T(8,128)(2,1)}, u32[]{:S(2)}, u32[]{:S(2)}) collective-permute-start(bf16[768,2048]{1,0:T(8,128)(2,1)} %convolution_convert_fusion.5), channel_id=1, source_target_pairs={{0,2},{2,0},{4,6},{6,4},{8,10},{10,8},{12,14},{14,12},{16,18},{18,... | collective-permute-start | bytes 9437192 | tf_op jit(solution)/shard_map/ppermute | solution.py:101
  434.1 70.6 %collective-permute-start.38 = (bf16[768,2048]{1,0:T(8,128)(2,1)}, bf16[768,2048]{1,0:T(8,128)(2,1)}, u32[]{:S(2)}, u32[]{:S(2)}) collective-permute-start(bf16[768,2048]{1,0:T(8,128)(2,1)} %convolution_convert_fusion.2), channel_id=1, source_target_pairs={{0,2},{2,0},{4,6},{6,4},{8,10},{10,8},{12,14},{14,12},{16,18},{18,... | collective-permute-start | bytes 9437192 | tf_op jit(solution)/shard_map/ppermute | solution.py:101
  465.4 96.7 %reduce-scatter.8.cloned.1.call-start = ((), (), s32[]{:S(2)}) async-start(), calls=%async_computation.13 | async-start | bytes 1966080 | tf_op jit(solution)/shard_map/reduce_scatter | solution.py:207
  524.8 75.3 %reduce-scatter.12.cloned.1.call-start = ((), (), s32[]{:S(2)}) async-start(), calls=%async_computation.15 | async-start | bytes 1966080 | tf_op jit(solution)/shard_map/reduce_scatter | solution.py:207
  566.7 76.0 %reduce-scatter.14.cloned.1.call-start = ((), (), s32[]{:S(2)}) async-start(), calls=%async_computation.16 | async-start | bytes 1720320 | tf_op jit(solution)/shard_map/reduce_scatter | solution.py:207
  604.4 97.8 %reduce-scatter.16.cloned.1.call-start = ((), (), s32[]{:S(2)}) async-start(), calls=%async_computation.17 | async-start | bytes 1966080 | tf_op jit(solution)/shard_map/reduce_scatter | solution.py:207
  659.0 98.3 %reduce-scatter.18.cloned.1.call-start = ((), (), s32[]{:S(2)}) async-start(), calls=%async_computation.18 | async-start | bytes 1966080 | tf_op jit(solution)/shard_map/reduce_scatter | solution.py:207
  659.0 42.0 %collective-permute-start.48 = (bf16[1024,768]{1,0:T(8,128)(2,1)}, bf16[1024,768]{1,0:T(8,128)(2,1)S(1)}, u32[]{:S(2)}, u32[]{:S(2)}) collective-permute-start(bf16[1024,768]{1,0:T(8,128)(2,1)} %add_rows.23), channel_id=1, source_target_pairs={{0,4},{2,6},{4,0},{6,2},{8,12},{10,14},{12,8},{14,10},{16,20},{18,... | collective-permute-start | bytes 4718600 | tf_op jit(solution)/shard_map/ppermute | solution.py:101
  709.6 94.0 %reduce-scatter.20.cloned.1.call-start = ((), (), s32[]{:S(2)}) async-start(), calls=%async_computation.19 | async-start | bytes 2211840 | tf_op jit(solution)/shard_map/reduce_scatter | solution.py:207
  710.9 46.4 %collective-permute-start.53 = (bf16[384,2304]{1,0:T(8,128)(2,1)S(1)}, bf16[384,2304]{1,0:T(8,128)(2,1)S(1)}, u32[]{:S(2)}, u32[]{:S(2)}) collective-permute-start(bf16[384,2304]{1,0:T(8,128)(2,1)S(1)} %copy-done.48), channel_id=1, source_target_pairs={{0,4},{2,6},{4,0},{6,2},{8,12},{10,14},{12,8},{14,10},{16,20},{18,... | collective-permute-start | bytes 5308424 | tf_op jit(solution)/shard_map/ppermute | solution.py:101
  (292 other events, 3606.0 us)
Sparse Core Ops, SparseCore 0:
  10.2 43.0 all-gather.6
  55.4 45.5 all-gather.8
  105.9 35.1 all-gather.10
  144.0 48.5 all-gather.12
  205.1 35.0 all-gather.14
  258.4 35.1 all-gather.16
  465.5 33.1 reduce-scatter.9
  524.9 33.0 reduce-scatter.7
  566.8 33.2 reduce-scatter.11
  604.5 31.3 reduce-scatter.13
  659.1 34.4 reduce-scatter.15
  709.7 38.4 reduce-scatter.17
  767.0 36.6 reduce-scatter.19

commit v3 on v2

--- a/solution.py
+++ b/solution.py
@@ -808,8 +808,8 @@
     up_away = contract_rows(ffn_in_bf[:, half_width:], grad_up_bf).astype(bf16)
     block_out = contract_cols(block_out, one_hot).astype(bf16)
     gate_away = core_away(grid, gate_kept, gate_core)
-    block_out, ffn_in_moved, down_moved, up_kept = fence(
-        block_out, ffn_in_moved, down_moved, up_kept
+    block_out, ffn_in_moved, down_moved, up_kept, gate_kept, gate_away = fence(
+        block_out, ffn_in_moved, down_moved, up_kept, gate_kept, gate_away
     )
 
     down_total = inner_total(grid, down_kept, down_core, down_moved)
@@ -1072,6 +1072,7 @@
     packed = jnp.pad(packed, (0, -packed.shape[0] % 1024)).reshape(-1, 1024)
     packed = packed + pair_sum(grid, packed, 1)
     packed = packed + pair_sum(grid, packed, 2)
+    packed = packed + swap_txt(packed)
     packed, qkv_sum = fence(packed, qkv_sum)
     packed = packed + pair_sum(grid, packed, 4)
     packed, null_moved = fence(packed, null_moved)
@@ -1080,7 +1081,7 @@
     )
     qkv_grad = qkv_sum.astype(f32).reshape(depth, 3, own_width)
     packed = sum_seq(grid, packed, 8)
-    packed = (packed + swap_txt(packed)).reshape(-1)
+    packed = packed.reshape(-1)
     condition_grad = packed[:cond_count].reshape(cond_part.shape)
     norm_gains_grad = packed[cond_count : cond_count + gains_count].reshape(gains_term.shape)
     head_gates_grad = packed[cond_count + gains_count : cond_count + gains_count + H]

time: 855 us -> 846 us (0.989)
  waiting for transfers between devices: 287 us -> 274 us
    reduce_scatter x7, waiting for transfers between devices: 9.44 us -> 0.3 us  [sum_outer(): lax.psum_scatter(total, 'seq', scatter_dimension=0, tiled=True, axis_inde...]
    unnamed x486 -> x500, local copies, waits for them, and re-layouts: 62.8 us -> 71.4 us
  transfers between devices with their start and end apart: 80 -> 80, of which waited for: 30 -> 31; matrix products, arithmetic and copies ran while one was open for 25% -> 25% of each run, Pallas kernels for 18% -> 18%
where the time goes in v3:
time: 846 us; the launch traced here: 835 us
  waiting for transfers between devices  274 us (32%)
  Pallas kernels  175 us (21%)
  matrix products  133 us (16%)
  local copies, waits for them, and re-layouts  112 us (13%)
  starting transfers between devices  54.9 us (6%)
  other arithmetic  42.9 us (5%)
  blocking collectives  23.9 us (3%)
  between operations  18.8 us (2%)
    ppermute x50, waiting for transfers between devices, send(): return lax.ppermute(values, 'seq', pairs)  137 us
    ppermute x9, waiting for transfers between devices, swap_txt(): return lax.ppermute(values, 'txt', [(0, 1), (1, 0)])  73.4 us
    unnamed x500, local copies, waits for them, and re-layouts  71.4 us
    pallas_call x6, Pallas kernels, attend_call(): pl.pallas_call(attend_heads_back if back else attend_heads, grid=(width /...  68 us
    dot_general x24, matrix products, dot(): return jnp.dot(left_side, right_side, preferred_element_type=f32)  51.3 us
    dot_general x22, matrix products, contract_cols(): lax.dot_general(left_side, right_side, (((1,), (1,)), ((), ())), preferre...  45.9 us
    ppermute x8, waiting for transfers between devices, pair_sum(): return lax.ppermute(values, 'seq', pairs)  43 us
    pallas_call x14, Pallas kernels, add_rows(): pl.pallas_call(add_blocks, grid=(rows // block,), in_specs=[from_row(star...  42.5 us
  transfers between devices with their start and end apart: 80, of which 31 were waited for; matrix products, arithmetic and copies ran while one was open for 25% of the time, Pallas kernels for 18%

profile of v3, /device:TPU:0, one launch (start us, length us, event | category | flops | bytes accessed | tf_op | source)
XLA Modules:
  0.0 835.0 jit_solution(3922654246517169509)
XLA Ops:
  40.0 13.2 %all-gather.7.cloned.1.call-done = bf16[384,2304]{1,0:T(8,128)(2,1)} async-done(((bf16[96,2304]{1,0:T(8,128)(2,1)}), bf16[384,2304]{1,0:T(8,128)(2,1)}) %all-gather.7.cloned.1.call-update) | async-done | bytes 1769488 | tf_op jit(solution)/shard_map/all_gather | solution.py:116
  60.9 23.9 %all_gather.23 = bf16[384,768]{1,0:T(8,128)(2,1)} all-gather(bf16[96,768]{1,0:T(8,128)(2,1)} %param.32), channel_id=1, replica_groups={{0,8,16,24},{2,10,18,26},{4,12,20,28},{6,14,22,30},{1,9,17,25},{3,11,19..., dimensions={0}, use_global_device_ids=true | all-gather | bytes 737280 | tf_op jit(solution)/shard_map/all_gather | solution.py:116
  93.9 7.0 all-gather.9.cloned.1.call-done
  128.2 13.7 %collective-permute-done.10 = bf16[1024,768]{1,0:T(8,128)(2,1)} collective-permute-done((bf16[1024,768]{1,0:T(8,128)(2,1)}, bf16[1024,768]{1,0:T(8,128)(2,1)}, u32[]{:S(2)}, u32[]{:S(2)}) %collective-permute-start.10) | collective-permute-done | bytes 1572896 | tf_op jit(solution)/shard_map/ppermute | solution.py:101
  152.1 11.6 %attend_short.1 = (f32[448,768]{1,0:T(8,128)S(1)}, f32[448,768]{1,0:T(8,128)S(1)}) custom-call(s32[448,1]{1,0:T(8,128)S(1)} %copy.183.clip_ref, s32[1,448]{1,0:T(1,128)S(1)} %bitcast.184, bf16[448,768]{1,0:T(8,128)(2,1)S(1)} %slice.301.query_ref, bf16[448,768]{1,0:T(8,128)(2,1)S(1)} %slice.302.key_ref, bf16[448,768]{1,0:T(8,128)(2,1)S(1)} %slice.303.value_ref), custom_call_target="tpu_custom_call" | custom-call | flops 1 | bytes 1 | tf_op jit(solution)/shard_map/attend_short/pallas_call | solution.py:504
  168.5 27.9 %collective-permute-done.16 = bf16[384,768]{1,0:T(8,128)(2,1)} collective-permute-done((bf16[384,768]{1,0:T(8,128)(2,1)}, bf16[384,768]{1,0:T(8,128)(2,1)}, u32[]{:S(2)}, u32[]{:S(2)}) %collective-permute-start.16) | collective-permute-done | bytes 589856 | tf_op jit(solution)/shard_map/ppermute | solution.py:101
  228.6 12.0 %attend_cross.1 = (f32[512,768]{1,0:T(8,128)S(1)}, f32[512,768]{1,0:T(8,128)S(1)}) custom-call(s32[512,1]{1,0:T(8,128)S(1)} %copy.190.clip_ref, s32[1,256]{1,0:T(1,128)S(1)} %compare_select_fusion.key_clip_ref, bf16[512,768]{1,0:T(8,128)(2,1)S(1)} %copy-done.17, bf16[256,768]{1,0:T(8,128)(2,1)S(1)} %norm_text.1.key_ref, bf16[256,768]{1,0:T(8,128)(2,1)S(1)} %fusion.38.value_ref), custom_call_target="tpu_custom_call" | custom-call | flops 1 | bytes 1 | tf_op jit(solution)/shard_map/attend_cross/pallas_call | solution.py:504
  242.0 7.2 attend_long.1
  270.4 24.0 %collective-permute-done.24.moved_ref = bf16[512,1536]{1,0:T(8,128)(2,1)S(1)} collective-permute-done((bf16[512,1536]{1,0:T(8,128)(2,1)S(1)}, bf16[512,1536]{1,0:T(8,128)(2,1)S(1)}, u32[]{:S(2)}, u32[]{:S(2)}) %collective-permute-start.24) | collective-permute-done | bytes 1572896 | tf_op jit(solution)/shard_map/ppermute | solution.py:73
  326.3 7.6 collective-permute-done.29
  343.6 36.0 %collective-permute-done.32.moved_ref = bf16[512,1536]{1,0:T(8,128)(2,1)S(1)} collective-permute-done((bf16[512,1536]{1,0:T(8,128)(2,1)S(1)}, bf16[512,1536]{1,0:T(8,128)(2,1)S(1)}, u32[]{:S(2)}, u32[]{:S(2)}) %collective-permute-start.32) | collective-permute-done | bytes 1572896 | tf_op jit(solution)/shard_map/ppermute | solution.py:73
  396.7 7.5 multiply_convert_fusion.1
  440.6 19.2 %collective-permute-done.35.refs_2_ = bf16[384,2048]{1,0:T(8,128)(2,1)S(1)} collective-permute-done((bf16[384,2048]{1,0:T(8,128)(2,1)S(1)}, bf16[384,2048]{1,0:T(8,128)(2,1)S(1)}, u32[]{:S(2)}, u32[]{:S(2)}) %collective-permute-start.35) | collective-permute-done | bytes 1572896 | tf_op jit(solution)/shard_map/ppermute | solution.py:101
  470.8 11.7 %middle_rows.1 = (f32[512,1536]{1,0:T(8,128)}, bf16[512,1536]{1,0:T(8,128)(2,1)S(1)}, f32[4,1536]{1,0:T(4,128)S(1)}, f32[4,1536]{1,0:T(4,128)S(1)}) custom-call(s32[512,1]{1,0:T(8,128)S(1)} %copy.190.clip_ref, f32[512,1536]{1,0:T(8,128)} %get-tuple-element.239.res_ref, bf16[512,1536]{1,0:T(8,128)(2,1)S(1)} %copy-done.32, bf16[512,1536]{1,0:T(8,128)(2,1)S(1)} %copy-done.57, ...), custom_call_target="tpu_custom_call" | custom-call | flops 1 | bytes 1 | tf_op jit(solution)/shard_map/middle_rows/pallas_call | solution.py:375
  488.5 9.7 %attend_long_back.1 = (f32[64,768]{1,0:T(8,128)S(1)}, bf16[1024,768]{1,0:T(8,128)(2,1)S(1)}, bf16[1024,768]{1,0:T(8,128)(2,1)S(1)}) custom-call(s32[64,1]{1,0:T(8,128)S(1)} %copy-done.79, s32[1,1024]{1,0:T(1,128)S(1)} %broadcast_in_dim.215.key_clip_ref, bf16[64,768]{1,0:T(8,128)(2,1)S(1)} %copy-done.72, bf16[1024,1536]{1,0:T(8,128)(2,1)} %copy-done.3, ...), custom_call_target="tpu_custom_call" | custom-call | flops 1 | bytes 1 | tf_op jit(solution)/shard_map/attend_long_back/pallas_call | solution.py:504
  507.4 11.7 %collective-permute-done.37.refs_2_ = bf16[384,2048]{1,0:T(8,128)(2,1)S(1)} collective-permute-done((bf16[384,2048]{1,0:T(8,128)(2,1)S(1)}, bf16[384,2048]{1,0:T(8,128)(2,1)S(1)}, u32[]{:S(2)}, u32[]{:S(2)}) %collective-permute-start.37) | collective-permute-done | bytes 1572896 | tf_op jit(solution)/shard_map/ppermute | solution.py:101
  527.0 10.8 %attend_cross_back.1 = (f32[512,768]{1,0:T(8,128)S(1)}, f32[256,768]{1,0:T(8,128)S(1)}, f32[256,768]{1,0:T(8,128)S(1)}) custom-call(s32[512,1]{1,0:T(8,128)S(1)} %copy.190.clip_ref, s32[1,256]{1,0:T(1,128)S(1)} %compare_select_fusion.key_clip_ref, bf16[512,768]{1,0:T(8,128)(2,1)S(1)} %copy-done.18, bf16[256,768]{1,0:T(8,128)(2,1)S(1)} %copy-done.47, ...), custom_call_target="tpu_custom_call" | custom-call | flops 1 | bytes 1 | tf_op jit(solution)/shard_map/attend_cross_back/pallas_call | solution.py:504
  550.3 10.1 %collective-permute-done.39.refs_2_ = bf16[384,2048]{1,0:T(8,128)(2,1)} collective-permute-done((bf16[384,2048]{1,0:T(8,128)(2,1)}, bf16[384,2048]{1,0:T(8,128)(2,1)}, u32[]{:S(2)}, u32[]{:S(2)}) %collective-permute-start.39) | collective-permute-done | bytes 1572896 | tf_op jit(solution)/shard_map/ppermute | solution.py:101
  571.6 16.7 %attend_short_back.1 = (f32[448,768]{1,0:T(8,128)S(1)}, f32[448,768]{1,0:T(8,128)S(1)}, f32[448,768]{1,0:T(8,128)}) custom-call(s32[448,1]{1,0:T(8,128)S(1)} %copy-done.49, s32[1,448]{1,0:T(1,128)S(1)} %bitcast.185, bf16[448,768]{1,0:T(8,128)(2,1)S(1)} %copy-done.39, bf16[448,768]{1,0:T(8,128)(2,1)S(1)} %copy-done.35, bf16[448,768]{1,0:T(8,128)(2,1)S(1)} %copy-done.37, ...), custom_call_target="tpu_custom_call" | custom-call | flops 1 | bytes 1 | tf_op jit(solution)/shard_map/attend_short_back/pallas_call | solution.py:504
  616.5 23.4 %collective-permute-done.45.refs_2_ = bf16[1024,768]{1,0:T(8,128)(2,1)S(1)} collective-permute-done((bf16[1024,768]{1,0:T(8,128)(2,1)}, bf16[1024,768]{1,0:T(8,128)(2,1)S(1)}, u32[]{:S(2)}, u32[]{:S(2)}) %collective-permute-start.45) | collective-permute-done | bytes 1572896 | tf_op jit(solution)/shard_map/ppermute | solution.py:101
  675.9 22.7 %collective-permute-done.49 = bf16[64,1536]{1,0:T(8,128)(2,1)S(1)} collective-permute-done((bf16[64,1536]{1,0:T(8,128)(2,1)S(1)}, bf16[64,1536]{1,0:T(8,128)(2,1)S(1)}, u32[]{:S(2)}, u32[]{:S(2)}) %collective-permute-start.49) | collective-permute-done | bytes 196640 | tf_op jit(solution)/shard_map/ppermute | solution.py:214
  725.6 9.7 %collective-permute-done.52 = bf16[256,1536]{1,0:T(8,128)(2,1)S(1)} collective-permute-done((bf16[256,1536]{1,0:T(8,128)(2,1)}, bf16[256,1536]{1,0:T(8,128)(2,1)S(1)}, u32[]{:S(2)}, u32[]{:S(2)}) %collective-permute-start.52) | collective-permute-done | bytes 786464 | tf_op jit(solution)/shard_map/ppermute | solution.py:73
  737.7 6.6 last_rows.1
  819.6 6.7 collective-permute-done.66
  (955 shorter events, 465.5 us)
Async XLA Ops:
  7.2 46.0 %all-gather.7.cloned.1.call-start = ((), (), s32[]{:S(2)}) async-start(), calls=%async_computation.7 | async-start | bytes 2211840 | tf_op jit(solution)/shard_map/all_gather | solution.py:116
  9.3 91.7 %all-gather.9.cloned.1.call-start = ((), (), s32[]{:S(2)}) async-start(), calls=%async_computation.8 | async-start | bytes 1966080 | tf_op jit(solution)/shard_map/all_gather | solution.py:116
  53.3 40.7 %collective-permute-start.8 = (bf16[384,2304]{1,0:T(8,128)(2,1)}, bf16[384,2304]{1,0:T(8,128)(2,1)}, u32[]{:S(2)}, u32[]{:S(2)}) collective-permute-start(bf16[384,2304]{1,0:T(8,128)(2,1)} %all-gather.7.cloned.1.call-done), channel_id=1, source_target_pairs={{0,4},{2,6},{4,0},{6,2},{8,12},{10,14},{12,8},{14,10},{16,20},{18,... | collective-permute-start | bytes 5308424 | tf_op jit(solution)/shard_map/ppermute | solution.py:101
  54.7 39.2 %collective-permute-start.7 = (bf16[384,2304]{1,0:T(8,128)(2,1)}, bf16[384,2304]{1,0:T(8,128)(2,1)}, u32[]{:S(2)}, u32[]{:S(2)}) collective-permute-start(bf16[384,2304]{1,0:T(8,128)(2,1)} %all-gather.7.cloned.1.call-done), channel_id=1, source_target_pairs={{0,2},{2,0},{4,6},{6,4},{8,10},{10,8},{12,14},{14,12},{16,18},{18,... | collective-permute-start | bytes 5308424 | tf_op jit(solution)/shard_map/ppermute | solution.py:101
  55.1 86.7 %all-gather.11.cloned.1.call-start = ((), (), s32[]{:S(2)}) async-start(), calls=%async_computation.9 | async-start | bytes 1966080 | tf_op jit(solution)/shard_map/all_gather | solution.py:116
  105.8 93.0 %all-gather.13.cloned.1.call-start = ((), (), s32[]{:S(2)}) async-start(), calls=%async_computation.10 | async-start | bytes 2949120 | tf_op jit(solution)/shard_map/all_gather | solution.py:116
  143.9 114.2 %all-gather.15.cloned.1.call-start = ((), (), s32[]{:S(2)}) async-start(), calls=%async_computation.11 | async-start | bytes 1966080 | tf_op jit(solution)/shard_map/all_gather | solution.py:116
  146.6 51.0 %collective-permute-start.14 = (bf16[1024,768]{1,0:T(8,128)(2,1)}, bf16[1024,768]{1,0:T(8,128)(2,1)S(1)}, u32[]{:S(2)}, u32[]{:S(2)}) collective-permute-start(bf16[1024,768]{1,0:T(8,128)(2,1)} %all-gather.11.cloned.1.call-done), channel_id=1, source_target_pairs={{0,2},{2,0},{4,6},{6,4},{8,10},{10,8},{12,14},{14,12},{16,18},{18,... | collective-permute-start | bytes 4718600 | tf_op jit(solution)/shard_map/ppermute | solution.py:101
  146.6 52.1 %collective-permute-start.13 = (bf16[1024,768]{1,0:T(8,128)(2,1)}, bf16[1024,768]{1,0:T(8,128)(2,1)}, u32[]{:S(2)}, u32[]{:S(2)}) collective-permute-start(bf16[1024,768]{1,0:T(8,128)(2,1)} %all-gather.11.cloned.1.call-done), channel_id=1, source_target_pairs={{0,4},{2,6},{4,0},{6,2},{8,12},{10,14},{12,8},{14,10},{16,20},{18,... | collective-permute-start | bytes 4718600 | tf_op jit(solution)/shard_map/ppermute | solution.py:101
  147.4 49.0 %collective-permute-start.15 = (bf16[1024,768]{1,0:T(8,128)(2,1)}, bf16[1024,768]{1,0:T(8,128)(2,1)S(1)}, u32[]{:S(2)}, u32[]{:S(2)}) collective-permute-start(bf16[1024,768]{1,0:T(8,128)(2,1)} %collective-permute-done.10), channel_id=1, source_target_pairs={{0,2},{2,0},{4,6},{6,4},{8,10},{10,8},{12,14},{14,12},{16,18},{18,... | collective-permute-start | bytes 4718600 | tf_op jit(solution)/shard_map/ppermute | solution.py:101
  149.0 47.4 %collective-permute-start.16 = (bf16[384,768]{1,0:T(8,128)(2,1)}, bf16[384,768]{1,0:T(8,128)(2,1)}, u32[]{:S(2)}, u32[]{:S(2)}) collective-permute-start(bf16[384,768]{1,0:T(8,128)(2,1)} %all_gather.23), channel_id=1, source_target_pairs={{0,4},{2,6},{4,0},{6,2},{8,12},{10,14},{12,8},{14,10},{16,20},{18,... | collective-permute-start | bytes 1769480 | tf_op jit(solution)/shard_map/ppermute | solution.py:101
  204.9 91.9 %all-gather.17.cloned.1.call-start = ((), (), s32[]{:S(2)}) async-start(), calls=%async_computation.12 | async-start | bytes 1966080 | tf_op jit(solution)/shard_map/all_gather | solution.py:116
  212.1 41.1 %collective-permute-start.23 = (bf16[384,2048]{1,0:T(8,128)(2,1)S(1)}, bf16[384,2048]{1,0:T(8,128)(2,1)}, u32[]{:S(2)}, u32[]{:S(2)}) collective-permute-start(bf16[384,2048]{1,0:T(8,128)(2,1)S(1)} %bitcast.198), channel_id=1, source_target_pairs={{0,2},{2,0},{4,6},{6,4},{8,10},{10,8},{12,14},{14,12},{16,18},{18,... | collective-permute-start | bytes 4718600 | tf_op jit(solution)/shard_map/ppermute | solution.py:101
  220.3 37.8 %collective-permute-start.22 = (bf16[384,2048]{1,0:T(8,128)(2,1)S(1)}, bf16[384,2048]{1,0:T(8,128)(2,1)}, u32[]{:S(2)}, u32[]{:S(2)}) collective-permute-start(bf16[384,2048]{1,0:T(8,128)(2,1)S(1)} %bitcast.199), channel_id=1, source_target_pairs={{0,4},{2,6},{4,0},{6,2},{8,12},{10,14},{12,8},{14,10},{16,20},{18,... | collective-permute-start | bytes 4718600 | tf_op jit(solution)/shard_map/ppermute | solution.py:101
  258.2 292.1 %reduce-scatter.10.cloned.1.call-start = ((), (), s32[]{:S(2)}) async-start(), calls=%async_computation.14 | async-start | bytes 1966080 | tf_op jit(solution)/shard_map/reduce_scatter | solution.py:207
  429.0 69.2 %collective-permute-start.38 = (bf16[768,2048]{1,0:T(8,128)(2,1)}, bf16[768,2048]{1,0:T(8,128)(2,1)}, u32[]{:S(2)}, u32[]{:S(2)}) collective-permute-start(bf16[768,2048]{1,0:T(8,128)(2,1)} %convolution_convert_fusion.2), channel_id=1, source_target_pairs={{0,2},{2,0},{4,6},{6,4},{8,10},{10,8},{12,14},{14,12},{16,18},{18,... | collective-permute-start | bytes 9437192 | tf_op jit(solution)/shard_map/ppermute | solution.py:101
  465.7 94.7 %reduce-scatter.8.cloned.1.call-start = ((), (), s32[]{:S(2)}) async-start(), calls=%async_computation.13 | async-start | bytes 1966080 | tf_op jit(solution)/shard_map/reduce_scatter | solution.py:207
  523.1 75.3 %reduce-scatter.12.cloned.1.call-start = ((), (), s32[]{:S(2)}) async-start(), calls=%async_computation.15 | async-start | bytes 1966080 | tf_op jit(solution)/shard_map/reduce_scatter | solution.py:207
  565.0 76.0 %reduce-scatter.14.cloned.1.call-start = ((), (), s32[]{:S(2)}) async-start(), calls=%async_computation.16 | async-start | bytes 1720320 | tf_op jit(solution)/shard_map/reduce_scatter | solution.py:207
  602.7 97.8 %reduce-scatter.16.cloned.1.call-start = ((), (), s32[]{:S(2)}) async-start(), calls=%async_computation.17 | async-start | bytes 1966080 | tf_op jit(solution)/shard_map/reduce_scatter | solution.py:207
  657.3 98.1 %reduce-scatter.18.cloned.1.call-start = ((), (), s32[]{:S(2)}) async-start(), calls=%async_computation.18 | async-start | bytes 1966080 | tf_op jit(solution)/shard_map/reduce_scatter | solution.py:207
  657.4 42.0 %collective-permute-start.48 = (bf16[1024,768]{1,0:T(8,128)(2,1)}, bf16[1024,768]{1,0:T(8,128)(2,1)S(1)}, u32[]{:S(2)}, u32[]{:S(2)}) collective-permute-start(bf16[1024,768]{1,0:T(8,128)(2,1)} %add_rows.23), channel_id=1, source_target_pairs={{0,4},{2,6},{4,0},{6,2},{8,12},{10,14},{12,8},{14,10},{16,20},{18,... | collective-permute-start | bytes 4718600 | tf_op jit(solution)/shard_map/ppermute | solution.py:101
  707.9 97.0 %reduce-scatter.20.cloned.1.call-start = ((), (), s32[]{:S(2)}) async-start(), calls=%async_computation.19 | async-start | bytes 2211840 | tf_op jit(solution)/shard_map/reduce_scatter | solution.py:207
  709.2 46.3 %collective-permute-start.53 = (bf16[384,2304]{1,0:T(8,128)(2,1)S(1)}, bf16[384,2304]{1,0:T(8,128)(2,1)S(1)}, u32[]{:S(2)}, u32[]{:S(2)}) collective-permute-start(bf16[384,2304]{1,0:T(8,128)(2,1)S(1)} %copy-done.51), channel_id=1, source_target_pairs={{0,4},{2,6},{4,0},{6,2},{8,12},{10,14},{12,8},{14,10},{16,20},{18,... | collective-permute-start | bytes 5308424 | tf_op jit(solution)/shard_map/ppermute | solution.py:101
  (299 other events, 3509.0 us)
Sparse Core Ops, SparseCore 0:
  10.2 43.0 all-gather.6
  55.4 45.4 all-gather.8
  105.9 35.1 all-gather.10
  144.0 48.5 all-gather.12
  205.0 35.0 all-gather.14
  258.3 35.1 all-gather.16
  465.8 33.1 reduce-scatter.9
  523.3 33.1 reduce-scatter.7
  565.1 33.2 reduce-scatter.11
  602.8 31.3 reduce-scatter.13
  657.4 34.3 reduce-scatter.15
  708.0 38.4 reduce-scatter.17
  765.8 36.6 reduce-scatter.19

commit v4 on v3

--- a/solution.py
+++ b/solution.py
@@ -318,31 +318,43 @@
     in_ref[...] = (res_hat * gains_ref[2:3] * choose(clip, scale_ref[...])).astype(bf16)
 
 
-def leave_rows(clip_ref, res_ref, part_ref, moved_ref, up_ref, tanh_ref, gains_ref, out_ref, grad_ref, sums_ref):
+def leave_rows(clip_ref, part_ref, moved_ref, up_ref, tanh_ref, gains_ref, grad_ref):
+    hat, inverse = rms_parts(add_pair(part_ref, moved_ref))
+    grad_hat = up_ref[...].astype(f32) * choose(clip_ref[...], tanh_ref[...]) * gains_ref[3:4]
+    grad_ref[...] = rms_back(grad_hat, hat, inverse).astype(bf16)
+
+
+def block_rows(clip_ref, res_ref, part_ref, moved_ref, up_ref, tanh_ref, gains_ref, out_ref, sums_ref):
     clip = clip_ref[...]
-    hat, inverse = rms_parts(add_pair(part_ref, moved_ref))
-    upstream = up_ref[...].astype(f32)
-    tanh_tok = choose(clip, tanh_ref[...])
-    out_ref[...] = (res_ref[...] + tanh_tok * hat * gains_ref[3:4]).astype(bf16)
-    grad_ref[...] = rms_back(upstream * tanh_tok * gains_ref[3:4], hat, inverse).astype(bf16)
-    add_clip_sums(clip, upstream * hat, sums_ref)
+    hat, _ = rms_parts(add_pair(part_ref, moved_ref))
+    out_ref[...] = (res_ref[...] + choose(clip, tanh_ref[...]) * hat * gains_ref[3:4]).astype(bf16)
+    add_clip_sums(clip, up_ref[...].astype(f32) * hat, sums_ref)
 
 
 def middle_rows(
     clip_ref, res_ref, grad_part_ref, grad_moved_ref, up_ref, part_ref, moved_ref, tanh_ref,
-    scale_ref, gains_ref, grad_res_ref, grad_attn_ref, res_sums_ref, attn_sums_ref,
+    scale_ref, gains_ref, grad_res_ref, grad_attn_ref,
 ):
     clip = clip_ref[...]
-    grad = add_pair(grad_part_ref, grad_moved_ref)
     hat, inverse = rms_parts(res_ref[...])
-    add_clip_sums(clip, grad * hat, res_sums_ref)
-    grad_hat = grad * gains_ref[2:3] * choose(clip, scale_ref[...])
+    grad_hat = add_pair(grad_part_ref, grad_moved_ref) * gains_ref[2:3]
+    grad_hat = grad_hat * choose(clip, scale_ref[...])
     grad_res = up_ref[...].astype(f32) + rms_back(grad_hat, hat, inverse)
     grad_res_ref[...] = grad_res
     hat, inverse = rms_parts(add_pair(part_ref, moved_ref))
-    add_clip_sums(clip, grad_res * hat, attn_sums_ref)
     grad_hat = grad_res * gains_ref[1:2] * choose(clip, tanh_ref[...])
     grad_attn_ref[...] = rms_back(grad_hat, hat, inverse).astype(bf16)
+
+
+def sum_rows(
+    clip_ref, res_ref, grad_part_ref, grad_moved_ref, grad_res_ref, part_ref, moved_ref, _,
+    res_sums_ref, attn_sums_ref,
+):
+    clip = clip_ref[...]
+    hat, _ = rms_parts(res_ref[...])
+    add_clip_sums(clip, add_pair(grad_part_ref, grad_moved_ref) * hat, res_sums_ref)
+    hat, _ = rms_parts(add_pair(part_ref, moved_ref))
+    add_clip_sums(clip, grad_res_ref[...] * hat, attn_sums_ref)
 
 
 def last_rows(
@@ -747,32 +759,35 @@
     up_core, gate_value = fence(up_core, gate_value)
     up_own, up_other = stack([up_near] + up_y), stack(up_near_core + up_core)
     up_value = dot(ffn_in_bf[:, :half_width], up_own) + dot(ffn_in_bf[:, half_width:], up_other)
-    sigmoid_gate = jax.nn.sigmoid(gate_value)
-    silu_gate = gate_value * sigmoid_gate
-    inner_bf = (silu_gate * up_value).astype(bf16)
+    inner_bf = (gate_value * jax.nn.sigmoid(gate_value) * up_value).astype(bf16)
     inner_bf, down_y, down_near_core = fence(inner_bf, down_y, down_near_core)
 
     down_core = send_core(grid, down_y)
-    upstream = dot(cotangent, one_hot).astype(bf16)
-    down_core, inner_bf, upstream = fence(down_core, inner_bf, upstream)
+    down_core, inner_bf, cotangent = fence(down_core, inner_bf, cotangent)
     down_own, down_other = stack([down_near] + down_y), stack(down_near_core + down_core)
     ffn_part = rounded(
         jnp.concatenate(
             [contract_cols(inner_bf, down_own), contract_cols(inner_bf, down_other)], axis=1
         )
     ).astype(bf16)
-    (ffn_part,) = fence(ffn_part)
+    ffn_part, gate_value, cotangent = fence(ffn_part, gate_value, cotangent)
 
     ffn_moved = swap_txt(ffn_part)
-    ffn_moved, ffn_part = fence(ffn_moved, ffn_part)
-
-    block_out, grad_ffn_out, ffn_sums = row_call(
+    upstream = dot(cotangent, one_hot).astype(bf16)
+    sigmoid_gate = jax.nn.sigmoid(gate_value)
+    silu_gate = gate_value * sigmoid_gate
+    gate_slope = up_value * (sigmoid_gate * (1.0 + gate_value * (1.0 - sigmoid_gate)))
+    ffn_moved, ffn_part, upstream, silu_gate, gate_slope = fence(
+        ffn_moved, ffn_part, upstream, silu_gate, gate_slope
+    )
+
+    (grad_ffn_out,) = row_call(
         leave_rows,
         "leave_rows",
-        [clip_column, residual, ffn_part, ffn_moved, upstream],
+        [clip_column, ffn_part, ffn_moved, upstream],
         [own_tanhs[1], gains],
-        [bf16, bf16],
-        1,
+        [bf16],
+        0,
     )
     down_kept = contract_rows(grad_ffn_out[:, :half_width], inner_bf).astype(bf16)
     down_away = contract_rows(grad_ffn_out[:, half_width:], inner_bf).astype(bf16)
@@ -782,8 +797,7 @@
     grad_inner = dot(grad_ffn_out[:, :half_width], down_own) + dot(
         grad_ffn_out[:, half_width:], down_other
     )
-    silu_slope = sigmoid_gate * (1.0 + gate_value * (1.0 - sigmoid_gate))
-    grad_gate_bf = (grad_inner * up_value * silu_slope).astype(bf16)
+    grad_gate_bf = (grad_inner * gate_slope).astype(bf16)
     grad_up_bf = (grad_inner * silu_gate).astype(bf16)
     ffn_in_part = rounded(
         jnp.concatenate(
@@ -806,6 +820,14 @@
     gate_kept = contract_rows(ffn_in_bf[:, :half_width], grad_gate_bf).astype(bf16)
     up_kept = contract_rows(ffn_in_bf[:, :half_width], grad_up_bf).astype(bf16)
     up_away = contract_rows(ffn_in_bf[:, half_width:], grad_up_bf).astype(bf16)
+    block_out, ffn_sums = row_call(
+        block_rows,
+        "block_rows",
+        [clip_column, residual, ffn_part, ffn_moved, upstream],
+        [own_tanhs[1], gains],
+        [bf16],
+        1,
+    )
     block_out = contract_cols(block_out, one_hot).astype(bf16)
     gate_away = core_away(grid, gate_kept, gate_core)
     block_out, ffn_in_moved, down_moved, up_kept, gate_kept, gate_away = fence(
@@ -817,13 +839,13 @@
     up_core = grid.send(up_away, core=1)
     ffn_in_moved, down_total = fence(ffn_in_moved, down_total)
     down_sum = sum_outer(grid, down_total)
-    grad_residual, grad_attn_bf, res_sums, attn_sums = row_call(
+    grad_residual, grad_attn_bf = row_call(
         middle_rows,
         "middle_rows",
         [clip_column, residual, ffn_in_part, ffn_in_moved, upstream, attn_part, attn_moved],
         [own_tanhs[0], own_scales[1], gains],
         [f32, bf16],
-        2,
+        0,
     )
     grad_combined = dot(grad_attn_bf[:, :half_width], out_own) + dot(
         grad_attn_bf[:, half_width:], out_other
@@ -927,13 +949,21 @@
         norm_heads_back, "norm_queries_back", projected, 0, query_gain, turns,
         (grad_query, jnp.concatenate([grad_long_q, grad_short_q], axis=0)),
     )
+    res_sums, attn_sums = row_call(
+        sum_rows,
+        "sum_rows",
+        [clip_column, residual, ffn_in_part, ffn_in_moved, grad_residual, attn_part, attn_moved],
+        [own_tanhs[0]],
+        [],
+        2,
+    )
     tval_away = core_away(grid, tval_kept, tval_core)
     (
         both_sum, tkey_moved, tval_core, tval_away, null_moved, grad_query_raw, grad_short_k,
-        grad_short_v, query_gain_grad,
+        grad_short_v, query_gain_grad, res_sums, attn_sums,
     ) = fence(
         both_sum, tkey_moved, tval_core, tval_away, null_moved, grad_query_raw, grad_short_k,
-        grad_short_v, query_gain_grad,
+        grad_short_v, query_gain_grad, res_sums, attn_sums,
     )
 
     tval_moved = swap_inner(grid, tval_away)

time: 846 us -> 821 us (0.970)
  waiting for transfers between devices: 274 us -> 245 us
    ppermute x9, waiting for transfers between devices: 73.4 us -> 41.5 us  [swap_txt(): return lax.ppermute(values, 'txt', [(0, 1), (1, 0)])]
    pallas_call x4 -> x6, Pallas kernels: 30.4 us -> 36.3 us  [row_call(): pl.pallas_call(body, grid=(4,), in_specs=[by_rows(array) for array in arr...]
    unnamed x500 -> x450, local copies, waits for them, and re-layouts: 71.4 us -> 69.1 us
  transfers between devices with their start and end apart: 80 -> 80, of which waited for: 31 -> 32; matrix products, arithmetic and copies ran while one was open for 25% -> 25% of each run, Pallas kernels for 18% -> 19%
where the time goes in v4:
time: 821 us; the launch traced here: 810 us
  waiting for transfers between devices  245 us (30%)
  Pallas kernels  182 us (22%)
  matrix products  132 us (16%)
  local copies, waits for them, and re-layouts  109 us (13%)
  starting transfers between devices  57.5 us (7%)
  other arithmetic  42.5 us (5%)
  blocking collectives  23.9 us (3%)
  between operations  18.5 us (2%)
    ppermute x50, waiting for transfers between devices, send(): return lax.ppermute(values, 'seq', pairs)  137 us
    unnamed x450, local copies, waits for them, and re-layouts  69.1 us
    pallas_call x6, Pallas kernels, attend_call(): pl.pallas_call(attend_heads_back if back else attend_heads, grid=(width /...  68 us
    dot_general x22, matrix products, contract_cols(): lax.dot_general(left_side, right_side, (((1,), (1,)), ((), ())), preferre...  47.1 us
    ppermute x8, waiting for transfers between devices, pair_sum(): return lax.ppermute(values, 'seq', pairs)  45.9 us
    dot_general x24, matrix products, dot(): return jnp.dot(left_side, right_side, preferred_element_type=f32)  43.8 us
    pallas_call x14, Pallas kernels, add_rows(): pl.pallas_call(add_blocks, grid=(rows // block,), in_specs=[from_row(star...  43.7 us
    ppermute x9, waiting for transfers between devices, swap_txt(): return lax.ppermute(values, 'txt', [(0, 1), (1, 0)])  41.5 us
  transfers between devices with their start and end apart: 80, of which 32 were waited for; matrix products, arithmetic and copies ran while one was open for 25% of the time, Pallas kernels for 19%

profile of v4, /device:TPU:0, one launch (start us, length us, event | category | flops | bytes accessed | tf_op | source)
XLA Modules:
  0.0 809.7 jit_solution(729396826588368249)
XLA Ops:
  40.1 13.2 %all-gather.7.cloned.1.call-done = bf16[384,2304]{1,0:T(8,128)(2,1)} async-done(((bf16[96,2304]{1,0:T(8,128)(2,1)}), bf16[384,2304]{1,0:T(8,128)(2,1)}) %all-gather.7.cloned.1.call-update) | async-done | bytes 1769488 | tf_op jit(solution)/shard_map/all_gather | solution.py:116
  60.8 23.9 %all_gather.23 = bf16[384,768]{1,0:T(8,128)(2,1)} all-gather(bf16[96,768]{1,0:T(8,128)(2,1)} %param.32), channel_id=1, replica_groups={{0,8,16,24},{2,10,18,26},{4,12,20,28},{6,14,22,30},{1,9,17,25},{3,11,19..., dimensions={0}, use_global_device_ids=true | all-gather | bytes 737280 | tf_op jit(solution)/shard_map/all_gather | solution.py:116
  87.9 6.0 collective-permute-done.8
  93.9 7.0 all-gather.9.cloned.1.call-done
  128.1 13.7 %collective-permute-done.10 = bf16[1024,768]{1,0:T(8,128)(2,1)} collective-permute-done((bf16[1024,768]{1,0:T(8,128)(2,1)}, bf16[1024,768]{1,0:T(8,128)(2,1)}, u32[]{:S(2)}, u32[]{:S(2)}) %collective-permute-start.10) | collective-permute-done | bytes 1572896 | tf_op jit(solution)/shard_map/ppermute | solution.py:101
  152.1 11.6 %attend_short.1 = (f32[448,768]{1,0:T(8,128)S(1)}, f32[448,768]{1,0:T(8,128)S(1)}) custom-call(s32[448,1]{1,0:T(8,128)S(1)} %copy.186.clip_ref, s32[1,448]{1,0:T(1,128)S(1)} %bitcast.182, bf16[448,768]{1,0:T(8,128)(2,1)S(1)} %slice.301.query_ref, bf16[448,768]{1,0:T(8,128)(2,1)S(1)} %slice.302.key_ref, bf16[448,768]{1,0:T(8,128)(2,1)S(1)} %slice.303.value_ref), custom_call_target="tpu_custom_call" | custom-call | flops 1 | bytes 1 | tf_op jit(solution)/shard_map/attend_short/pallas_call | solution.py:516
  168.5 27.8 %collective-permute-done.16 = bf16[384,768]{1,0:T(8,128)(2,1)} collective-permute-done((bf16[384,768]{1,0:T(8,128)(2,1)}, bf16[384,768]{1,0:T(8,128)(2,1)}, u32[]{:S(2)}, u32[]{:S(2)}) %collective-permute-start.16) | collective-permute-done | bytes 589856 | tf_op jit(solution)/shard_map/ppermute | solution.py:101
  228.5 12.0 %attend_cross.1 = (f32[512,768]{1,0:T(8,128)S(1)}, f32[512,768]{1,0:T(8,128)S(1)}) custom-call(s32[512,1]{1,0:T(8,128)S(1)} %copy.192.clip_ref, s32[1,256]{1,0:T(1,128)S(1)} %compare_select_fusion.key_clip_ref, bf16[512,768]{1,0:T(8,128)(2,1)S(1)} %copy-done.18, bf16[256,768]{1,0:T(8,128)(2,1)S(1)} %norm_text.1.key_ref, bf16[256,768]{1,0:T(8,128)(2,1)S(1)} %fusion.37.value_ref), custom_call_target="tpu_custom_call" | custom-call | flops 1 | bytes 1 | tf_op jit(solution)/shard_map/attend_cross/pallas_call | solution.py:516
  241.8 7.2 attend_long.1
  270.4 25.1 %collective-permute-done.25 = bf16[384,2048]{1,0:T(8,128)(2,1)} collective-permute-done((bf16[384,2048]{1,0:T(8,128)(2,1)}, bf16[384,2048]{1,0:T(8,128)(2,1)}, u32[]{:S(2)}, u32[]{:S(2)}) %collective-permute-start.25) | collective-permute-done | bytes 1572896 | tf_op jit(solution)/shard_map/ppermute | solution.py:101
  324.9 8.2 %collective-permute-done.29 = bf16[384,2048]{1,0:T(8,128)(2,1)S(1)} collective-permute-done((bf16[384,2048]{1,0:T(8,128)(2,1)}, bf16[384,2048]{1,0:T(8,128)(2,1)S(1)}, u32[]{:S(2)}, u32[]{:S(2)}) %collective-permute-start.29) | collective-permute-done | bytes 1572896 | tf_op jit(solution)/shard_map/ppermute | solution.py:101
  352.1 26.8 %collective-permute-done.32.moved_ref = bf16[512,1536]{1,0:T(8,128)(2,1)S(1)} collective-permute-done((bf16[512,1536]{1,0:T(8,128)(2,1)S(1)}, bf16[512,1536]{1,0:T(8,128)(2,1)S(1)}, u32[]{:S(2)}, u32[]{:S(2)}) %collective-permute-start.32) | collective-permute-done | bytes 1572896 | tf_op jit(solution)/shard_map/ppermute | solution.py:73
  439.1 13.8 %collective-permute-done.35.refs_2_ = bf16[384,2048]{1,0:T(8,128)(2,1)S(1)} collective-permute-done((bf16[384,2048]{1,0:T(8,128)(2,1)S(1)}, bf16[384,2048]{1,0:T(8,128)(2,1)S(1)}, u32[]{:S(2)}, u32[]{:S(2)}) %collective-permute-start.35) | collective-permute-done | bytes 1572896 | tf_op jit(solution)/shard_map/ppermute | solution.py:101
  462.7 8.1 %middle_rows.1 = (f32[512,1536]{1,0:T(8,128)}, bf16[512,1536]{1,0:T(8,128)(2,1)S(1)}) custom-call(s32[512,1]{1,0:T(8,128)S(1)} %copy.192.clip_ref, f32[512,1536]{1,0:T(8,128)} %get-tuple-element.246.res_ref, bf16[512,1536]{1,0:T(8,128)(2,1)S(1)} %fusion.22.grad_part_ref, bf16[512,1536]{1,0:T(8,128)(2,1)S(1)} %copy-done.33, bf16[512,1536]{1,0:T(8,128)(2,1)} %fusion.25.up_ref, ...), custom_call_target="tpu_custom_call" | custom-call | flops 1 | bytes 1 | tf_op jit(solution)/shard_map/middle_rows/pallas_call | solution.py:387
  475.0 9.8 %attend_long_back.1 = (f32[64,768]{1,0:T(8,128)S(1)}, bf16[1024,768]{1,0:T(8,128)(2,1)S(1)}, bf16[1024,768]{1,0:T(8,128)(2,1)S(1)}) custom-call(s32[64,1]{1,0:T(8,128)S(1)} %copy-done.82, s32[1,1024]{1,0:T(1,128)S(1)} %broadcast_in_dim.215.key_clip_ref, bf16[64,768]{1,0:T(8,128)(2,1)S(1)} %copy-done.72, bf16[1024,1536]{1,0:T(8,128)(2,1)} %copy-done.3, ...), custom_call_target="tpu_custom_call" | custom-call | flops 1 | bytes 1 | tf_op jit(solution)/shard_map/attend_long_back/pallas_call | solution.py:516
  502.8 10.8 %attend_cross_back.1 = (f32[512,768]{1,0:T(8,128)S(1)}, f32[256,768]{1,0:T(8,128)S(1)}, f32[256,768]{1,0:T(8,128)S(1)}) custom-call(s32[512,1]{1,0:T(8,128)S(1)} %copy.192.clip_ref, s32[1,256]{1,0:T(1,128)S(1)} %compare_select_fusion.key_clip_ref, bf16[512,768]{1,0:T(8,128)(2,1)S(1)} %copy-done.19, bf16[256,768]{1,0:T(8,128)(2,1)S(1)} %copy-done.49, ...), custom_call_target="tpu_custom_call" | custom-call | flops 1 | bytes 1 | tf_op jit(solution)/shard_map/attend_cross_back/pallas_call | solution.py:516
  526.7 9.7 %collective-permute-done.39.refs_2_ = bf16[384,2048]{1,0:T(8,128)(2,1)} collective-permute-done((bf16[384,2048]{1,0:T(8,128)(2,1)}, bf16[384,2048]{1,0:T(8,128)(2,1)}, u32[]{:S(2)}, u32[]{:S(2)}) %collective-permute-start.39) | collective-permute-done | bytes 1572896 | tf_op jit(solution)/shard_map/ppermute | solution.py:101
  548.1 16.7 %attend_short_back.1 = (f32[448,768]{1,0:T(8,128)S(1)}, f32[448,768]{1,0:T(8,128)S(1)}, f32[448,768]{1,0:T(8,128)}) custom-call(s32[448,1]{1,0:T(8,128)S(1)} %copy-done.51, s32[1,448]{1,0:T(1,128)S(1)} %bitcast.183, bf16[448,768]{1,0:T(8,128)(2,1)S(1)} %copy-done.41, bf16[448,768]{1,0:T(8,128)(2,1)S(1)} %copy-done.37, bf16[448,768]{1,0:T(8,128)(2,1)S(1)} %copy-done.39, ...), custom_call_target="tpu_custom_call" | custom-call | flops 1 | bytes 1 | tf_op jit(solution)/shard_map/attend_short_back/pallas_call | solution.py:516
  585.2 6.6 sum_rows.1
  603.6 12.6 %collective-permute-done.45.refs_2_ = bf16[1024,768]{1,0:T(8,128)(2,1)S(1)} collective-permute-done((bf16[1024,768]{1,0:T(8,128)(2,1)}, bf16[1024,768]{1,0:T(8,128)(2,1)S(1)}, u32[]{:S(2)}, u32[]{:S(2)}) %collective-permute-start.45) | collective-permute-done | bytes 1572896 | tf_op jit(solution)/shard_map/ppermute | solution.py:101
  651.4 23.9 %collective-permute-done.49 = bf16[64,1536]{1,0:T(8,128)(2,1)S(1)} collective-permute-done((bf16[64,1536]{1,0:T(8,128)(2,1)S(1)}, bf16[64,1536]{1,0:T(8,128)(2,1)S(1)}, u32[]{:S(2)}, u32[]{:S(2)}) %collective-permute-start.49) | collective-permute-done | bytes 196640 | tf_op jit(solution)/shard_map/ppermute | solution.py:214
  695.8 9.2 %collective-permute-done.52 = bf16[256,1536]{1,0:T(8,128)(2,1)S(1)} collective-permute-done((bf16[256,1536]{1,0:T(8,128)(2,1)S(1)}, bf16[256,1536]{1,0:T(8,128)(2,1)S(1)}, u32[]{:S(2)}, u32[]{:S(2)}) %collective-permute-start.52) | collective-permute-done | bytes 786464 | tf_op jit(solution)/shard_map/ppermute | solution.py:73
  707.4 6.4 last_rows.1
  719.7 8.3 %collective-permute-done.55 = bf16[64,1536]{1,0:T(8,128)(2,1)S(1)} collective-permute-done((bf16[64,1536]{1,0:T(8,128)(2,1)S(1)}, bf16[64,1536]{1,0:T(8,128)(2,1)S(1)}, u32[]{:S(2)}, u32[]{:S(2)}) %collective-permute-start.55) | collective-permute-done | bytes 196640 | tf_op jit(solution)/shard_map/ppermute | solution.py:214
  (908 shorter events, 473.1 us)
Async XLA Ops:
  7.2 46.0 %all-gather.7.cloned.1.call-start = ((), (), s32[]{:S(2)}) async-start(), calls=%async_computation.7 | async-start | bytes 2211840 | tf_op jit(solution)/shard_map/all_gather | solution.py:116
  9.3 91.6 %all-gather.9.cloned.1.call-start = ((), (), s32[]{:S(2)}) async-start(), calls=%async_computation.8 | async-start | bytes 1966080 | tf_op jit(solution)/shard_map/all_gather | solution.py:116
  53.3 40.7 %collective-permute-start.8 = (bf16[384,2304]{1,0:T(8,128)(2,1)}, bf16[384,2304]{1,0:T(8,128)(2,1)}, u32[]{:S(2)}, u32[]{:S(2)}) collective-permute-start(bf16[384,2304]{1,0:T(8,128)(2,1)} %all-gather.7.cloned.1.call-done), channel_id=1, source_target_pairs={{0,4},{2,6},{4,0},{6,2},{8,12},{10,14},{12,8},{14,10},{16,20},{18,... | collective-permute-start | bytes 5308424 | tf_op jit(solution)/shard_map/ppermute | solution.py:101
  54.7 39.2 %collective-permute-start.7 = (bf16[384,2304]{1,0:T(8,128)(2,1)}, bf16[384,2304]{1,0:T(8,128)(2,1)}, u32[]{:S(2)}, u32[]{:S(2)}) collective-permute-start(bf16[384,2304]{1,0:T(8,128)(2,1)} %all-gather.7.cloned.1.call-done), channel_id=1, source_target_pairs={{0,2},{2,0},{4,6},{6,4},{8,10},{10,8},{12,14},{14,12},{16,18},{18,... | collective-permute-start | bytes 5308424 | tf_op jit(solution)/shard_map/ppermute | solution.py:101
  55.1 86.7 %all-gather.11.cloned.1.call-start = ((), (), s32[]{:S(2)}) async-start(), calls=%async_computation.9 | async-start | bytes 1966080 | tf_op jit(solution)/shard_map/all_gather | solution.py:116
  105.7 92.9 %all-gather.13.cloned.1.call-start = ((), (), s32[]{:S(2)}) async-start(), calls=%async_computation.10 | async-start | bytes 2949120 | tf_op jit(solution)/shard_map/all_gather | solution.py:116
  143.8 114.2 %all-gather.15.cloned.1.call-start = ((), (), s32[]{:S(2)}) async-start(), calls=%async_computation.11 | async-start | bytes 1966080 | tf_op jit(solution)/shard_map/all_gather | solution.py:116
  146.5 51.0 %collective-permute-start.14 = (bf16[1024,768]{1,0:T(8,128)(2,1)}, bf16[1024,768]{1,0:T(8,128)(2,1)S(1)}, u32[]{:S(2)}, u32[]{:S(2)}) collective-permute-start(bf16[1024,768]{1,0:T(8,128)(2,1)} %all-gather.11.cloned.1.call-done), channel_id=1, source_target_pairs={{0,2},{2,0},{4,6},{6,4},{8,10},{10,8},{12,14},{14,12},{16,18},{18,... | collective-permute-start | bytes 4718600 | tf_op jit(solution)/shard_map/ppermute | solution.py:101
  146.5 52.1 %collective-permute-start.13 = (bf16[1024,768]{1,0:T(8,128)(2,1)}, bf16[1024,768]{1,0:T(8,128)(2,1)}, u32[]{:S(2)}, u32[]{:S(2)}) collective-permute-start(bf16[1024,768]{1,0:T(8,128)(2,1)} %all-gather.11.cloned.1.call-done), channel_id=1, source_target_pairs={{0,4},{2,6},{4,0},{6,2},{8,12},{10,14},{12,8},{14,10},{16,20},{18,... | collective-permute-start | bytes 4718600 | tf_op jit(solution)/shard_map/ppermute | solution.py:101
  147.3 49.0 %collective-permute-start.15 = (bf16[1024,768]{1,0:T(8,128)(2,1)}, bf16[1024,768]{1,0:T(8,128)(2,1)S(1)}, u32[]{:S(2)}, u32[]{:S(2)}) collective-permute-start(bf16[1024,768]{1,0:T(8,128)(2,1)} %collective-permute-done.10), channel_id=1, source_target_pairs={{0,2},{2,0},{4,6},{6,4},{8,10},{10,8},{12,14},{14,12},{16,18},{18,... | collective-permute-start | bytes 4718600 | tf_op jit(solution)/shard_map/ppermute | solution.py:101
  148.9 47.4 %collective-permute-start.16 = (bf16[384,768]{1,0:T(8,128)(2,1)}, bf16[384,768]{1,0:T(8,128)(2,1)}, u32[]{:S(2)}, u32[]{:S(2)}) collective-permute-start(bf16[384,768]{1,0:T(8,128)(2,1)} %all_gather.23), channel_id=1, source_target_pairs={{0,4},{2,6},{4,0},{6,2},{8,12},{10,14},{12,8},{14,10},{16,20},{18,... | collective-permute-start | bytes 1769480 | tf_op jit(solution)/shard_map/ppermute | solution.py:101
  204.8 91.3 %all-gather.17.cloned.1.call-start = ((), (), s32[]{:S(2)}) async-start(), calls=%async_computation.12 | async-start | bytes 1966080 | tf_op jit(solution)/shard_map/all_gather | solution.py:116
  212.0 41.0 %collective-permute-start.23 = (bf16[384,2048]{1,0:T(8,128)(2,1)S(1)}, bf16[384,2048]{1,0:T(8,128)(2,1)}, u32[]{:S(2)}, u32[]{:S(2)}) collective-permute-start(bf16[384,2048]{1,0:T(8,128)(2,1)S(1)} %bitcast.196), channel_id=1, source_target_pairs={{0,2},{2,0},{4,6},{6,4},{8,10},{10,8},{12,14},{14,12},{16,18},{18,... | collective-permute-start | bytes 4718600 | tf_op jit(solution)/shard_map/ppermute | solution.py:101
  220.2 37.8 %collective-permute-start.22 = (bf16[384,2048]{1,0:T(8,128)(2,1)S(1)}, bf16[384,2048]{1,0:T(8,128)(2,1)}, u32[]{:S(2)}, u32[]{:S(2)}) collective-permute-start(bf16[384,2048]{1,0:T(8,128)(2,1)S(1)} %bitcast.197), channel_id=1, source_target_pairs={{0,4},{2,6},{4,0},{6,2},{8,12},{10,14},{12,8},{14,10},{16,20},{18,... | collective-permute-start | bytes 4718600 | tf_op jit(solution)/shard_map/ppermute | solution.py:101
  258.1 268.6 %reduce-scatter.10.cloned.1.call-start = ((), (), s32[]{:S(2)}) async-start(), calls=%async_computation.14 | async-start | bytes 1966080 | tf_op jit(solution)/shard_map/reduce_scatter | solution.py:207
  421.7 63.2 %collective-permute-start.38 = (bf16[768,2048]{1,0:T(8,128)(2,1)}, bf16[768,2048]{1,0:T(8,128)(2,1)}, u32[]{:S(2)}, u32[]{:S(2)}) collective-permute-start(bf16[768,2048]{1,0:T(8,128)(2,1)} %convolution_convert_fusion.2), channel_id=1, source_target_pairs={{0,2},{2,0},{4,6},{6,4},{8,10},{10,8},{12,14},{14,12},{16,18},{18,... | collective-permute-start | bytes 9437192 | tf_op jit(solution)/shard_map/ppermute | solution.py:101
  459.1 77.3 %reduce-scatter.8.cloned.1.call-start = ((), (), s32[]{:S(2)}) async-start(), calls=%async_computation.13 | async-start | bytes 1966080 | tf_op jit(solution)/shard_map/reduce_scatter | solution.py:207
  499.2 75.6 %reduce-scatter.12.cloned.1.call-start = ((), (), s32[]{:S(2)}) async-start(), calls=%async_computation.15 | async-start | bytes 1966080 | tf_op jit(solution)/shard_map/reduce_scatter | solution.py:207
  541.1 76.2 %reduce-scatter.14.cloned.1.call-start = ((), (), s32[]{:S(2)}) async-start(), calls=%async_computation.16 | async-start | bytes 1720320 | tf_op jit(solution)/shard_map/reduce_scatter | solution.py:207
  579.0 98.1 %reduce-scatter.16.cloned.1.call-start = ((), (), s32[]{:S(2)}) async-start(), calls=%async_computation.17 | async-start | bytes 1966080 | tf_op jit(solution)/shard_map/reduce_scatter | solution.py:207
  633.7 95.6 %reduce-scatter.18.cloned.1.call-start = ((), (), s32[]{:S(2)}) async-start(), calls=%async_computation.18 | async-start | bytes 1966080 | tf_op jit(solution)/shard_map/reduce_scatter | solution.py:207
  633.9 41.3 %collective-permute-start.48 = (bf16[1024,768]{1,0:T(8,128)(2,1)}, bf16[1024,768]{1,0:T(8,128)(2,1)S(1)}, u32[]{:S(2)}, u32[]{:S(2)}) collective-permute-start(bf16[1024,768]{1,0:T(8,128)(2,1)} %add_rows.23), channel_id=1, source_target_pairs={{0,4},{2,6},{4,0},{6,2},{8,12},{10,14},{12,8},{14,10},{16,20},{18,... | collective-permute-start | bytes 4718600 | tf_op jit(solution)/shard_map/ppermute | solution.py:101
  683.8 96.6 %reduce-scatter.20.cloned.1.call-start = ((), (), s32[]{:S(2)}) async-start(), calls=%async_computation.19 | async-start | bytes 2211840 | tf_op jit(solution)/shard_map/reduce_scatter | solution.py:207
  684.1 43.9 %collective-permute-start.53 = (bf16[384,2304]{1,0:T(8,128)(2,1)S(1)}, bf16[384,2304]{1,0:T(8,128)(2,1)S(1)}, u32[]{:S(2)}, u32[]{:S(2)}) collective-permute-start(bf16[384,2304]{1,0:T(8,128)(2,1)S(1)} %add_rows.25), channel_id=1, source_target_pairs={{0,4},{2,6},{4,0},{6,2},{8,12},{10,14},{12,8},{14,10},{16,20},{18,... | collective-permute-start | bytes 5308424 | tf_op jit(solution)/shard_map/ppermute | solution.py:101
  (274 other events, 2991.4 us)
Sparse Core Ops, SparseCore 0:
  10.2 43.0 all-gather.6
  55.4 45.4 all-gather.8
  105.8 35.1 all-gather.10
  144.0 48.5 all-gather.12
  204.9 35.0 all-gather.14
  258.2 35.1 all-gather.16
  459.3 33.3 reduce-scatter.9
  499.3 33.3 reduce-scatter.7
  541.2 33.4 reduce-scatter.11
  579.1 31.3 reduce-scatter.13
  633.8 34.4 reduce-scatter.15
  683.9 42.4 reduce-scatter.17
  740.9 36.5 reduce-scatter.19

commit v5 on v4

--- a/solution.py
+++ b/solution.py
@@ -968,7 +968,7 @@
 
     tval_moved = swap_inner(grid, tval_away)
     null_rows = null_rows + null_moved
-    null_moved = pair_sum(grid, null_rows, 2)
+    null_moved = pair_sum(grid, null_rows, 4)
     out_grad = both_sum[2 * LONG_DEV :].astype(f32)
     tkey_total = inner_total(grid, tkey_kept, tkey_core, tkey_moved)
     both_sum, tkey_total = fence(both_sum, tkey_total)
@@ -1007,7 +1007,6 @@
         tval_total, null_rows, moved_first, grad_residual
     )
     tval_sum = sum_outer(grid, tval_total)
-    null_rows = null_rows + pair_sum(grid, null_rows, 4)
     null_moved = pair_sum(grid, null_rows, 8)
     normed_moved = jnp.concatenate([moved_first, moved_last], axis=0)
     video_high, video_low, hidden_sums = row_call(
@@ -1061,7 +1060,8 @@
         keepdims=False,
     )
     mod_blocks = turn_seq(grid, jnp.transpose(mod_blocks, (1, 0, 2)))
-    null_rows = sum_seq(grid, null_rows + null_moved, 16)
+    null_rows = null_rows + null_moved
+    null_rows = sum_seq(grid, null_rows + pair_sum(grid, null_rows, 2), 16)
     null_part = jnp.concatenate(
         [
             contract_cols(null_rows[:, :own_width], key_piece)

time: 821 us -> 821 us (level)
    ppermute x50, waiting for transfers between devices: 137 us -> 150 us  [send(): return lax.ppermute(values, 'seq', pairs)]
    ppermute x8, waiting for transfers between devices: 45.9 us -> 33.7 us  [pair_sum(): return lax.ppermute(values, 'seq', pairs)]
    unnamed x450 -> x454, local copies, waits for them, and re-layouts: 69.1 us -> 68.1 us
  transfers between devices with their start and end apart: 80 -> 80, of which waited for: 32 -> 37; matrix products, arithmetic and copies ran while one was open for 25% -> 25% of each run, Pallas kernels for 19% -> 19%
where the time goes in v5:
time: 821 us; the launch traced here: 810 us
  waiting for transfers between devices  247 us (30%)
  Pallas kernels  182 us (22%)
  matrix products  131 us (16%)
  local copies, waits for them, and re-layouts  108 us (13%)
  starting transfers between devices  57.3 us (7%)
  other arithmetic  42.1 us (5%)
  blocking collectives  23.9 us (3%)
  between operations  18.4 us (2%)
    ppermute x50, waiting for transfers between devices, send(): return lax.ppermute(values, 'seq', pairs)  150 us
    unnamed x454, local copies, waits for them, and re-layouts  68.1 us
    pallas_call x6, Pallas kernels, attend_call(): pl.pallas_call(attend_heads_back if back else attend_heads, grid=(width /...  68 us
    dot_general x22, matrix products, contract_cols(): lax.dot_general(left_side, right_side, (((1,), (1,)), ((), ())), preferre...  47 us
    pallas_call x14, Pallas kernels, add_rows(): pl.pallas_call(add_blocks, grid=(rows // block,), in_specs=[from_row(star...  44.1 us
    dot_general x24, matrix products, dot(): return jnp.dot(left_side, right_side, preferred_element_type=f32)  43.7 us
    ppermute x9, waiting for transfers between devices, swap_txt(): return lax.ppermute(values, 'txt', [(0, 1), (1, 0)])  41.9 us
    dot_general x14, matrix products, contract_rows(): lax.dot_general(left_side, right_side, (((0,), (0,)), ((), ())), preferre...  38.1 us
  transfers between devices with their start and end apart: 80, of which 37 were waited for; matrix products, arithmetic and copies ran while one was open for 25% of the time, Pallas kernels for 19%

profile of v5, /device:TPU:0, one launch (start us, length us, event | category | flops | bytes accessed | tf_op | source)
XLA Modules:
  0.0 809.7 jit_solution(5215740947978089587)
XLA Ops:
  40.1 13.1 %all-gather.7.cloned.1.call-done = bf16[384,2304]{1,0:T(8,128)(2,1)} async-done(((bf16[96,2304]{1,0:T(8,128)(2,1)}), bf16[384,2304]{1,0:T(8,128)(2,1)}) %all-gather.7.cloned.1.call-update) | async-done | bytes 1769488 | tf_op jit(solution)/shard_map/all_gather | solution.py:116
  60.9 23.9 %all_gather.23 = bf16[384,768]{1,0:T(8,128)(2,1)} all-gather(bf16[96,768]{1,0:T(8,128)(2,1)} %param.32), channel_id=1, replica_groups={{0,8,16,24},{2,10,18,26},{4,12,20,28},{6,14,22,30},{1,9,17,25},{3,11,19..., dimensions={0}, use_global_device_ids=true | all-gather | bytes 737280 | tf_op jit(solution)/shard_map/all_gather | solution.py:116
  93.9 7.0 all-gather.9.cloned.1.call-done
  128.2 13.7 %collective-permute-done.10 = bf16[1024,768]{1,0:T(8,128)(2,1)} collective-permute-done((bf16[1024,768]{1,0:T(8,128)(2,1)}, bf16[1024,768]{1,0:T(8,128)(2,1)}, u32[]{:S(2)}, u32[]{:S(2)}) %collective-permute-start.10) | collective-permute-done | bytes 1572896 | tf_op jit(solution)/shard_map/ppermute | solution.py:101
  152.1 11.6 %attend_short.1 = (f32[448,768]{1,0:T(8,128)S(1)}, f32[448,768]{1,0:T(8,128)S(1)}) custom-call(s32[448,1]{1,0:T(8,128)S(1)} %copy.186.clip_ref, s32[1,448]{1,0:T(1,128)S(1)} %bitcast.182, bf16[448,768]{1,0:T(8,128)(2,1)S(1)} %slice.301.query_ref, bf16[448,768]{1,0:T(8,128)(2,1)S(1)} %slice.302.key_ref, bf16[448,768]{1,0:T(8,128)(2,1)S(1)} %slice.303.value_ref), custom_call_target="tpu_custom_call" | custom-call | flops 1 | bytes 1 | tf_op jit(solution)/shard_map/attend_short/pallas_call | solution.py:516
  168.6 27.8 %collective-permute-done.16 = bf16[384,768]{1,0:T(8,128)(2,1)} collective-permute-done((bf16[384,768]{1,0:T(8,128)(2,1)}, bf16[384,768]{1,0:T(8,128)(2,1)}, u32[]{:S(2)}, u32[]{:S(2)}) %collective-permute-start.16) | collective-permute-done | bytes 589856 | tf_op jit(solution)/shard_map/ppermute | solution.py:101
  228.5 12.0 %attend_cross.1 = (f32[512,768]{1,0:T(8,128)S(1)}, f32[512,768]{1,0:T(8,128)S(1)}) custom-call(s32[512,1]{1,0:T(8,128)S(1)} %copy.192.clip_ref, s32[1,256]{1,0:T(1,128)S(1)} %compare_select_fusion.key_clip_ref, bf16[512,768]{1,0:T(8,128)(2,1)S(1)} %copy-done.18, bf16[256,768]{1,0:T(8,128)(2,1)S(1)} %norm_text.1.key_ref, bf16[256,768]{1,0:T(8,128)(2,1)S(1)} %fusion.37.value_ref), custom_call_target="tpu_custom_call" | custom-call | flops 1 | bytes 1 | tf_op jit(solution)/shard_map/attend_cross/pallas_call | solution.py:516
  241.8 7.2 attend_long.1
  270.4 25.1 %collective-permute-done.25 = bf16[384,2048]{1,0:T(8,128)(2,1)} collective-permute-done((bf16[384,2048]{1,0:T(8,128)(2,1)}, bf16[384,2048]{1,0:T(8,128)(2,1)}, u32[]{:S(2)}, u32[]{:S(2)}) %collective-permute-start.25) | collective-permute-done | bytes 1572896 | tf_op jit(solution)/shard_map/ppermute | solution.py:101
  325.0 8.2 %collective-permute-done.29 = bf16[384,2048]{1,0:T(8,128)(2,1)S(1)} collective-permute-done((bf16[384,2048]{1,0:T(8,128)(2,1)}, bf16[384,2048]{1,0:T(8,128)(2,1)S(1)}, u32[]{:S(2)}, u32[]{:S(2)}) %collective-permute-start.29) | collective-permute-done | bytes 1572896 | tf_op jit(solution)/shard_map/ppermute | solution.py:101
  352.1 26.8 %collective-permute-done.32.moved_ref = bf16[512,1536]{1,0:T(8,128)(2,1)S(1)} collective-permute-done((bf16[512,1536]{1,0:T(8,128)(2,1)S(1)}, bf16[512,1536]{1,0:T(8,128)(2,1)S(1)}, u32[]{:S(2)}, u32[]{:S(2)}) %collective-permute-start.32) | collective-permute-done | bytes 1572896 | tf_op jit(solution)/shard_map/ppermute | solution.py:73
  439.1 13.8 %collective-permute-done.35.refs_2_ = bf16[384,2048]{1,0:T(8,128)(2,1)S(1)} collective-permute-done((bf16[384,2048]{1,0:T(8,128)(2,1)S(1)}, bf16[384,2048]{1,0:T(8,128)(2,1)S(1)}, u32[]{:S(2)}, u32[]{:S(2)}) %collective-permute-start.35) | collective-permute-done | bytes 1572896 | tf_op jit(solution)/shard_map/ppermute | solution.py:101
  462.7 8.1 %middle_rows.1 = (f32[512,1536]{1,0:T(8,128)}, bf16[512,1536]{1,0:T(8,128)(2,1)S(1)}) custom-call(s32[512,1]{1,0:T(8,128)S(1)} %copy.192.clip_ref, f32[512,1536]{1,0:T(8,128)} %get-tuple-element.246.res_ref, bf16[512,1536]{1,0:T(8,128)(2,1)S(1)} %fusion.22.grad_part_ref, bf16[512,1536]{1,0:T(8,128)(2,1)S(1)} %copy-done.33, bf16[512,1536]{1,0:T(8,128)(2,1)} %fusion.25.up_ref, ...), custom_call_target="tpu_custom_call" | custom-call | flops 1 | bytes 1 | tf_op jit(solution)/shard_map/middle_rows/pallas_call | solution.py:387
  474.9 9.8 %attend_long_back.1 = (f32[64,768]{1,0:T(8,128)S(1)}, bf16[1024,768]{1,0:T(8,128)(2,1)S(1)}, bf16[1024,768]{1,0:T(8,128)(2,1)S(1)}) custom-call(s32[64,1]{1,0:T(8,128)S(1)} %copy-done.80, s32[1,1024]{1,0:T(1,128)S(1)} %broadcast_in_dim.215.key_clip_ref, bf16[64,768]{1,0:T(8,128)(2,1)S(1)} %copy-done.70, bf16[1024,1536]{1,0:T(8,128)(2,1)} %copy-done.3, ...), custom_call_target="tpu_custom_call" | custom-call | flops 1 | bytes 1 | tf_op jit(solution)/shard_map/attend_long_back/pallas_call | solution.py:516
  502.7 10.8 %attend_cross_back.1 = (f32[512,768]{1,0:T(8,128)S(1)}, f32[256,768]{1,0:T(8,128)S(1)}, f32[256,768]{1,0:T(8,128)S(1)}) custom-call(s32[512,1]{1,0:T(8,128)S(1)} %copy.192.clip_ref, s32[1,256]{1,0:T(1,128)S(1)} %compare_select_fusion.key_clip_ref, bf16[512,768]{1,0:T(8,128)(2,1)S(1)} %copy-done.19, bf16[256,768]{1,0:T(8,128)(2,1)S(1)} %copy-done.49, ...), custom_call_target="tpu_custom_call" | custom-call | flops 1 | bytes 1 | tf_op jit(solution)/shard_map/attend_cross_back/pallas_call | solution.py:516
  526.7 9.7 %collective-permute-done.39.refs_2_ = bf16[384,2048]{1,0:T(8,128)(2,1)} collective-permute-done((bf16[384,2048]{1,0:T(8,128)(2,1)}, bf16[384,2048]{1,0:T(8,128)(2,1)}, u32[]{:S(2)}, u32[]{:S(2)}) %collective-permute-start.39) | collective-permute-done | bytes 1572896 | tf_op jit(solution)/shard_map/ppermute | solution.py:101
  548.0 16.7 %attend_short_back.1 = (f32[448,768]{1,0:T(8,128)S(1)}, f32[448,768]{1,0:T(8,128)S(1)}, f32[448,768]{1,0:T(8,128)}) custom-call(s32[448,1]{1,0:T(8,128)S(1)} %copy-done.51, s32[1,448]{1,0:T(1,128)S(1)} %bitcast.183, bf16[448,768]{1,0:T(8,128)(2,1)S(1)} %copy-done.41, bf16[448,768]{1,0:T(8,128)(2,1)S(1)} %copy-done.37, bf16[448,768]{1,0:T(8,128)(2,1)S(1)} %copy-done.39, ...), custom_call_target="tpu_custom_call" | custom-call | flops 1 | bytes 1 | tf_op jit(solution)/shard_map/attend_short_back/pallas_call | solution.py:516
  585.1 6.6 sum_rows.1
  603.5 12.6 %collective-permute-done.45.refs_2_ = bf16[1024,768]{1,0:T(8,128)(2,1)S(1)} collective-permute-done((bf16[1024,768]{1,0:T(8,128)(2,1)}, bf16[1024,768]{1,0:T(8,128)(2,1)S(1)}, u32[]{:S(2)}, u32[]{:S(2)}) %collective-permute-start.45) | collective-permute-done | bytes 1572896 | tf_op jit(solution)/shard_map/ppermute | solution.py:101
  650.8 10.5 %collective-permute-done.49 = bf16[64,1536]{1,0:T(8,128)(2,1)S(1)} collective-permute-done((bf16[64,1536]{1,0:T(8,128)(2,1)S(1)}, bf16[64,1536]{1,0:T(8,128)(2,1)S(1)}, u32[]{:S(2)}, u32[]{:S(2)}) %collective-permute-start.49) | collective-permute-done | bytes 196640 | tf_op jit(solution)/shard_map/ppermute | solution.py:214
  662.7 8.2 %collective-permute-done.48.refs_2_ = bf16[1024,768]{1,0:T(8,128)(2,1)S(1)} collective-permute-done((bf16[1024,768]{1,0:T(8,128)(2,1)}, bf16[1024,768]{1,0:T(8,128)(2,1)S(1)}, u32[]{:S(2)}, u32[]{:S(2)}) %collective-permute-start.48) | collective-permute-done | bytes 1572896 | tf_op jit(solution)/shard_map/ppermute | solution.py:101
  691.8 8.1 %collective-permute-done.52 = bf16[256,1536]{1,0:T(8,128)(2,1)S(1)} collective-permute-done((bf16[256,1536]{1,0:T(8,128)(2,1)S(1)}, bf16[256,1536]{1,0:T(8,128)(2,1)S(1)}, u32[]{:S(2)}, u32[]{:S(2)}) %collective-permute-start.52) | collective-permute-done | bytes 786464 | tf_op jit(solution)/shard_map/ppermute | solution.py:73
  702.3 6.4 last_rows.1
  792.4 7.7 collective-permute-done.66
  (912 shorter events, 485.9 us)
Async XLA Ops:
  7.2 46.0 %all-gather.7.cloned.1.call-start = ((), (), s32[]{:S(2)}) async-start(), calls=%async_computation.7 | async-start | bytes 2211840 | tf_op jit(solution)/shard_map/all_gather | solution.py:116
  9.3 91.7 %all-gather.9.cloned.1.call-start = ((), (), s32[]{:S(2)}) async-start(), calls=%async_computation.8 | async-start | bytes 1966080 | tf_op jit(solution)/shard_map/all_gather | solution.py:116
  53.3 40.7 %collective-permute-start.8 = (bf16[384,2304]{1,0:T(8,128)(2,1)}, bf16[384,2304]{1,0:T(8,128)(2,1)}, u32[]{:S(2)}, u32[]{:S(2)}) collective-permute-start(bf16[384,2304]{1,0:T(8,128)(2,1)} %all-gather.7.cloned.1.call-done), channel_id=1, source_target_pairs={{0,4},{2,6},{4,0},{6,2},{8,12},{10,14},{12,8},{14,10},{16,20},{18,... | collective-permute-start | bytes 5308424 | tf_op jit(solution)/shard_map/ppermute | solution.py:101
  54.7 39.2 %collective-permute-start.7 = (bf16[384,2304]{1,0:T(8,128)(2,1)}, bf16[384,2304]{1,0:T(8,128)(2,1)}, u32[]{:S(2)}, u32[]{:S(2)}) collective-permute-start(bf16[384,2304]{1,0:T(8,128)(2,1)} %all-gather.7.cloned.1.call-done), channel_id=1, source_target_pairs={{0,2},{2,0},{4,6},{6,4},{8,10},{10,8},{12,14},{14,12},{16,18},{18,... | collective-permute-start | bytes 5308424 | tf_op jit(solution)/shard_map/ppermute | solution.py:101
  55.1 86.7 %all-gather.11.cloned.1.call-start = ((), (), s32[]{:S(2)}) async-start(), calls=%async_computation.9 | async-start | bytes 1966080 | tf_op jit(solution)/shard_map/all_gather | solution.py:116
  105.7 92.9 %all-gather.13.cloned.1.call-start = ((), (), s32[]{:S(2)}) async-start(), calls=%async_computation.10 | async-start | bytes 2949120 | tf_op jit(solution)/shard_map/all_gather | solution.py:116
  143.9 114.2 %all-gather.15.cloned.1.call-start = ((), (), s32[]{:S(2)}) async-start(), calls=%async_computation.11 | async-start | bytes 1966080 | tf_op jit(solution)/shard_map/all_gather | solution.py:116
  146.5 51.0 %collective-permute-start.14 = (bf16[1024,768]{1,0:T(8,128)(2,1)}, bf16[1024,768]{1,0:T(8,128)(2,1)S(1)}, u32[]{:S(2)}, u32[]{:S(2)}) collective-permute-start(bf16[1024,768]{1,0:T(8,128)(2,1)} %all-gather.11.cloned.1.call-done), channel_id=1, source_target_pairs={{0,2},{2,0},{4,6},{6,4},{8,10},{10,8},{12,14},{14,12},{16,18},{18,... | collective-permute-start | bytes 4718600 | tf_op jit(solution)/shard_map/ppermute | solution.py:101
  146.6 52.1 %collective-permute-start.13 = (bf16[1024,768]{1,0:T(8,128)(2,1)}, bf16[1024,768]{1,0:T(8,128)(2,1)}, u32[]{:S(2)}, u32[]{:S(2)}) collective-permute-start(bf16[1024,768]{1,0:T(8,128)(2,1)} %all-gather.11.cloned.1.call-done), channel_id=1, source_target_pairs={{0,4},{2,6},{4,0},{6,2},{8,12},{10,14},{12,8},{14,10},{16,20},{18,... | collective-permute-start | bytes 4718600 | tf_op jit(solution)/shard_map/ppermute | solution.py:101
  147.3 49.0 %collective-permute-start.15 = (bf16[1024,768]{1,0:T(8,128)(2,1)}, bf16[1024,768]{1,0:T(8,128)(2,1)S(1)}, u32[]{:S(2)}, u32[]{:S(2)}) collective-permute-start(bf16[1024,768]{1,0:T(8,128)(2,1)} %collective-permute-done.10), channel_id=1, source_target_pairs={{0,2},{2,0},{4,6},{6,4},{8,10},{10,8},{12,14},{14,12},{16,18},{18,... | collective-permute-start | bytes 4718600 | tf_op jit(solution)/shard_map/ppermute | solution.py:101
  148.9 47.4 %collective-permute-start.16 = (bf16[384,768]{1,0:T(8,128)(2,1)}, bf16[384,768]{1,0:T(8,128)(2,1)}, u32[]{:S(2)}, u32[]{:S(2)}) collective-permute-start(bf16[384,768]{1,0:T(8,128)(2,1)} %all_gather.23), channel_id=1, source_target_pairs={{0,4},{2,6},{4,0},{6,2},{8,12},{10,14},{12,8},{14,10},{16,20},{18,... | collective-permute-start | bytes 1769480 | tf_op jit(solution)/shard_map/ppermute | solution.py:101
  204.8 91.3 %all-gather.17.cloned.1.call-start = ((), (), s32[]{:S(2)}) async-start(), calls=%async_computation.12 | async-start | bytes 1966080 | tf_op jit(solution)/shard_map/all_gather | solution.py:116
  212.0 41.0 %collective-permute-start.23 = (bf16[384,2048]{1,0:T(8,128)(2,1)S(1)}, bf16[384,2048]{1,0:T(8,128)(2,1)}, u32[]{:S(2)}, u32[]{:S(2)}) collective-permute-start(bf16[384,2048]{1,0:T(8,128)(2,1)S(1)} %bitcast.196), channel_id=1, source_target_pairs={{0,2},{2,0},{4,6},{6,4},{8,10},{10,8},{12,14},{14,12},{16,18},{18,... | collective-permute-start | bytes 4718600 | tf_op jit(solution)/shard_map/ppermute | solution.py:101
  220.2 37.8 %collective-permute-start.22 = (bf16[384,2048]{1,0:T(8,128)(2,1)S(1)}, bf16[384,2048]{1,0:T(8,128)(2,1)}, u32[]{:S(2)}, u32[]{:S(2)}) collective-permute-start(bf16[384,2048]{1,0:T(8,128)(2,1)S(1)} %bitcast.197), channel_id=1, source_target_pairs={{0,4},{2,6},{4,0},{6,2},{8,12},{10,14},{12,8},{14,10},{16,20},{18,... | collective-permute-start | bytes 4718600 | tf_op jit(solution)/shard_map/ppermute | solution.py:101
  258.1 268.6 %reduce-scatter.10.cloned.1.call-start = ((), (), s32[]{:S(2)}) async-start(), calls=%async_computation.14 | async-start | bytes 1966080 | tf_op jit(solution)/shard_map/reduce_scatter | solution.py:207
  421.7 63.1 %collective-permute-start.38 = (bf16[768,2048]{1,0:T(8,128)(2,1)}, bf16[768,2048]{1,0:T(8,128)(2,1)}, u32[]{:S(2)}, u32[]{:S(2)}) collective-permute-start(bf16[768,2048]{1,0:T(8,128)(2,1)} %convolution_convert_fusion.2), channel_id=1, source_target_pairs={{0,2},{2,0},{4,6},{6,4},{8,10},{10,8},{12,14},{14,12},{16,18},{18,... | collective-permute-start | bytes 9437192 | tf_op jit(solution)/shard_map/ppermute | solution.py:101
  459.1 77.3 %reduce-scatter.8.cloned.1.call-start = ((), (), s32[]{:S(2)}) async-start(), calls=%async_computation.13 | async-start | bytes 1966080 | tf_op jit(solution)/shard_map/reduce_scatter | solution.py:207
  499.1 75.6 %reduce-scatter.12.cloned.1.call-start = ((), (), s32[]{:S(2)}) async-start(), calls=%async_computation.15 | async-start | bytes 1966080 | tf_op jit(solution)/shard_map/reduce_scatter | solution.py:207
  499.3 37.1 %collective-permute-start.39 = (bf16[384,2048]{1,0:T(8,128)(2,1)}, bf16[384,2048]{1,0:T(8,128)(2,1)}, u32[]{:S(2)}, u32[]{:S(2)}) collective-permute-start(bf16[384,2048]{1,0:T(8,128)(2,1)} %copy-done.59), channel_id=1, source_target_pairs={{0,4},{2,6},{4,0},{6,2},{8,12},{10,14},{12,8},{14,10},{16,20},{18,... | collective-permute-start | bytes 4718600 | tf_op jit(solution)/shard_map/ppermute | solution.py:101
  541.0 76.2 %reduce-scatter.14.cloned.1.call-start = ((), (), s32[]{:S(2)}) async-start(), calls=%async_computation.16 | async-start | bytes 1720320 | tf_op jit(solution)/shard_map/reduce_scatter | solution.py:207
  579.0 93.4 %reduce-scatter.16.cloned.1.call-start = ((), (), s32[]{:S(2)}) async-start(), calls=%async_computation.17 | async-start | bytes 1966080 | tf_op jit(solution)/shard_map/reduce_scatter | solution.py:207
  633.6 87.0 %reduce-scatter.18.cloned.1.call-start = ((), (), s32[]{:S(2)}) async-start(), calls=%async_computation.18 | async-start | bytes 1966080 | tf_op jit(solution)/shard_map/reduce_scatter | solution.py:207
  679.1 101.4 %reduce-scatter.20.cloned.1.call-start = ((), (), s32[]{:S(2)}) async-start(), calls=%async_computation.19 | async-start | bytes 2211840 | tf_op jit(solution)/shard_map/reduce_scatter | solution.py:207
  679.1 40.3 %collective-permute-start.53 = (bf16[384,2304]{1,0:T(8,128)(2,1)S(1)}, bf16[384,2304]{1,0:T(8,128)(2,1)}, u32[]{:S(2)}, u32[]{:S(2)}) collective-permute-start(bf16[384,2304]{1,0:T(8,128)(2,1)S(1)} %add_rows.25), channel_id=1, source_target_pairs={{0,4},{2,6},{4,0},{6,2},{8,12},{10,14},{12,8},{14,10},{16,20},{18,... | collective-permute-start | bytes 5308424 | tf_op jit(solution)/shard_map/ppermute | solution.py:101
  (276 other events, 3004.1 us)
Sparse Core Ops, SparseCore 0:
  10.2 43.0 all-gather.6
  55.4 45.5 all-gather.8
  105.9 35.1 all-gather.10
  144.0 48.5 all-gather.12
  204.9 35.0 all-gather.14
  258.2 35.1 all-gather.16
  459.2 33.3 reduce-scatter.9
  499.2 33.3 reduce-scatter.7
  541.1 33.4 reduce-scatter.11
  579.1 31.3 reduce-scatter.13
  633.7 38.6 reduce-scatter.15
  679.2 41.4 reduce-scatter.17
  739.5 37.7 reduce-scatter.19
